TPU v7x, 256 devices: a whole 4x4x8 slice. The times are simulated.
256 devices in a mesh: blk: 64 (over x, z, core), rep: 4 (over y).
Axes of the slice: x: 4, y: 4, z: 8, core: 2. Of those that a mesh axis runs over, the one named last changes fastest.
Arguments:
- right_side: float32 [64, 262144], P(None, 'blk'), may hold values from -6 to 6
- points: float32 [3, 262144], P(None, 'blk'), may hold values from -1 to 544, as said below
- active: int32 [64, 5], replicated, may hold values 0 or 1
Outputs:
- posterior_mean: float32 [64, 262144], P(None, 'blk')
- residual: float32 [64, 262144], P(None, 'blk')
Inputs may be any that keep to these rules, and one draw needn't show every extreme that they name: `points`: point coordinates in lattice units.
All inputs are finite; a program needn't handle non-finite values.
Results may differ from a plain program's by a relative error of at most 0.0003.
Values sent between devices are 32-bit elements; how exact they have to be, the bound alone decides.
No kernel may reach another device: no remote copies, remote signals or barrier semaphores. Data moves between devices by JAX's collectives and lax.ppermute only.
A program may use at most 128 MiB of HBM per device.

v0:
```python
from functools import partial

import jax
import jax.numpy as jnp
from jax import lax
from jax.sharding import PartitionSpec as P

ITERS = 2
B = 2048


support_radius = 2.5
noise_level = 8.0


def from_behind(block, axis, distance):
    devices = range(lax.axis_size(axis))
    route = [(i - distance, i) for i in devices if i - distance in devices]
    return lax.ppermute(block, axis, route)


def wendland(rows, cols):
    delta_x = rows[0][:, None] - cols[0][None, :]
    delta_y = rows[1][:, None] - cols[1][None, :]
    delta_z = rows[2][:, None] - cols[2][None, :]
    scaled = jnp.sqrt(delta_x * delta_x + delta_y * delta_y + delta_z * delta_z) / support_radius
    inside = jnp.maximum(1.0 - scaled, 0.0)
    square = inside * inside
    return square * square * (4.0 * scaled + 1.0)


def apply_rows(vector, kernel_tile):
    return lax.dot_general(
        vector,
        kernel_tile,
        (((1,), (1,)), ((), ())),
        precision=lax.Precision.HIGHEST,
        preferred_element_type=jnp.float32,
    )


def apply_cols(vector, kernel_tile):
    return jnp.dot(
        vector, kernel_tile, precision=lax.Precision.HIGHEST, preferred_element_type=jnp.float32
    )


def pair_flags(active, column, count):
    here = lax.dynamic_slice_in_dim(active, column, 1, 0)[0].astype(jnp.float32)
    before = lax.dynamic_slice_in_dim(active, jnp.maximum(column - 1, 0), 1, 0)[0].astype(
        jnp.float32
    )
    has_before = (column >= 1).astype(jnp.float32)
    has_after = (column + 1 < count).astype(jnp.float32)
    table = []
    for c in range(2):
        entry = []
        for k in range(6):
            if k < 2:
                entry.append(before[1 + 2 * k + c] * has_before)
            elif k == 2 + c:
                entry.append(has_after * 0.0 + 1.0)
            elif k < 4:
                entry.append(here[0])
            else:
                entry.append(here[1 + 2 * c + (k - 4)] * has_after)
        table.append(entry)
    return table


def gated(flag, compute, operands):
    return flag * compute(*operands)


def place_rows(values, start, total):
    return lax.dynamic_update_slice_in_dim(
        jnp.zeros((values.shape[0], total), jnp.float32), values, start, 1
    )


def shards(right_side, points, active):
    count = lax.axis_size("blk")
    column = lax.axis_index("blk")
    groups = lax.axis_size("rep")
    member = lax.axis_index("rep")
    flags = pair_flags(active, column, count)
    rows_each = B // groups
    row_start = member * rows_each
    sides = right_side.shape[0]

    def row_slice(array, c):
        return lax.dynamic_slice_in_dim(array, c * B + row_start, rows_each, 1)

    def fetch(stored, index):
        return stored[index]

    pts_next = from_behind(points, "blk", -1)
    makers = [
        partial(wendland, row_slice(points, c), points[:, c * B : (c + 1) * B]) for c in range(2)
    ]
    makers.append(partial(wendland, row_slice(points, 0), points[:, B : 2 * B]))
    for c in range(2):
        for k in range(2):
            makers.append(partial(wendland, row_slice(points, c), pts_next[:, k * B : (k + 1) * B]))
    stored = [maker() for maker in makers]

    def matvec(vector):
        vec_next = from_behind(vector, "blk", -1)
        own_rows = [row_slice(vector, c) for c in range(2)]
        row_terms = [apply_rows(vector[:, c * B : (c + 1) * B], fetch(stored, c)) for c in range(2)]
        across_tile = fetch(stored, 2)
        row_terms[0] = row_terms[0] + gated(
            flags[0][3], apply_rows, (vector[:, B : 2 * B], across_tile)
        )
        across_back = gated(flags[0][3], apply_cols, (own_rows[0], across_tile))
        next_terms = [jnp.zeros((sides, B), jnp.float32), jnp.zeros((sides, B), jnp.float32)]
        for c in range(2):
            for k in range(2):
                kernel_tile = fetch(stored, 3 + 2 * c + k)
                flag = flags[c][4 + k]
                row_terms[c] = row_terms[c] + gated(
                    flag, apply_rows, (vec_next[:, k * B : (k + 1) * B], kernel_tile)
                )
                next_terms[k] = next_terms[k] + gated(flag, apply_cols, (own_rows[c], kernel_tile))
        own_full = jnp.concatenate(
            [
                place_rows(row_terms[0], row_start, B),
                across_back + place_rows(row_terms[1], row_start, B),
            ],
            axis=1,
        )
        returned = from_behind(jnp.concatenate(next_terms, axis=1), "blk", 1)
        total = lax.psum(own_full + returned, "rep")
        return total + noise_level * vector

    def squares(residual):
        return lax.psum(jnp.sum(residual * residual, axis=1), "blk")

    solution = jnp.zeros_like(right_side)
    residual = right_side
    direction = right_side
    norm_now = squares(residual)
    for step in range(ITERS):
        image = matvec(direction)
        alpha = norm_now / lax.psum(jnp.sum(direction * image, axis=1), "blk")
        solution = solution + alpha[:, None] * direction
        residual = residual - alpha[:, None] * image
        norm_next = squares(residual)
        direction = residual + (norm_next / norm_now)[:, None] * direction
        norm_now = norm_next
    posterior = right_side - noise_level * solution
    return (posterior, residual)


def solution(mesh):
    return jax.shard_map(
        shards,
        mesh=mesh,
        in_specs=(P(None, "blk"), P(None, "blk"), P()),
        out_specs=(P(None, "blk"), P(None, "blk")),
        check_vma=False,
    )
```

profile of v0, /device:TPU:8, one launch (start us, length us, event | category | flops | bytes accessed | tf_op | source)
XLA Modules:
  0.0 681.2 jit_solution(9274392147604572619)
XLA Ops:
  13.1 8.3 %fusion.17 = f32[512,64]{0,1:T(8,128)S(1)} fusion(f32[512]{0:T(512)S(1)} %bitcast.125, f32[512]{0:T(512)S(1)} %bitcast.115, f32[512]{0:T(512)S(1)} %bitcast.105, f32[2048]{0:T(1024)S(1)} %bitcast.39, f32[2048]{0:T(1024)S(1)} %bitcast.45, f32[2048]{0:T(1024)S(1)} %bitcast.51, f32[64,4096]{1,0:T(8,128)} %param.3), kind=kOutput, calls=%fused_computation.34 | convolution fusion | flops 822083584 | bytes 686080 | tf_op jit(solution)/shard_map/dot_general | solution.py:33
  21.4 8.1 %fusion.44 = f32[512,64]{0,1:T(8,128)S(1)} fusion(f32[2048]{0:T(1024)S(1)} %bitcast.40, f32[2048]{0:T(1024)S(1)} %bitcast.46, f32[2048]{0:T(1024)S(1)} %bitcast.52, f32[512]{0:T(512)S(1)} %bitcast.163, f32[512]{0:T(512)S(1)} %bitcast.135, f32[512]{0:T(512)S(1)} %bitcast.149, f32[64,4096]{1,0:T(8,128)S(1)} %copy-done, f32[]{:T(128)} %bitcast.6), kind=kOutput, calls=%fused_computation.61 | convolution fusion | flops 822116352 | bytes 686084 | tf_op jit(solution)/shard_map/dot_general | solution.py:33
  29.5 7.2 %fusion.18 = f32[512,64]{0,1:T(8,128)S(1)} fusion(f32[512,64]{0,1:T(8,128)S(1)} %fusion.44, f32[2048]{0:T(1024)S(1)} %bitcast.35, f32[512]{0:T(512)S(1)} %bitcast.164, f32[2048]{0:T(1024)S(1)} %bitcast.37, f32[512]{0:T(512)S(1)} %bitcast.136, f32[2048]{0:T(1024)S(1)} %bitcast.33, f32[512]{0:T(512)S(1)} %bitcast.150, f32[64,4096]{1,0:T(8,128)S(1)} %copy-done), kind=kOutput, calls=%fused_computation.35 | convolution fusion | flops 822116352 | bytes 817152 | tf_op jit(solution)/shard_map/dot_general | solution.py:33
  36.7 6.6 convolution_multiply_fusion.9
  45.8 5.7 convolution_multiply_fusion.8
  51.6 5.7 fusion.3
  57.3 5.9 convolution_multiply_fusion.6
  63.3 5.7 fusion.2
  69.1 4.1 collective-permute-start.2
  73.2 7.2 %fusion.41 = f32[512,64]{0,1:T(8,128)S(1)} fusion(f32[512,64]{0,1:T(8,128)S(1)} %fusion.18, f32[2048]{0:T(1024)S(1)} %bitcast.91, f32[2048]{0:T(1024)S(1)} %bitcast.99, f32[2048]{0:T(1024)S(1)} %bitcast.83, f32[512]{0:T(512)S(1)} %bitcast.168, f32[512]{0:T(512)S(1)} %bitcast.140, f32[512]{0:T(512)S(1)} %bitcast.154, ...), kind=kOutput, calls=%fused_computation.58 | convolution fusion | flops 822149120 | bytes 817156 | tf_op jit(solution)/shard_map/dot_general | solution.py:33
  80.4 7.3 %fusion.36 = f32[64,2048]{1,0:T(8,128)S(1)} fusion(f32[64,2048]{1,0:T(8,128)S(1)} %broadcast.47.clone, s32[]{:T(128)S(6)} %select_n.10, f32[512,64]{0,1:T(8,128)S(1)} %fusion.41, f32[2048]{0:T(1024)S(1)} %bitcast.59, f32[2048]{0:T(1024)S(1)} %bitcast.67, f32[2048]{0:T(1024)S(1)} %bitcast.75, f32[512]{0:T(512)S(1)} %bitcast.169, f32[512]{0:T(512)S(1)} %bitcast.141, ...), kind=kOutput, calls=%fused_computation.53 | convolution fusion | flops 822149120 | bytes 817160 | tf_op jit(solution)/shard_map/dot_general | solution.py:33
  87.8 7.2 %fusion.30 = f32[512,64]{0,1:T(8,128)S(1)} fusion(f32[512,64]{0,1:T(8,128)S(1)} %fusion.17, f32[512]{0:T(512)S(1)} %bitcast.128, f32[512]{0:T(512)S(1)} %bitcast.118, f32[512]{0:T(512)S(1)} %bitcast.108, f32[2048]{0:T(1024)S(1)} %bitcast.92, f32[2048]{0:T(1024)S(1)} %bitcast.100, f32[2048]{0:T(1024)S(1)} %bitcast.84, ...), kind=kOutput, calls=%fused_computation.47 | convolution fusion | flops 822149120 | bytes 817156 | tf_op jit(solution)/shard_map/dot_general | solution.py:33
  95.0 7.4 %fusion.24 = f32[64,2048]{1,0:T(8,128)S(1)} fusion(f32[64,2048]{1,0:T(8,128)S(1)} %convolution_multiply_fusion.9, s32[]{:T(128)S(6)} %select_n.10, f32[512,64]{0,1:T(8,128)S(1)} %fusion.30, f32[512]{0:T(512)S(1)} %bitcast.129, f32[512]{0:T(512)S(1)} %bitcast.119, f32[512]{0:T(512)S(1)} %bitcast.109, f32[2048]{0:T(1024)S(1)} %bitcast.60, ...), kind=kOutput, calls=%fused_computation.41 | convolution fusion | flops 822181888 | bytes 948232 | tf_op jit(solution)/shard_map/dot_general | solution.py:33
  103.5 55.2 %all-reduce.4.cloned.1.call-done = f32[64,4096]{1,0:T(8,128)} async-done(((f32[64,4096]{1,0:T(8,128)}), f32[64,4096]{1,0:T(8,128)}) %all-reduce.4.cloned.1.call-update) | async-done | bytes 1048592 | tf_op jit(solution)/shard_map/psum | solution.py:133
  160.4 127.9 %all-reduce = (f32[64]{0:T(128)S(1)}, f32[64]{0:T(128)S(1)}) all-reduce(f32[64]{0:T(128)S(1)} %get-tuple-element.3, f32[64]{0:T(128)S(1)} %get-tuple-element.2), channel_id=1, replica_groups=mesh['blk'=64,'rep'=4] {'blk'}, use_global_device_ids=true, to_apply=%region_1.0 | all-reduce | flops 128 | bytes 1024 | tf_op jit(solution)/shard_map/psum | solution.py:137
  288.6 124.1 %psum.45 = f32[64]{0:T(128)S(1)} all-reduce(f32[64]{0:T(128)S(1)} %multiply_reduce_fusion.1), channel_id=1, replica_groups=mesh['blk'=64,'rep'=4] {'blk'}, use_global_device_ids=true, to_apply=%region_6.0 | all-reduce | flops 64 | bytes 512 | tf_op jit(solution)/shard_map/psum | solution.py:137
  412.9 7.4 %fusion.45 = f32[64,512]{1,0:T(8,128)S(1)} fusion(f32[2048]{0:T(1024)S(1)} %bitcast.42, f32[2048]{0:T(1024)S(1)} %bitcast.48, f32[2048]{0:T(1024)S(1)} %bitcast.54, f32[512]{0:T(512)S(1)} %bitcast.170, f32[512]{0:T(512)S(1)} %bitcast.142, f32[512]{0:T(512)S(1)} %bitcast.156, f32[64,4096]{1,0:T(8,128)S(1)} %multiply_add_fusion.1, f32[]{:T(128)} %bitcast.6), kind=kOutput, calls=%fused_computation.62 | convolution fusion | flops 822116352 | bytes 686084 | tf_op jit(solution)/shard_map/dot_general | solution.py:33
  422.0 6.7 fusion.16
  428.8 5.7 convolution_multiply_fusion.3
  434.5 5.9 convolution_multiply_fusion.1
  440.4 5.7 fusion.1
  446.2 6.1 fusion
  452.4 3.1 collective-permute-start.4
  455.5 6.4 convolution_multiply_fusion.4
  461.9 6.7 fusion.19
  468.7 6.9 %fusion.43 = f32[64,512]{1,0:T(8,128)S(1)} fusion(f32[64,512]{1,0:T(8,128)S(1)} %fusion.19, f32[2048]{0:T(1024)S(1)} %bitcast.95, f32[2048]{0:T(1024)S(1)} %bitcast.103, f32[2048]{0:T(1024)S(1)} %bitcast.87, f32[512]{0:T(512)S(1)} %bitcast.175, f32[512]{0:T(512)S(1)} %bitcast.147, f32[512]{0:T(512)S(1)} %bitcast.161, ...), kind=kOutput, calls=%fused_computation.60 | convolution fusion | flops 822149120 | bytes 817156 | tf_op jit(solution)/shard_map/dot_general | solution.py:33
  475.6 6.8 fusion.39
  482.4 7.0 %fusion.32 = f32[64,512]{1,0:T(8,128)S(1)} fusion(f32[64,512]{1,0:T(8,128)S(1)} %fusion.16, f32[512]{0:T(512)S(1)} %bitcast.133, f32[512]{0:T(512)S(1)} %bitcast.123, f32[512]{0:T(512)S(1)} %bitcast.113, f32[2048]{0:T(1024)S(1)} %bitcast.96, f32[2048]{0:T(1024)S(1)} %bitcast.104, f32[2048]{0:T(1024)S(1)} %bitcast.88, ...), kind=kOutput, calls=%fused_computation.49 | convolution fusion | flops 822149120 | bytes 817156 | tf_op jit(solution)/shard_map/dot_general | solution.py:33
  489.3 6.8 fusion.28
  497.2 44.3 %all-reduce.6.cloned.1.call-done = f32[64,4096]{1,0:T(8,128)} async-done(((f32[64,4096]{1,0:T(8,128)}), f32[64,4096]{1,0:T(8,128)}) %all-reduce.6.cloned.1.call-update) | async-done | bytes 1048592 | tf_op jit(solution)/shard_map/psum | solution.py:133
  543.0 127.9 %psum.47 = f32[64]{0:T(128)S(1)} all-reduce(f32[64]{0:T(128)S(1)} %multiply_reduce_fusion), channel_id=1, replica_groups=mesh['blk'=64,'rep'=4] {'blk'}, use_global_device_ids=true, to_apply=%region_9.0 | all-reduce | flops 64 | bytes 512 | tf_op jit(solution)/shard_map/psum | solution.py:145
  670.9 3.0 multiply_subtract_fusion
  (34 shorter events, 13.8 us)
Async XLA Ops:
  7.2 151.6 %all-reduce.4.cloned.1.call-start = ((), (), s32[]{:S(2)}) async-start(), calls=%async_computation | async-start | bytes 2097152 | tf_op jit(solution)/shard_map/psum | solution.py:133
  7.2 38.5 %collective-permute-start = (f32[3,4096]{1,0:T(4,128)}, f32[3,4096]{1,0:T(4,128)S(1)}, u32[]{:S(2)}, u32[]{:S(2)}) collective-permute-start(f32[3,4096]{1,0:T(4,128)} %param.4), channel_id=1, source_target_pairs={{4,0},{8,4},{12,8},{16,12},{20,16},{24,20},{28,24},{32,28},{36,32}... | collective-permute-start | bytes 147464 | tf_op jit(solution)/shard_map/ppermute | solution.py:19
  8.5 64.7 %collective-permute-start.1 = (f32[64,4096]{1,0:T(8,128)}, f32[64,4096]{1,0:T(8,128)S(1)}, u32[]{:S(2)}, u32[]{:S(2)}) collective-permute-start(f32[64,4096]{1,0:T(8,128)} %param.3), channel_id=1, source_target_pairs={{4,0},{8,4},{12,8},{16,12},{20,16},{24,20},{28,24},{32,28},{36,32}... | collective-permute-start | bytes 3145736 | tf_op jit(solution)/shard_map/ppermute | solution.py:19
  13.1 8.3 %copy-start = (f32[64,4096]{1,0:T(8,128)S(1)}, f32[64,4096]{1,0:T(8,128)}, u32[]{:S(2)}) copy-start(f32[64,4096]{1,0:T(8,128)} %param.3) | copy-start | bytes 3145732
  69.1 33.2 %collective-permute-start.2 = (f32[64,4096]{1,0:T(8,128)S(1)}, f32[64,4096]{1,0:T(8,128)S(1)}, u32[]{:S(2)}, u32[]{:S(2)}) collective-permute-start(f32[64,4096]{1,0:T(8,128)S(1)} %pad_maximum_fusion), channel_id=1, source_target_pairs={{0,4},{4,8},{8,12},{12,16},{16,20},{20,24},{24,28},{28,32},{32,36}... | collective-permute-start | bytes 3145736 | tf_op jit(solution)/shard_map/ppermute | solution.py:19
  103.5 438.1 %all-reduce.6.cloned.1.call-start = ((), (), s32[]{:S(2)}) async-start(), calls=%async_computation.1 | async-start | bytes 2097152 | tf_op jit(solution)/shard_map/psum | solution.py:133
  158.7 129.5 %copy-start.1 = (f32[64,4096]{1,0:T(8,128)S(1)}, f32[64,4096]{1,0:T(8,128)}, u32[]{:S(2)}) copy-start(f32[64,4096]{1,0:T(8,128)} %all-reduce.4.cloned.1.call-done) | copy-start | bytes 3145732
  420.3 48.3 %collective-permute-start.3 = (f32[64,4096]{1,0:T(8,128)S(1)}, f32[64,4096]{1,0:T(8,128)S(1)}, u32[]{:S(2)}, u32[]{:S(2)}) collective-permute-start(f32[64,4096]{1,0:T(8,128)S(1)} %multiply_add_fusion.1), channel_id=1, source_target_pairs={{4,0},{8,4},{12,8},{16,12},{20,16},{24,20},{28,24},{32,28},{36,32}... | collective-permute-start | bytes 3145736 | tf_op jit(solution)/shard_map/ppermute | solution.py:19
  452.4 43.7 %collective-permute-start.4 = (f32[64,4096]{1,0:T(8,128)S(1)}, f32[64,4096]{1,0:T(8,128)S(1)}, u32[]{:S(2)}, u32[]{:S(2)}) collective-permute-start(f32[64,4096]{1,0:T(8,128)S(1)} %pad_maximum_fusion.1), channel_id=1, source_target_pairs={{0,4},{4,8},{8,12},{12,16},{16,20},{20,24},{24,28},{28,32},{32,36}... | collective-permute-start | bytes 3145736 | tf_op jit(solution)/shard_map/ppermute | solution.py:19
Sparse Core Ops, SparseCore 0:
  103.6 55.1 all-reduce.3
  497.3 44.1 all-reduce.5
where the time goes:
time: 690 us; the launch traced here: 681 us
  blocking collectives  380 us (55%)
  matrix products  161 us (23%)
  waiting for transfers between devices  99.6 us (14%)
  between operations  17.2 us (2%)
  starting transfers between devices  11.6 us (2%)
  other arithmetic  9.81 us (1%)
    psum x2, blocking collectives, squares(): return lax.psum(jnp.sum(residual * residual, axis=1), 'blk')  252 us
    psum x1, blocking collectives, shards(): alpha = norm_now / lax.psum(jnp.sum(direction * image, axis=1), 'blk')  128 us
    dot_general x14, matrix products, apply_rows(): lax.dot_general(vector, kernel_tile, (((1,), (1,)), ((), ())), precision=...  101 us
    psum x2, waiting for transfers between devices, matvec(): total = lax.psum(own_full + returned, 'rep')  99.6 us
    dot_general x10, matrix products, apply_cols(): jnp.dot(vector, kernel_tile, precision=lax.Precision.HIGHEST, preferred_e...  59.7 us
  transfers between devices with their start and end apart: 7, of which 2 were waited for; matrix products, arithmetic and copies ran while one was open for 23% of the time, Pallas kernels for 0%

commit v1 on v0

v1 whole, which is shorter than its diff:
```python
from functools import partial

import jax
import jax.numpy as jnp
from jax import lax
from jax.experimental import pallas as pl
from jax.experimental.pallas import tpu as pltpu
from jax.sharding import PartitionSpec as P

B = 2048
SUB = 64
TILE = 128
STRIP = 256
BATCH = 4
CELLS_X = 4
CELLS_Y = 8
CELLS = CELLS_X * CELLS_Y
FAR = 1.0e6

support_radius = 2.5
noise_level = 8.0
shift = noise_level + 1.0
profile_scale = 4.0 / support_radius**5
VMEM = pl.BlockSpec(memory_space=pltpu.VMEM)
SMEM = pl.BlockSpec(memory_space=pltpu.SMEM)
PARAMS = pltpu.CompilerParams(vmem_limit_bytes=48 * 1024 * 1024)


def from_behind(block, axis, distance):
    devices = range(lax.axis_size(axis))
    route = [(i - distance, i) for i in devices if i - distance in devices]
    return lax.ppermute(block, axis, route)


def exchange(values, mask, axis):
    devices = range(lax.axis_size(axis))
    return lax.ppermute(values, axis, [(i, i ^ mask) for i in devices])


def sum_over_blk(values):
    for base in (1, 4, 16):
        near = values + exchange(values, base, "blk")
        far = exchange(values, 2 * base, "blk") + exchange(values, 3 * base, "blk")
        values = near + far
    return values


def split3(values):
    high = values.astype(jnp.bfloat16)
    rest = values - high.astype(jnp.float32)
    middle = rest.astype(jnp.bfloat16)
    low = (rest - middle.astype(jnp.float32)).astype(jnp.bfloat16)
    return high, middle, low


def one_hot_strip(rank, start):
    place = lax.broadcasted_iota(jnp.int32, (STRIP, B), 0) + start
    return jnp.where(rank == place, 1.0, 0.0).astype(jnp.bfloat16)


def cell_of(values, cells):
    low = jnp.min(values, axis=1, keepdims=True)
    high = jnp.max(values, axis=1, keepdims=True)
    scaled = (values - low) * (cells / jnp.maximum(high - low, 1e-30))
    return jnp.minimum(jnp.floor(scaled), cells - 1.0)


def sort_kernel(points_ref, vector_ref, rows_ref, cols_ref, rank_ref, feature_ref, split_ref):
    upper = lax.broadcasted_iota(jnp.int32, (TILE, TILE), 0) <= lax.broadcasted_iota(
        jnp.int32, (TILE, TILE), 1
    )
    upper = jnp.where(upper, 1.0, 0.0).astype(jnp.bfloat16)
    lower = lax.broadcasted_iota(jnp.int32, (CELLS, CELLS), 0) > lax.broadcasted_iota(
        jnp.int32, (CELLS, CELLS), 1
    )
    lower = jnp.where(lower, 1.0, 0.0)
    number = lax.broadcasted_iota(jnp.int32, (CELLS, TILE), 0).astype(jnp.float32)
    feature_ref[16:32, :] = jnp.zeros((16, B), jnp.float32)
    split_ref[96:128, :] = jnp.zeros((32, B), jnp.bfloat16)
    for c in range(2):
        span = slice(c * B, (c + 1) * B)
        cell = cell_of(points_ref[0:1, span], CELLS_X) * CELLS_Y + cell_of(
            points_ref[1:2, span], CELLS_Y
        )
        base = jnp.zeros((CELLS, TILE), jnp.float32)
        chosen, place = [], []
        for t in range(B // TILE):
            hit = jnp.where(number == cell[:, t * TILE : (t + 1) * TILE], 1.0, 0.0)
            count = jnp.dot(hit.astype(jnp.bfloat16), upper, preferred_element_type=jnp.float32)
            chosen.append(hit)
            place.append(count + base)
            base = base + count[:, TILE - 1 :]
        offset = jnp.dot(
            lower, base, precision=lax.Precision.HIGHEST, preferred_element_type=jnp.float32
        )
        for t in range(B // TILE):
            rank = jnp.sum(chosen[t] * (place[t] + (offset - 1.0)), axis=0, keepdims=True)
            rank_ref[0:1, c * B + t * TILE : c * B + (t + 1) * TILE] = rank.astype(jnp.int32)
        feature_ref[0:16, :] = vector_ref[:, span]
        feature_ref[16:19, :] = points_ref[:, span]
        for k, part in enumerate(split3(feature_ref[...])):
            split_ref[32 * k : 32 * k + 32, :] = part
        rank = rank_ref[0:1, span]
        for k in range(B // STRIP):
            found = lax.dot_general(
                one_hot_strip(rank, k * STRIP),
                split_ref[...],
                (((1,), (1,)), ((), ())),
                preferred_element_type=jnp.float32,
            )
            found = found + pltpu.roll(found, 96, 1) + pltpu.roll(found, 64, 1)
            spot = slice(c * B + k * STRIP, c * B + (k + 1) * STRIP)
            cols_ref[spot, :] = found
            rows_ref[:, spot] = found.T[0:24, :]


def sort_points(points, vector):
    width = 2 * B
    return pl.pallas_call(
        sort_kernel,
        out_shape=(
            jax.ShapeDtypeStruct((24, width), jnp.float32),
            jax.ShapeDtypeStruct((width, TILE), jnp.float32),
            jax.ShapeDtypeStruct((8, width), jnp.int32),
        ),
        in_specs=[VMEM, VMEM],
        out_specs=(VMEM, VMEM, VMEM),
        scratch_shapes=[pltpu.VMEM((32, B), jnp.float32), pltpu.VMEM((128, B), jnp.bfloat16)],
        compiler_params=PARAMS,
        name="sort_points",
    )(points, vector)


def unsort_kernel(sorted_ref, rank_ref, out_ref, split_ref, total_ref):
    for c in range(2):
        span = slice(c * B, (c + 1) * B)
        for k, part in enumerate(split3(sorted_ref[:, span])):
            split_ref[16 * k : 16 * k + 16, :] = part
        rank = rank_ref[0:1, span]
        for k in range(B // STRIP):
            found = jnp.dot(
                split_ref[:, k * STRIP : (k + 1) * STRIP],
                one_hot_strip(rank, k * STRIP),
                preferred_element_type=jnp.float32,
            )
            total_ref[...] = found if k == 0 else total_ref[...] + found
        out_ref[:, span] = (total_ref[0:16, :] + total_ref[16:32, :]) + total_ref[32:48, :]


def unsort(values, rank):
    return pl.pallas_call(
        unsort_kernel,
        out_shape=jax.ShapeDtypeStruct(values.shape, jnp.float32),
        in_specs=[VMEM, VMEM],
        out_specs=VMEM,
        scratch_shapes=[pltpu.VMEM((48, B), jnp.bfloat16), pltpu.VMEM((48, B), jnp.float32)],
        compiler_params=PARAMS,
        name="unsort",
    )(values, rank)


def apply_kernel(
    own, tiles, stride, counts_ref, list_ref, cols_ref, coords_ref, vec_ref, *rest
):
    if own:
        add_ref = None
        out_ref, left_xyz, right_xyz, left_w, right_w, target, tile_a, tile_b = rest
    else:
        add_ref, out_ref, left_xyz, right_xyz, left_w, right_w, target, tile_a, tile_b = rest
    lane = lax.broadcasted_iota(jnp.int32, (8, TILE), 1)
    is_left = lane < SUB

    def spread(values):
        turned = pltpu.roll(values, SUB, 1)
        mask = jnp.concatenate([is_left] * (values.shape[0] // 8), axis=0)
        zero = jnp.zeros_like(values)
        return (
            jnp.where(mask, values, zero),
            jnp.where(mask, zero, turned),
            jnp.where(mask, turned, zero),
            jnp.where(mask, zero, values),
        )

    def weights(values):
        high = values.astype(jnp.bfloat16)
        low = (values - high.astype(jnp.float32)).astype(jnp.bfloat16)
        return jnp.concatenate([high, low], axis=0)

    def prepare(t, carry):
        spot = pl.ds(pl.multiple_of(t * TILE, TILE), TILE)
        xyz = spread(coords_ref[:, spot])
        left_xyz[2 * t] = xyz[0]
        right_xyz[2 * t] = xyz[1]
        left_xyz[2 * t + 1] = xyz[2]
        right_xyz[2 * t + 1] = xyz[3]
        vec = spread(vec_ref[:, spot])
        left_w[2 * t] = weights(vec[0])
        right_w[2 * t] = weights(vec[1])
        left_w[2 * t + 1] = weights(vec[2])
        right_w[2 * t + 1] = weights(vec[3])
        return carry

    lax.fori_loop(0, tiles, prepare, 0)
    left_xyz[2 * tiles] = jnp.where(is_left, FAR, 0.0)
    right_xyz[2 * tiles] = jnp.where(is_left, 0.0, FAR)
    left_w[2 * tiles] = jnp.zeros((32, TILE), jnp.bfloat16)
    right_w[2 * tiles] = jnp.zeros((32, TILE), jnp.bfloat16)

    def pair(base, slot, tile):
        first = list_ref[base + 2 * slot]
        second = list_ref[base + 2 * slot + 1]
        xyz = left_xyz[first] + right_xyz[second]
        weight = left_w[first] + right_w[second]
        for r in range(TILE // 16):
            rows = slice(16 * r, 16 * r + 16)
            dx = target[0, rows, :] - xyz[0:1, :]
            dy = target[1, rows, :] - xyz[1:2, :]
            dz = target[2, rows, :] - xyz[2:3, :]
            square = jnp.maximum(dx * dx + dy * dy + dz * dz, 1e-30)
            distance = square * lax.rsqrt(square)
            inside = jnp.maximum(support_radius - distance, 0.0)
            inside = inside * inside
            value = (inside * inside) * (distance + 0.25 * support_radius)
            high = value.astype(jnp.bfloat16)
            tile[rows, 0:TILE] = high
            tile[rows, TILE : 2 * TILE] = (value - high.astype(jnp.float32)).astype(jnp.bfloat16)
        return jnp.concatenate([weight, weight], axis=1)

    def apply(weight, tile):
        return lax.dot_general(
            weight, tile[...], (((1,), (1,)), ((), ())), preferred_element_type=jnp.float32
        )

    def row(j, carry):
        spot = pl.ds(pl.multiple_of(j * TILE, TILE), TILE)
        count = counts_ref[j]
        for axis in range(3):
            target[axis] = jnp.broadcast_to(cols_ref[spot, 16 + axis : 17 + axis], (TILE, TILE))

        def step(n, total):
            base = j * stride + n * BATCH
            weight_a = pair(base, 0, tile_a)
            weight_b = pair(base, 1, tile_b)
            return total + (apply(weight_a, tile_a) + apply(weight_b, tile_b))

        total = lax.fori_loop(
            0, (count + BATCH - 1) // BATCH, step, jnp.zeros((32, TILE), jnp.float32)
        )
        image = (total[0:16, :] + total[16:32, :]) * profile_scale
        if own:
            held = (left_w[2 * j] + right_w[2 * j + 1]).astype(jnp.float32)
            out_ref[:, spot] = image - (held[0:16, :] + held[16:32, :])
        else:
            out_ref[:, spot] = image + add_ref[:, spot]
        return carry

    lax.fori_loop(0, out_ref.shape[1] // TILE, row, 0)


def apply_pairs(lists, cols, coords, vector, added=None):
    counts, table = lists
    own = added is None
    tiles = vector.shape[1] // TILE
    operands = [counts, table.reshape(-1), cols, coords, vector] + ([] if own else [added])
    slots = 2 * tiles + 1
    return pl.pallas_call(
        partial(apply_kernel, own, tiles, table.shape[1]),
        out_shape=jax.ShapeDtypeStruct((16, 2 * B), jnp.float32),
        in_specs=[SMEM, SMEM] + [VMEM] * (len(operands) - 2),
        out_specs=VMEM,
        scratch_shapes=[
            pltpu.VMEM((slots, 8, TILE), jnp.float32),
            pltpu.VMEM((slots, 8, TILE), jnp.float32),
            pltpu.VMEM((slots, 32, TILE), jnp.bfloat16),
            pltpu.VMEM((slots, 32, TILE), jnp.bfloat16),
            pltpu.VMEM((3, TILE, TILE), jnp.float32),
            pltpu.VMEM((TILE, 2 * TILE), jnp.bfloat16),
            pltpu.VMEM((TILE, 2 * TILE), jnp.bfloat16),
        ],
        compiler_params=PARAMS,
        name="apply_own" if own else "apply_cross",
    )(*operands)


def boxes(coords, size):
    grouped = coords[0:3].reshape(3, -1, size)
    return jnp.min(grouped, axis=2), jnp.max(grouped, axis=2)


def close_lists(target_box, source_box, flags):
    low_t, high_t = (edge[:, :, None] for edge in target_box)
    low_s, high_s = (edge[:, None, :] for edge in source_box)
    gap = jnp.maximum(jnp.maximum(low_s - high_t, low_t - high_s), 0.0)
    reach = support_radius * support_radius * (1.0 + 1e-4)
    near = jnp.where(jnp.sum(gap * gap, axis=0) <= reach, 1.0, 0.0)
    rows, columns = near.shape
    near = near.reshape(2, rows // 2, flags.shape[1], -1) * flags[:, None, :, None]
    near = near.reshape(rows, columns)
    order = lax.broadcasted_iota(jnp.int32, (columns, columns), 0) <= lax.broadcasted_iota(
        jnp.int32, (columns, columns), 1
    )
    place = jnp.dot(near, order.astype(jnp.float32)).astype(jnp.int32)
    length = columns + BATCH
    wanted = lax.broadcasted_iota(jnp.int32, (rows, length, columns), 1) + 1
    source = lax.broadcasted_iota(jnp.int32, (rows, length, columns), 2)
    match = (place[:, None, :] == wanted) & (near[:, None, :] > 0.0)
    table = jnp.sum(jnp.where(match, source - columns, 0), axis=2) + columns
    return jnp.max(place, axis=1), table


def pair_flags(active, column, count):
    here = lax.dynamic_slice_in_dim(active, column, 1, 0)[0].astype(jnp.float32)
    before = lax.dynamic_slice_in_dim(active, jnp.maximum(column - 1, 0), 1, 0)[0]
    before = before.astype(jnp.float32) * (column >= 1)
    after = here * (column + 1 < count)
    one = jnp.ones((), jnp.float32)
    own = jnp.stack([one, here[0], here[0], one]).reshape(2, 2)
    cross = jnp.stack(
        [before[1], before[3], after[1], after[2], before[2], before[4], after[3], after[4]]
    ).reshape(2, 4)
    return own, cross


def shards(right_side, points, active):
    count = lax.axis_size("blk")
    column = lax.axis_index("blk")
    member = lax.axis_index("rep")
    sides = right_side.shape[0] // lax.axis_size("rep")
    own_flags, cross_flags = pair_flags(active, column, count)

    mine = lax.dynamic_slice_in_dim(right_side, member * sides, sides, 0)
    rows, cols, rank = sort_points(points, mine)
    r0 = rows[0:16]
    around = jnp.concatenate([from_behind(rows, "blk", 1), from_behind(rows, "blk", -1)], axis=1)
    low, high = boxes(rows[16:24], TILE)
    own_lists = close_lists((low, high), boxes(rows[16:24], SUB), own_flags)
    part = apply_pairs(own_lists, cols, rows[16:24], r0)
    cross_lists = close_lists((low, high), boxes(around[16:24], SUB), cross_flags)
    w0 = apply_pairs(cross_lists, cols, around[16:24], around[0:16], part)
    w0_around = jnp.concatenate([from_behind(w0, "blk", 1), from_behind(w0, "blk", -1)], axis=1)
    w0_all = lax.all_gather(unsort(w0, rank), "rep", axis=0, tiled=True)
    part = apply_pairs(own_lists, cols, rows[16:24], w0)
    w1 = apply_pairs(cross_lists, cols, around[16:24], w0_around, part)
    w1_all = lax.all_gather(unsort(w1, rank), "rep", axis=0, tiled=True)

    sums = sum_over_blk(
        jnp.stack([jnp.sum(a * b, axis=1) for a, b in ((r0, r0), (r0, w0), (w0, w0), (w0, w1))])
    )
    s00, s01, s11, s12 = (sums[k] for k in range(4))
    image_norm = shift * s00 + s01
    alpha = s00 / image_norm
    keep = s01 / image_norm
    rr1 = alpha * alpha * (s11 - s01 * (s01 / s00))
    beta = rr1 / s00
    both = keep + beta
    curved = both * both * s01 - 2.0 * both * alpha * s11 + alpha * alpha * s12
    alpha1 = rr1 / (shift * rr1 * (1.0 + beta) + curved)
    factors = jnp.stack(
        [
            (s00 + s01) / image_norm - noise_level * alpha1 * both,
            noise_level * alpha1 * alpha,
            keep - shift * alpha1 * both,
            shift * alpha1 * alpha - alpha - alpha1 * both,
            alpha1 * alpha,
        ]
    )
    spread = jnp.zeros((5, 4, sides), jnp.float32)
    for mask in range(4):
        piece = factors if mask == 0 else exchange(factors, mask, "rep")
        spread = lax.dynamic_update_slice_in_dim(spread, piece[:, None], member ^ mask, 1)
    factor = spread.reshape(5, 4 * sides, 1)
    posterior = factor[0] * right_side + factor[1] * w0_all
    residual = factor[2] * right_side + factor[3] * w0_all + factor[4] * w1_all
    return (posterior, residual)


def solution(mesh):
    return jax.shard_map(
        shards,
        mesh=mesh,
        in_specs=(P(None, "blk"), P(None, "blk"), P()),
        out_specs=(P(None, "blk"), P(None, "blk")),
        check_vma=False,
    )
```

time: 690 us -> 189 us (0.27)
  blocking collectives: 380 us -> 0 us
  matrix products: 161 us -> 1.07 us
  Pallas kernels: 0 us -> 90.2 us
  waiting for transfers between devices: 99.6 us -> 13.7 us
  starting transfers between devices: 11.6 us -> 35 us
  local copies, waits for them, and re-layouts: 2.58 us -> 19.7 us
    psum x3 -> x0, blocking collectives: 380 us -> none  [the longest x2 252 us: squares(): return lax.psum(jnp.sum(residual * residual, axis=1), 'blk')]
    dot_general x24 -> x2, matrix products: 161 us -> 1.07 us  [close_lists(): place = jnp.dot(near, order.astype(jnp.float32)).astype(jnp.int32)]
    psum x2 -> x0, waiting for transfers between devices: 99.6 us -> none  [matvec(): total = lax.psum(own_full + returned, 'rep')]
    pallas_call x0 -> x7, Pallas kernels: none -> 90.2 us  [the longest x4 77.3 us: apply_pairs(): pl.pallas_call(partial(apply_kernel, own, tiles, table.shape[1]), out_sha...]
    ppermute x0 -> x12, starting transfers between devices: none -> 22.5 us  [exchange(): return lax.ppermute(values, axis, [(i, i ^ mask) for i in devices])]
    ppermute x0 -> x12, waiting for transfers between devices: none -> 13.6 us  [exchange(): return lax.ppermute(values, axis, [(i, i ^ mask) for i in devices])]
    unnamed x4 -> x37, local copies, waits for them, and re-layouts: 0.01 us -> 8.18 us
  transfers between devices with their start and end apart: 7 -> 18, of which waited for: 2 -> 9; matrix products, arithmetic and copies ran while one was open for 23% -> 7% of each run, Pallas kernels for 0% -> 38%
where the time goes in v1:
time: 189 us; the launch traced here: 186 us
  Pallas kernels  90.2 us (48%)
  starting transfers between devices  35 us (19%)
  local copies, waits for them, and re-layouts  19.7 us (10%)
  between operations  14.5 us (8%)
  waiting for transfers between devices  13.7 us (7%)
  other arithmetic  11.7 us (6%)
    pallas_call x4, Pallas kernels, apply_pairs(): pl.pallas_call(partial(apply_kernel, own, tiles, table.shape[1]), out_sha...  77.3 us
    ppermute x12, starting transfers between devices, exchange(): return lax.ppermute(values, axis, [(i, i ^ mask) for i in devices])  22.5 us
    ppermute x12, waiting for transfers between devices, exchange(): return lax.ppermute(values, axis, [(i, i ^ mask) for i in devices])  13.6 us
    ppermute x4, starting transfers between devices, from_behind(): return lax.ppermute(block, axis, route)  12.5 us
    unnamed x37, local copies, waits for them, and re-layouts  8.18 us
    pallas_call x2, Pallas kernels, unsort(): pl.pallas_call(unsort_kernel, out_shape=jax.ShapeDtypeStruct(values.shape...  7.01 us
    pallas_call x1, Pallas kernels, sort_points(): pl.pallas_call(sort_kernel, out_shape=(jax.ShapeDtypeStruct((24, width),...  5.87 us
    reduce_sum x2, other arithmetic, close_lists(): table = jnp.sum(jnp.where(match, source - columns, 0), axis=2) + columns  3.86 us
  transfers between devices with their start and end apart: 18, of which 9 were waited for; matrix products, arithmetic and copies ran while one was open for 7% of the time, Pallas kernels for 38%

profile of v1, /device:TPU:8, one launch (start us, length us, event | category | flops | bytes accessed | tf_op | source)
XLA Modules:
  0.0 185.9 jit_solution(1603745125213434957)
XLA Ops:
  7.2 1.0 constant_dynamic-slice_fusion.vector_ref
  9.0 5.9 %sort_points.1 = (f32[24,4096]{1,0:T(8,128)S(1)}, f32[4096,128]{1,0:T(8,128)S(1)}, s32[8,4096]{1,0:T(8,128)S(1)}) custom-call(f32[3,4096]{1,0:T(4,128)S(1)} %copy-done.9, f32[16,4096]{1,0:T(8,128)S(1)} %constant_dynamic-slice_fusion.vector_ref), custom_call_target="tpu_custom_call" | custom-call | tf_op jit(solution)/shard_map/sort_points/pallas_call | solution.py:119
  14.9 2.5 %collective-permute-start = (f32[24,4096]{1,0:T(8,128)S(1)}, f32[24,4096]{1,0:T(8,128)}, u32[]{:S(2)}, u32[]{:S(2)}) collective-permute-start(f32[24,4096]{1,0:T(8,128)S(1)} %get-tuple-element.5), channel_id=1, source_target_pairs={{0,4},{4,8},{8,12},{12,16},{16,20},{20,24},{24,28},{28,32},{32,36}... | collective-permute-start | bytes 1179656 | tf_op jit(solution)/shard_map/ppermute | solution.py:32
  17.4 1.3 collective-permute-start.1
  22.6 2.6 %stack.31 = f32[8]{0:T(128)S(1)} concatenate(f32[1]{0:T(128)} %bitcast.1, f32[1]{0:T(128)} %bitcast.2, f32[2]{0:T(128)S(1)} %get-tuple-element.19, f32[1]{0:T(128)} %bitcast.3, f32[1]{0:T(128)} %bitcast.4, f32[2]{0:T(128)S(1)} %get-tuple-element.18), dimensions={0} | concatenate | bytes 64 | tf_op jit(solution)/shard_map/stack | solution.py:318
  26.9 28.0 %apply_own.2.rest_0_ = f32[16,4096]{1,0:T(8,128)S(1)} custom-call(s32[32]{0:T(128)S(1)} %get-tuple-element.48.counts_ref, s32[2176]{0:T(1024)S(1)} %add.153.list_ref, f32[4096,128]{1,0:T(8,128)S(1)} %get-tuple-element.6.cols_ref, f32[8,4096]{1,0:T(8,128)S(1)} %slice.124.coords_ref, f32[16,4096]{1,0:T(8,128)S(1)} %slice.105.vec_ref), custom_call_target="tpu_custom_call" | custom-call | tf_op jit(solution)/shard_map/apply_own/pallas_call | solution.py:266
  56.1 1.8 constant_dynamic-update-slice_fusion.1
  58.6 1.0 slice.134
  60.9 1.0 slice.135.coords_ref
  61.9 1.1 slice.136.vec_ref
  63.0 3.1 %select_reduce_fusion = s32[32,132]{0,1:T(8,128)S(1)} fusion(s32[128]{0:T(128)} %iota_add_fusion.3, s32[32,128]{1,0:T(8,128)S(1)} %get-tuple-element.47, s32[132]{0:T(256)} %iota_add_fusion, pred[32,128]{1,0:T(8,128)(4,1)S(1)} %broadcast_compare_fusion.1), kind=kLoop, calls=%fused_computation | loop fusion | flops 2158464 | bytes 38416 | tf_op jit(solution)/shard_map/reduce_sum | solution.py:307
  66.9 0.9 copy-done.3
  69.3 10.7 %apply_cross.2.vec_ref.sorted_ref = f32[16,4096]{1,0:T(8,128)S(1)} custom-call(s32[32]{0:T(128)S(1)} %copy-done.10, s32[4224]{0:T(1024)S(1)} %copy-done.7, f32[4096,128]{1,0:T(8,128)S(1)} %get-tuple-element.6.cols_ref, f32[8,8192]{1,0:T(8,128)S(1)} %slice.135.coords_ref, f32[16,8192]{1,0:T(8,128)S(1)} %slice.136.vec_ref, f32[16,4096]{1,0:T(8,128)S(1)} %copy-done.3), custom_call_target="tpu_custom_call" | custom-call | tf_op jit(solution)/shard_map/apply_cross/pallas_call | solution.py:266
  80.9 3.5 %unsort.2 = f32[16,4096]{1,0:T(8,128)} custom-call(f32[16,4096]{1,0:T(8,128)S(1)} %apply_cross.2.vec_ref.sorted_ref, s32[8,4096]{1,0:T(8,128)S(1)} %copy-done.5), custom_call_target="tpu_custom_call" | custom-call | tf_op jit(solution)/shard_map/unsort/pallas_call | solution.py:151
  84.4 1.3 collective-permute-start.3
  85.7 7.4 %collective-permute-start.2 = (f32[16,4096]{1,0:T(8,128)S(1)}, f32[16,4096]{1,0:T(8,128)}, u32[]{:S(2)}, u32[]{:S(2)}) collective-permute-start(f32[16,4096]{1,0:T(8,128)S(1)} %apply_cross.2.vec_ref.sorted_ref), channel_id=1, source_target_pairs={{0,4},{4,8},{8,12},{12,16},{16,20},{20,24},{24,28},{28,32},{32,36}... | collective-permute-start | bytes 786440 | tf_op jit(solution)/shard_map/ppermute | solution.py:32
  94.1 28.0 %apply_own.3.rest_0_ = f32[16,4096]{1,0:T(8,128)S(1)} custom-call(s32[32]{0:T(128)S(1)} %get-tuple-element.48.counts_ref, s32[2176]{0:T(1024)S(1)} %add.153.list_ref, f32[4096,128]{1,0:T(8,128)S(1)} %get-tuple-element.6.cols_ref, f32[8,4096]{1,0:T(8,128)S(1)} %copy-done.1, f32[16,4096]{1,0:T(8,128)S(1)} %apply_cross.2.vec_ref.sorted_ref), custom_call_target="tpu_custom_call" | custom-call | tf_op jit(solution)/shard_map/apply_own/pallas_call | solution.py:266
  122.1 1.0 pad_maximum_fusion.vec_ref
  124.5 10.7 %apply_cross.3.sorted_ref = f32[16,4096]{1,0:T(8,128)S(1)} custom-call(s32[32]{0:T(128)S(1)} %copy-done.11, s32[4224]{0:T(1024)S(1)} %copy-done.8, f32[4096,128]{1,0:T(8,128)S(1)} %get-tuple-element.6.cols_ref, f32[8,8192]{1,0:T(8,128)S(1)} %slice.135.coords_ref, f32[16,8192]{1,0:T(8,128)S(1)} %pad_maximum_fusion.vec_ref, f32[16,4096]{1,0:T(8,128)S(1)} %apply_own.3.rest_0_), custom_call_target="tpu_custom_call" | custom-call | tf_op jit(solution)/shard_map/apply_cross/pallas_call | solution.py:266
  135.2 3.5 %unsort.3 = f32[16,4096]{1,0:T(8,128)} custom-call(f32[16,4096]{1,0:T(8,128)S(1)} %apply_cross.3.sorted_ref, s32[8,4096]{1,0:T(8,128)S(1)} %copy-done.6), custom_call_target="tpu_custom_call" | custom-call | tf_op jit(solution)/shard_map/unsort/pallas_call | solution.py:151
  138.9 4.1 %collective-permute-start.5 = (f32[4,16]{1,0:T(4,128)S(1)}, f32[4,16]{1,0:T(4,128)S(1)}, u32[]{:S(2)}, u32[]{:S(2)}) collective-permute-start(f32[4,16]{1,0:T(4,128)S(1)} %pad_maximum_fusion.1), channel_id=1, source_target_pairs={{0,8},{4,12},{8,0},{12,4},{16,24},{20,28},{24,16},{28,20},{32,40},... | collective-permute-start | bytes 776 | tf_op jit(solution)/shard_map/ppermute | solution.py:37
  144.6 1.4 collective-permute-done.6
  146.1 8.7 %collective-permute-start.8 = (f32[4,16]{1,0:T(4,128)S(1)}, f32[4,16]{1,0:T(4,128)S(1)}, u32[]{:S(2)}, u32[]{:S(2)}) collective-permute-start(f32[4,16]{1,0:T(4,128)S(1)} %add_add_fusion.2), channel_id=1, source_target_pairs={{0,32},{4,36},{8,40},{12,44},{16,48},{20,52},{24,56},{28,60},{32,0... | collective-permute-start | bytes 776 | tf_op jit(solution)/shard_map/ppermute | solution.py:37
  154.8 1.8 collective-permute-start.9
  156.5 3.9 %collective-permute-done.9 = f32[4,16]{1,0:T(4,128)S(1)} collective-permute-done((f32[4,16]{1,0:T(4,128)S(1)}, f32[4,16]{1,0:T(4,128)S(1)}, u32[]{:S(2)}, u32[]{:S(2)}) %collective-permute-start.9) | collective-permute-done | bytes 288 | tf_op jit(solution)/shard_map/ppermute | solution.py:37
  161.0 2.6 %collective-permute-start.11 = (f32[4,16]{1,0:T(4,128)S(1)}, f32[4,16]{1,0:T(4,128)S(1)}, u32[]{:S(2)}, u32[]{:S(2)}) collective-permute-start(f32[4,16]{1,0:T(4,128)S(1)} %add_add_fusion.1), channel_id=1, source_target_pairs={{0,128},{4,132},{8,136},{12,140},{16,144},{20,148},{24,152},{28,15... | collective-permute-start | bytes 776 | tf_op jit(solution)/shard_map/ppermute | solution.py:37
  164.7 1.5 collective-permute-done.11
  166.1 2.3 %collective-permute-done.12 = f32[4,16]{1,0:T(4,128)S(1)} collective-permute-done((f32[4,16]{1,0:T(4,128)S(1)}, f32[4,16]{1,0:T(4,128)S(1)}, u32[]{:S(2)}, u32[]{:S(2)}) %collective-permute-start.12) | collective-permute-done | bytes 288 | tf_op jit(solution)/shard_map/ppermute | solution.py:37
  169.0 2.6 %collective-permute-start.14 = (f32[5,16]{1,0:T(8,128)S(1)}, f32[5,16]{1,0:T(8,128)S(1)}, u32[]{:S(2)}, u32[]{:S(2)}) collective-permute-start(f32[5,16]{1,0:T(8,128)S(1)} %stack.37), channel_id=1, source_target_pairs={{0,2},{1,3},{2,0},{3,1},{4,6},{5,7},{6,4},{7,5},{8,10},{9,11},{10,... | collective-permute-start | bytes 968 | tf_op jit(solution)/shard_map/ppermute | solution.py:37
  172.2 1.9 %collective-permute-done.14 = f32[5,16]{1,0:T(8,128)S(1)} collective-permute-done((f32[5,16]{1,0:T(8,128)S(1)}, f32[5,16]{1,0:T(8,128)S(1)}, u32[]{:S(2)}, u32[]{:S(2)}) %collective-permute-start.14) | collective-permute-done | bytes 352 | tf_op jit(solution)/shard_map/ppermute | solution.py:37
  174.2 1.1 collective-permute-done.15
  175.8 3.2 %multiply_add_fusion = (f32[64,4096]{1,0:T(8,128)}, f32[64,4096]{1,0:T(8,128)}) fusion(f32[64,4096]{1,0:T(8,128)} %all-gather.5.cloned.1.call-done, f32[64,4096]{1,0:T(8,128)} %all-gather.3.cloned.1.call-done, f32[64,4096]{1,0:T(8,128)S(1)} %copy-done.12, f32[64]{0:T(128)S(1)} %mul.305, f32[64]{0:T(128)S(1)} %mul.302, f32[64]{0:T(128)S(1)} %mul.299, ...), kind=kLoop, calls=%fused_computation.3 | loop fusion | flops 2097152 | bytes 5244160 | tf_op jit(solution)/shard_map/add | solution.py:373
  (118 shorter events, 20.1 us)
Async XLA Ops:
  7.2 168.6 %all-gather.3.cloned.1.call-start = ((), (), s32[]{:S(2)}) async-start(), calls=%async_computation | async-start | bytes 1310720 | tf_op jit(solution)/shard_map/all_gather | solution.py:341
  8.2 0.8 copy-start.9
  14.9 12.0 %copy-start.4 = (s32[8,4096]{1,0:T(8,128)}, s32[8,4096]{1,0:T(8,128)S(1)}, u32[]{:S(2)}) copy-start(s32[8,4096]{1,0:T(8,128)S(1)} %get-tuple-element.7.rank_ref) | copy-start | bytes 393220
  14.9 41.2 %collective-permute-start = (f32[24,4096]{1,0:T(8,128)S(1)}, f32[24,4096]{1,0:T(8,128)}, u32[]{:S(2)}, u32[]{:S(2)}) collective-permute-start(f32[24,4096]{1,0:T(8,128)S(1)} %get-tuple-element.5), channel_id=1, source_target_pairs={{0,4},{4,8},{8,12},{12,16},{16,20},{20,24},{24,28},{28,32},{32,36}... | collective-permute-start | bytes 1179656 | tf_op jit(solution)/shard_map/ppermute | solution.py:32
  17.4 40.4 %collective-permute-start.1 = (f32[24,4096]{1,0:T(8,128)S(1)}, f32[24,4096]{1,0:T(8,128)S(1)}, u32[]{:S(2)}, u32[]{:S(2)}) collective-permute-start(f32[24,4096]{1,0:T(8,128)S(1)} %get-tuple-element.5), channel_id=1, source_target_pairs={{4,0},{8,4},{12,8},{16,12},{20,16},{24,20},{28,24},{32,28},{36,32}... | collective-permute-start | bytes 1179656 | tf_op jit(solution)/shard_map/ppermute | solution.py:32
  18.9 7.2 %copy-start.14 = (f32[3,32]{1,0:T(4,128)}, f32[3,32]{1,0:T(4,128)S(1)}, u32[]{:S(2)}) copy-start(f32[3,32]{1,0:T(4,128)S(1)} %get-tuple-element.16) | copy-start | bytes 1156
  18.9 7.2 %copy-start.16 = (f32[3,32]{1,0:T(4,128)}, f32[3,32]{1,0:T(4,128)S(1)}, u32[]{:S(2)}) copy-start(f32[3,32]{1,0:T(4,128)S(1)} %get-tuple-element.17) | copy-start | bytes 1156
  21.9 36.0 %copy-start = (f32[8,4096]{1,0:T(8,128)}, f32[8,4096]{1,0:T(8,128)S(1)}, u32[]{:S(2)}) copy-start(f32[8,4096]{1,0:T(8,128)S(1)} %slice.124.coords_ref) | copy-start | bytes 393220
  54.9 6.0 %copy-start.2 = (f32[16,4096]{1,0:T(8,128)}, f32[16,4096]{1,0:T(8,128)S(1)}, u32[]{:S(2)}) copy-start(f32[16,4096]{1,0:T(8,128)S(1)} %apply_own.2.rest_0_) | copy-start | bytes 786436
  54.9 5.0 %copy-start.15 = (f32[3,32]{1,0:T(4,128)S(1)}, f32[3,32]{1,0:T(4,128)}, u32[]{:S(2)}) copy-start(f32[3,32]{1,0:T(4,128)} %copy-done.14) | copy-start | bytes 1156
  54.9 5.0 %copy-start.17 = (f32[3,32]{1,0:T(4,128)S(1)}, f32[3,32]{1,0:T(4,128)}, u32[]{:S(2)}) copy-start(f32[3,32]{1,0:T(4,128)} %copy-done.16) | copy-start | bytes 1156
  55.0 5.1 %copy-start.13 = (f32[32,128]{1,0:T(8,128)S(1)}, f32[32,128]{1,0:T(8,128)}, u32[]{:S(2)}) copy-start(f32[32,128]{1,0:T(8,128)} %mul.263) | copy-start | bytes 49156
  66.9 0.9 copy-start.3
  79.9 0.9 copy-start.5
  84.4 91.4 %all-gather.5.cloned.1.call-start = ((), (), s32[]{:S(2)}) async-start(), calls=%async_computation.1 | async-start | bytes 1310720 | tf_op jit(solution)/shard_map/all_gather | solution.py:344
  84.4 37.6 %collective-permute-start.3 = (f32[16,4096]{1,0:T(8,128)S(1)}, f32[16,4096]{1,0:T(8,128)S(1)}, u32[]{:S(2)}, u32[]{:S(2)}) collective-permute-start(f32[16,4096]{1,0:T(8,128)S(1)} %apply_cross.2.vec_ref.sorted_ref), channel_id=1, source_target_pairs={{4,0},{8,4},{12,8},{16,12},{20,16},{24,20},{28,24},{32,28},{36,32}... | collective-permute-start | bytes 786440 | tf_op jit(solution)/shard_map/ppermute | solution.py:32
  85.7 36.4 %collective-permute-start.2 = (f32[16,4096]{1,0:T(8,128)S(1)}, f32[16,4096]{1,0:T(8,128)}, u32[]{:S(2)}, u32[]{:S(2)}) collective-permute-start(f32[16,4096]{1,0:T(8,128)S(1)} %apply_cross.2.vec_ref.sorted_ref), channel_id=1, source_target_pairs={{0,4},{4,8},{8,12},{12,16},{16,20},{20,24},{24,28},{28,32},{32,36}... | collective-permute-start | bytes 786440 | tf_op jit(solution)/shard_map/ppermute | solution.py:32
  93.2 0.9 copy-start.1
  122.1 13.1 %copy-start.6 = (s32[8,4096]{1,0:T(8,128)S(1)}, s32[8,4096]{1,0:T(8,128)}, u32[]{:S(2)}) copy-start(s32[8,4096]{1,0:T(8,128)} %copy-done.4) | copy-start | bytes 393220
  135.2 40.6 %copy-start.12 = (f32[64,4096]{1,0:T(8,128)S(1)}, f32[64,4096]{1,0:T(8,128)}, u32[]{:S(2)}) copy-start(f32[64,4096]{1,0:T(8,128)} %param.3) | copy-start | bytes 3145732
  138.9 5.7 %collective-permute-start.5 = (f32[4,16]{1,0:T(4,128)S(1)}, f32[4,16]{1,0:T(4,128)S(1)}, u32[]{:S(2)}, u32[]{:S(2)}) collective-permute-start(f32[4,16]{1,0:T(4,128)S(1)} %pad_maximum_fusion.1), channel_id=1, source_target_pairs={{0,8},{4,12},{8,0},{12,4},{16,24},{20,28},{24,16},{28,20},{32,40},... | collective-permute-start | bytes 776 | tf_op jit(solution)/shard_map/ppermute | solution.py:37
  143.1 3.0 %collective-permute-start.6 = (f32[4,16]{1,0:T(4,128)S(1)}, f32[4,16]{1,0:T(4,128)S(1)}, u32[]{:S(2)}, u32[]{:S(2)}) collective-permute-start(f32[4,16]{1,0:T(4,128)S(1)} %pad_maximum_fusion.1), channel_id=1, source_target_pairs={{0,12},{4,8},{8,4},{12,0},{16,28},{20,24},{24,20},{28,16},{32,44},... | collective-permute-start | bytes 776 | tf_op jit(solution)/shard_map/ppermute | solution.py:37
  143.8 2.3 %collective-permute-start.4 = (f32[4,16]{1,0:T(4,128)S(1)}, f32[4,16]{1,0:T(4,128)S(1)}, u32[]{:S(2)}, u32[]{:S(2)}) collective-permute-start(f32[4,16]{1,0:T(4,128)S(1)} %pad_maximum_fusion.1), channel_id=1, source_target_pairs={{0,4},{4,0},{8,12},{12,8},{16,20},{20,16},{24,28},{28,24},{32,36},... | collective-permute-start | bytes 776 | tf_op jit(solution)/shard_map/ppermute | solution.py:37
  146.1 10.5 %collective-permute-start.8 = (f32[4,16]{1,0:T(4,128)S(1)}, f32[4,16]{1,0:T(4,128)S(1)}, u32[]{:S(2)}, u32[]{:S(2)}) collective-permute-start(f32[4,16]{1,0:T(4,128)S(1)} %add_add_fusion.2), channel_id=1, source_target_pairs={{0,32},{4,36},{8,40},{12,44},{16,48},{20,52},{24,56},{28,60},{32,0... | collective-permute-start | bytes 776 | tf_op jit(solution)/shard_map/ppermute | solution.py:37
  154.8 5.7 %collective-permute-start.9 = (f32[4,16]{1,0:T(4,128)S(1)}, f32[4,16]{1,0:T(4,128)S(1)}, u32[]{:S(2)}, u32[]{:S(2)}) collective-permute-start(f32[4,16]{1,0:T(4,128)S(1)} %add_add_fusion.2), channel_id=1, source_target_pairs={{0,48},{4,52},{8,56},{12,60},{16,32},{20,36},{24,40},{28,44},{32,1... | collective-permute-start | bytes 776 | tf_op jit(solution)/shard_map/ppermute | solution.py:37
  156.5 4.5 %collective-permute-start.7 = (f32[4,16]{1,0:T(4,128)S(1)}, f32[4,16]{1,0:T(4,128)S(1)}, u32[]{:S(2)}, u32[]{:S(2)}) collective-permute-start(f32[4,16]{1,0:T(4,128)S(1)} %add_add_fusion.2), channel_id=1, source_target_pairs={{0,16},{4,20},{8,24},{12,28},{16,0},{20,4},{24,8},{28,12},{32,48},... | collective-permute-start | bytes 776 | tf_op jit(solution)/shard_map/ppermute | solution.py:37
  161.0 5.1 %collective-permute-start.11 = (f32[4,16]{1,0:T(4,128)S(1)}, f32[4,16]{1,0:T(4,128)S(1)}, u32[]{:S(2)}, u32[]{:S(2)}) collective-permute-start(f32[4,16]{1,0:T(4,128)S(1)} %add_add_fusion.1), channel_id=1, source_target_pairs={{0,128},{4,132},{8,136},{12,140},{16,144},{20,148},{24,152},{28,15... | collective-permute-start | bytes 776 | tf_op jit(solution)/shard_map/ppermute | solution.py:37
  163.6 4.8 %collective-permute-start.12 = (f32[4,16]{1,0:T(4,128)S(1)}, f32[4,16]{1,0:T(4,128)S(1)}, u32[]{:S(2)}, u32[]{:S(2)}) collective-permute-start(f32[4,16]{1,0:T(4,128)S(1)} %add_add_fusion.1), channel_id=1, source_target_pairs={{0,192},{4,196},{8,200},{12,204},{16,208},{20,212},{24,216},{28,22... | collective-permute-start | bytes 776 | tf_op jit(solution)/shard_map/ppermute | solution.py:37
  163.9 4.5 %collective-permute-start.10 = (f32[4,16]{1,0:T(4,128)S(1)}, f32[4,16]{1,0:T(4,128)S(1)}, u32[]{:S(2)}, u32[]{:S(2)}) collective-permute-start(f32[4,16]{1,0:T(4,128)S(1)} %add_add_fusion.1), channel_id=1, source_target_pairs={{0,64},{4,68},{8,72},{12,76},{16,80},{20,84},{24,88},{28,92},{32,9... | collective-permute-start | bytes 776 | tf_op jit(solution)/shard_map/ppermute | solution.py:37
  168.5 3.7 %collective-permute-start.13 = (f32[5,16]{1,0:T(8,128)S(1)}, f32[5,16]{1,0:T(8,128)S(1)}, u32[]{:S(2)}, u32[]{:S(2)}) collective-permute-start(f32[5,16]{1,0:T(8,128)S(1)} %stack.37), channel_id=1, source_target_pairs={{0,1},{1,0},{2,3},{3,2},{4,5},{5,4},{6,7},{7,6},{8,9},{9,8},{10,11... | collective-permute-start | bytes 968 | tf_op jit(solution)/shard_map/ppermute | solution.py:37
  169.0 5.1 %collective-permute-start.14 = (f32[5,16]{1,0:T(8,128)S(1)}, f32[5,16]{1,0:T(8,128)S(1)}, u32[]{:S(2)}, u32[]{:S(2)}) collective-permute-start(f32[5,16]{1,0:T(8,128)S(1)} %stack.37), channel_id=1, source_target_pairs={{0,2},{1,3},{2,0},{3,1},{4,6},{5,7},{6,4},{7,5},{8,10},{9,11},{10,... | collective-permute-start | bytes 968 | tf_op jit(solution)/shard_map/ppermute | solution.py:37
  171.6 3.6 %collective-permute-start.15 = (f32[5,16]{1,0:T(8,128)S(1)}, f32[5,16]{1,0:T(8,128)S(1)}, u32[]{:S(2)}, u32[]{:S(2)}) collective-permute-start(f32[5,16]{1,0:T(8,128)S(1)} %stack.37), channel_id=1, source_target_pairs={{0,3},{1,2},{2,1},{3,0},{4,7},{5,6},{6,5},{7,4},{8,11},{9,10},{10,... | collective-permute-start | bytes 968 | tf_op jit(solution)/shard_map/ppermute | solution.py:37
  (4 other events, 2.8 us)
Sparse Core Ops, SparseCore 0:
  84.5 34.7 all-gather.2
  143.9 30.7 all-gather.4

commit v2 on v1

v2 whole, which is shorter than its diff:
```python
from functools import partial

import jax
import jax.numpy as jnp
from jax import lax
from jax.experimental import pallas as pl
from jax.experimental.pallas import tpu as pltpu
from jax.sharding import PartitionSpec as P

B = 2048
SUB = 64
TILE = 128
STRIP = 256
BATCH = 4
CELLS_X = 4
CELLS_Y = 8
CELLS = CELLS_X * CELLS_Y
FAR = 1.0e6

support_radius = 2.5
noise_level = 8.0
shift = noise_level + 1.0
profile_scale = 4.0 / support_radius**5
VMEM = pl.BlockSpec(memory_space=pltpu.VMEM)
SMEM = pl.BlockSpec(memory_space=pltpu.SMEM)
PARAMS = pltpu.CompilerParams(vmem_limit_bytes=48 * 1024 * 1024)


def from_behind(block, axis, distance):
    devices = range(lax.axis_size(axis))
    route = [(i - distance, i) for i in devices if i - distance in devices]
    return lax.ppermute(block, axis, route)


def exchange(values, mask, axis):
    devices = range(lax.axis_size(axis))
    return lax.ppermute(values, axis, [(i, i ^ mask) for i in devices])


def sum_over_blk(values):
    for base in (1, 4, 16):
        near = values + exchange(values, base, "blk")
        far = exchange(values, 2 * base, "blk") + exchange(values, 3 * base, "blk")
        values = near + far
    return values


def split3(values):
    high = values.astype(jnp.bfloat16)
    rest = values - high.astype(jnp.float32)
    middle = rest.astype(jnp.bfloat16)
    low = (rest - middle.astype(jnp.float32)).astype(jnp.bfloat16)
    return high, middle, low


def one_hot_strip(rank, start):
    place = lax.broadcasted_iota(jnp.int32, (STRIP, B), 0) + start
    return jnp.where(rank == place, 1.0, 0.0).astype(jnp.bfloat16)


def cell_of(values, cells):
    low = jnp.min(values, axis=1, keepdims=True)
    high = jnp.max(values, axis=1, keepdims=True)
    scaled = (values - low) * (cells / jnp.maximum(high - low, 1e-30))
    return jnp.minimum(jnp.floor(scaled), cells - 1.0)


def sort_kernel(
    place_ref,
    points_ref,
    sides_ref,
    rows_ref,
    cols_ref,
    rank_ref,
    box_ref,
    vector_ref,
    feature_ref,
    split_ref,
    edge_ref,
    arrived,
):
    first = pl.multiple_of(place_ref[1] * 16, 16)
    fetch = pltpu.make_async_copy(sides_ref.at[pl.ds(first, 16), :], vector_ref, arrived)
    fetch.start()
    upper = lax.broadcasted_iota(jnp.int32, (TILE, TILE), 0) <= lax.broadcasted_iota(
        jnp.int32, (TILE, TILE), 1
    )
    upper = jnp.where(upper, 1.0, 0.0).astype(jnp.bfloat16)
    lower = lax.broadcasted_iota(jnp.int32, (CELLS, CELLS), 0) > lax.broadcasted_iota(
        jnp.int32, (CELLS, CELLS), 1
    )
    lower = jnp.where(lower, 1.0, 0.0)
    number = lax.broadcasted_iota(jnp.int32, (CELLS, TILE), 0).astype(jnp.float32)
    feature_ref[16:32, :] = jnp.zeros((16, B), jnp.float32)
    split_ref[96:128, :] = jnp.zeros((32, B), jnp.bfloat16)
    for c in range(2):
        span = slice(c * B, (c + 1) * B)
        cell = cell_of(points_ref[0:1, span], CELLS_X) * CELLS_Y + cell_of(
            points_ref[1:2, span], CELLS_Y
        )
        base = jnp.zeros((CELLS, TILE), jnp.float32)
        chosen, place = [], []
        for t in range(B // TILE):
            hit = jnp.where(number == cell[:, t * TILE : (t + 1) * TILE], 1.0, 0.0)
            count = jnp.dot(hit.astype(jnp.bfloat16), upper, preferred_element_type=jnp.float32)
            chosen.append(hit)
            place.append(count + base)
            base = base + count[:, TILE - 1 :]
        offset = jnp.dot(
            lower, base, precision=lax.Precision.HIGHEST, preferred_element_type=jnp.float32
        )
        for t in range(B // TILE):
            rank = jnp.sum(chosen[t] * (place[t] + (offset - 1.0)), axis=0, keepdims=True)
            rank_ref[0:1, c * B + t * TILE : c * B + (t + 1) * TILE] = rank.astype(jnp.int32)
        if c == 0:
            fetch.wait()
        feature_ref[0:16, :] = vector_ref[:, span]
        feature_ref[16:19, :] = points_ref[:, span]
        for k, part in enumerate(split3(feature_ref[...])):
            split_ref[32 * k : 32 * k + 32, :] = part
        rank = rank_ref[0:1, span]
        for k in range(B // STRIP):
            found = lax.dot_general(
                one_hot_strip(rank, k * STRIP),
                split_ref[...],
                (((1,), (1,)), ((), ())),
                preferred_element_type=jnp.float32,
            )
            found = found + pltpu.roll(found, 96, 1) + pltpu.roll(found, 64, 1)
            spot = slice(c * B + k * STRIP, c * B + (k + 1) * STRIP)
            cols_ref[spot, :] = found
            rows_ref[:, spot] = found.T[0:24, :]
            for t in range(STRIP // SUB):
                chunk = c * (B // SUB) + k * (STRIP // SUB) + t
                piece = found[t * SUB : (t + 1) * SUB, :]
                for e, edge in enumerate((jnp.min, jnp.max)):
                    value = edge(piece, axis=0, keepdims=True)
                    edge_ref[e, chunk : chunk + 1, :] = value
                    edge_ref[e, 64 + chunk : 65 + chunk, :] = value
            for t in range(STRIP // TILE):
                j = c * (B // TILE) + k * (STRIP // TILE) + t
                piece = found[t * TILE : (t + 1) * TILE, :]
                for e, edge in enumerate((jnp.min, jnp.max)):
                    box_ref[e, j : j + 1, :] = edge(piece, axis=0, keepdims=True)
    for e in range(2):
        turned = edge_ref[e].T
        for axis in range(3):
            rows_ref[19 + e : 20 + e, axis * TILE : (axis + 1) * TILE] = turned[
                16 + axis : 17 + axis, :
            ]


def sort_points(place, points, right_side):
    width = 2 * B
    return pl.pallas_call(
        sort_kernel,
        out_shape=(
            jax.ShapeDtypeStruct((24, width), jnp.float32),
            jax.ShapeDtypeStruct((width, TILE), jnp.float32),
            jax.ShapeDtypeStruct((8, width), jnp.int32),
            jax.ShapeDtypeStruct((2, width // TILE, TILE), jnp.float32),
        ),
        in_specs=[SMEM, VMEM, pl.BlockSpec(memory_space=pl.ANY)],
        out_specs=(VMEM, VMEM, VMEM, VMEM),
        scratch_shapes=[
            pltpu.VMEM((16, width), jnp.float32),
            pltpu.VMEM((32, B), jnp.float32),
            pltpu.VMEM((128, B), jnp.bfloat16),
            pltpu.VMEM((2, TILE, TILE), jnp.float32),
            pltpu.SemaphoreType.DMA,
        ],
        compiler_params=PARAMS,
        name="sort_points",
    )(place, points, right_side)


def unsort_kernel(sorted_ref, rank_ref, out_ref, split_ref, total_ref):
    for c in range(2):
        span = slice(c * B, (c + 1) * B)
        for k, part in enumerate(split3(sorted_ref[:, span])):
            split_ref[16 * k : 16 * k + 16, :] = part
        rank = rank_ref[0:1, span]
        for k in range(B // STRIP):
            found = jnp.dot(
                split_ref[:, k * STRIP : (k + 1) * STRIP],
                one_hot_strip(rank, k * STRIP),
                preferred_element_type=jnp.float32,
            )
            total_ref[...] = found if k == 0 else total_ref[...] + found
        out_ref[:, span] = (total_ref[0:16, :] + total_ref[16:32, :]) + total_ref[32:48, :]


def unsort(values, rank):
    return pl.pallas_call(
        unsort_kernel,
        out_shape=jax.ShapeDtypeStruct(values.shape, jnp.float32),
        in_specs=[VMEM, VMEM],
        out_specs=VMEM,
        scratch_shapes=[pltpu.VMEM((48, B), jnp.bfloat16), pltpu.VMEM((48, B), jnp.float32)],
        compiler_params=PARAMS,
        name="unsort",
    )(values, rank)


def pair_table(own, place_ref, active_ref, box_ref, xyz_refs, null):
    shape = (box_ref.shape[1], TILE)
    row = lax.broadcasted_iota(jnp.int32, shape, 0)
    lane = lax.broadcasted_iota(jnp.int32, shape, 1)
    total = jnp.zeros(shape, jnp.float32)
    for axis in range(3):
        low_t = box_ref[0, :, 16 + axis : 17 + axis]
        high_t = box_ref[1, :, 16 + axis : 17 + axis]
        span = slice(axis * TILE, (axis + 1) * TILE)
        edges = [[ref[19 + e : 20 + e, span] for e in range(2)] for ref in xyz_refs]
        if own:
            low_s, high_s = edges[0]
        else:
            is_before = lane[0:1] < SUB
            low_s, high_s = (jnp.where(is_before, edges[0][e], edges[1][e]) for e in range(2))
        gap = jnp.maximum(jnp.maximum(low_s - high_t, low_t - high_s), 0.0)
        total = total + gap * gap
    near = total <= support_radius * support_radius * (1.0 + 1e-4)
    column = place_ref[0]
    count = active_ref.shape[0]
    is_second = row >= shape[0] // 2
    quarter = lane // (TILE // 4)
    if own:
        across = active_ref[column, 0]
        same = is_second == (quarter == 1)
        flag = jnp.where(same, 1, across)
        flag = jnp.where(quarter < 2, flag, 0)
    else:
        behind = jnp.maximum(column - 1, 0)
        has_behind = jnp.where(column >= 1, 1, 0)
        has_ahead = jnp.where(column + 1 < count, 1, 0)
        flag = jnp.zeros(shape, jnp.int32)
        for c in range(2):
            for q in range(4):
                if q < 2:
                    value = active_ref[behind, 1 + 2 * q + c] * has_behind
                else:
                    value = active_ref[column, 1 + 2 * c + (q - 2)] * has_ahead
                here = (is_second == (c == 1)) & (quarter == q)
                flag = jnp.where(here, value, flag)
    near = near & (flag > 0)
    upper = lax.broadcasted_iota(jnp.int32, (TILE, TILE), 0) <= lax.broadcasted_iota(
        jnp.int32, (TILE, TILE), 1
    )
    place = jnp.dot(
        jnp.where(near, 1.0, 0.0).astype(jnp.bfloat16),
        jnp.where(upper, 1.0, 0.0).astype(jnp.bfloat16),
        preferred_element_type=jnp.float32,
    ).astype(jnp.int32)
    value = jnp.where(near, lane, null)
    left = jnp.where(near, lane + 1 - place, 0)
    for bit in range(7):
        amount = 1 << bit
        next_value = pltpu.roll(value, TILE - amount, 1)
        next_left = pltpu.roll(left, TILE - amount, 1)
        arrives = (next_left & amount) > 0
        stays = (left & amount) == 0
        value = jnp.where(arrives, next_value, jnp.where(stays, value, null))
        left = jnp.where(arrives, next_left, jnp.where(stays, left, 0))
    return value + 256 * place[:, TILE - 1 :]


def apply_kernel(own, sums, *refs):
    refs = list(refs)
    place_ref, active_ref, cols_ref, box_ref = refs[:4]
    del refs[:4]
    sources = 1 if own else 2
    xyz_refs = [refs.pop(0) for _ in range(sources)]
    vec_refs = [refs.pop(0) for _ in range(sources)]
    add_ref = None if own else refs.pop(0)
    base_refs = [refs.pop(0) for _ in range(2)] if sums else None
    out_ref = refs.pop(0)
    sums_ref = refs.pop(0) if sums else None
    left_xyz, right_xyz, left_w, right_w, target, tiles, weights, total_ref = refs[:8]
    table_ref, list_ref, arrived = refs[8:]
    rows = out_ref.shape[1] // TILE
    null = 2 * rows * sources
    lane = lax.broadcasted_iota(jnp.int32, (8, TILE), 1)
    is_left = lane < SUB

    table_ref[...] = pair_table(own, place_ref, active_ref, box_ref, xyz_refs, null)
    load = pltpu.make_async_copy(table_ref, list_ref, arrived)
    load.start()

    def spread(values):
        turned = pltpu.roll(values, SUB, 1)
        mask = jnp.concatenate([is_left] * (values.shape[0] // 8), axis=0)
        zero = jnp.zeros_like(values)
        return (
            jnp.where(mask, values, zero),
            jnp.where(mask, zero, turned),
            jnp.where(mask, turned, zero),
            jnp.where(mask, zero, values),
        )

    def parts(values):
        high = values.astype(jnp.bfloat16)
        low = (values - high.astype(jnp.float32)).astype(jnp.bfloat16)
        return jnp.concatenate([high, low], axis=0)

    for s in range(sources):

        def prepare(g, carry):
            for u in range(4):
                t = g * 4 + u
                spot = pl.ds(pl.multiple_of(t * TILE, TILE), TILE)
                slot = 2 * (t + s * rows)
                xyz = spread(xyz_refs[s][16:24, spot])
                left_xyz[slot] = xyz[0]
                right_xyz[slot] = xyz[1]
                left_xyz[slot + 1] = xyz[2]
                right_xyz[slot + 1] = xyz[3]
                vec = spread(vec_refs[s][0:16, spot])
                left_w[slot] = parts(vec[0])
                right_w[slot] = parts(vec[1])
                left_w[slot + 1] = parts(vec[2])
                right_w[slot + 1] = parts(vec[3])
            return carry

        lax.fori_loop(0, rows // 4, prepare, 0)
    left_xyz[null] = jnp.where(is_left, FAR, 0.0)
    right_xyz[null] = jnp.where(is_left, 0.0, FAR)
    left_w[null] = jnp.zeros((32, TILE), jnp.bfloat16)
    right_w[null] = jnp.zeros((32, TILE), jnp.bfloat16)
    total_ref[...] = jnp.zeros_like(total_ref)
    tiles[1] = jnp.zeros((TILE, 4 * TILE), jnp.bfloat16)
    weights[1] = jnp.zeros((32, 4 * TILE), jnp.bfloat16)

    def form(side, j, n):
        for s in range(2):
            first = list_ref[j, 4 * n + 2 * s] & 255
            second = list_ref[j, 4 * n + 2 * s + 1] & 255
            xyz = left_xyz[first] + right_xyz[second]
            weight = left_w[first] + right_w[second]
            near = slice(2 * s * TILE, (2 * s + 1) * TILE)
            far = slice((2 * s + 1) * TILE, (2 * s + 2) * TILE)
            weights[side, :, near] = weight
            weights[side, :, far] = weight
            for r in range(TILE // 16):
                span = slice(16 * r, 16 * r + 16)
                dx = target[3 * side, span, :] - xyz[0:1, :]
                dy = target[3 * side + 1, span, :] - xyz[1:2, :]
                dz = target[3 * side + 2, span, :] - xyz[2:3, :]
                square = jnp.maximum(dx * dx + dy * dy + dz * dz, 1e-30)
                distance = square * lax.rsqrt(square)
                inside = jnp.maximum(support_radius - distance, 0.0)
                inside = inside * inside
                value = (inside * inside) * (distance + 0.25 * support_radius)
                high = value.astype(jnp.bfloat16)
                tiles[side, span, near] = high
                tiles[side, span, far] = (value - high.astype(jnp.float32)).astype(jnp.bfloat16)

    def apply(side):
        return lax.dot_general(
            weights[side],
            tiles[side],
            (((1,), (1,)), ((), ())),
            preferred_element_type=jnp.float32,
        )

    load.wait()

    def row_pair(j, last):
        other = rows - 1 - j
        count = jnp.maximum(list_ref[j, 0], list_ref[other, 0]) // 256

        @pl.when(count > 0)
        def _():
            for side, k in enumerate((j, other)):
                spot = pl.ds(pl.multiple_of(k * TILE, TILE), TILE)
                for axis in range(3):
                    target[3 * side + axis] = jnp.broadcast_to(
                        cols_ref[spot, 16 + axis : 17 + axis], (TILE, TILE)
                    )

        def step(n, last):
            image = apply(1)
            form(0, j, n)
            total_ref[last] += image
            image = apply(0)
            form(1, other, n)
            total_ref[j] += image
            return other

        return lax.fori_loop(0, (count + BATCH - 1) // BATCH, step, last)

    last = lax.fori_loop(0, rows // 2, row_pair, 0)
    total_ref[last] += apply(1)

    def finish(g, running):
        for u in range(4):
            j = g * 4 + u
            spot = pl.ds(pl.multiple_of(j * TILE, TILE), TILE)
            total = total_ref[j]
            image = (total[0:16, :] + total[16:32, :]) * profile_scale
            if own:
                held = (left_w[2 * j] + right_w[2 * j + 1]).astype(jnp.float32)
                image = image - (held[0:16, :] + held[16:32, :])
            else:
                image = image + add_ref[:, spot]
            out_ref[:, spot] = image
            if sums:
                side = base_refs[0][0:16, spot]
                first = base_refs[1][:, spot]
                running = (
                    running[0] + side * side,
                    running[1] + side * first,
                    running[2] + first * first,
                    running[3] + first * image,
                )
        return running

    zero = jnp.zeros((16, TILE), jnp.float32)
    result = lax.fori_loop(0, rows // 4, finish, (zero,) * 4 if sums else 0)
    if sums:
        columns = lax.broadcasted_iota(jnp.int32, (16, TILE), 1)
        packed = zero
        for k in range(4):
            packed = jnp.where(columns == k, jnp.sum(result[k], axis=1, keepdims=True), packed)
        sums_ref[...] = packed


def apply_pairs(place, active, cols, box, coords, vectors, added=None, bases=()):
    own = added is None
    sums = bool(bases)
    operands = [place, active, cols, box, *coords, *vectors]
    operands += ([] if own else [added]) + list(bases)
    rows = 2 * B // TILE
    slots = 2 * rows * len(coords) + 1
    out_shape = [jax.ShapeDtypeStruct((16, 2 * B), jnp.float32)]
    if sums:
        out_shape.append(jax.ShapeDtypeStruct((16, TILE), jnp.float32))
    result = pl.pallas_call(
        partial(apply_kernel, own, sums),
        out_shape=out_shape,
        in_specs=[SMEM, SMEM] + [VMEM] * (len(operands) - 2),
        out_specs=[VMEM] * len(out_shape),
        scratch_shapes=[
            pltpu.VMEM((slots, 8, TILE), jnp.float32),
            pltpu.VMEM((slots, 8, TILE), jnp.float32),
            pltpu.VMEM((slots, 32, TILE), jnp.bfloat16),
            pltpu.VMEM((slots, 32, TILE), jnp.bfloat16),
            pltpu.VMEM((6, TILE, TILE), jnp.float32),
            pltpu.VMEM((2, TILE, 4 * TILE), jnp.bfloat16),
            pltpu.VMEM((2, 32, 4 * TILE), jnp.bfloat16),
            pltpu.VMEM((rows, 32, TILE), jnp.float32),
            pltpu.VMEM((rows, TILE), jnp.int32),
            pltpu.SMEM((rows, TILE), jnp.int32),
            pltpu.SemaphoreType.DMA,
        ],
        compiler_params=PARAMS,
        name="apply_own" if own else "apply_cross",
    )(*operands)
    return result if sums else result[0]


def shards(right_side, points, active):
    column = lax.axis_index("blk")
    member = lax.axis_index("rep")
    sides = right_side.shape[0] // lax.axis_size("rep")
    place = jnp.stack([column, member]).astype(jnp.int32)

    def neighbours(values):
        return from_behind(values, "blk", 1), from_behind(values, "blk", -1)

    rows, cols, rank, box = sort_points(place, points, right_side)
    around = neighbours(rows)
    fixed = (place, active, cols, box)
    part = apply_pairs(*fixed, (rows,), (rows,))
    w0 = apply_pairs(*fixed, around, around, part)
    w0_around = neighbours(w0)
    w0_all = lax.all_gather(unsort(w0, rank), "rep", axis=0, tiled=True)
    part = apply_pairs(*fixed, (rows,), (w0,))
    w1, sums = apply_pairs(*fixed, around, w0_around, part, (rows, w0))
    w1_all = lax.all_gather(unsort(w1, rank), "rep", axis=0, tiled=True)
    sums = sum_over_blk(sums[:, 0:4].T)
    s00, s01, s11, s12 = (sums[k] for k in range(4))
    image_norm = shift * s00 + s01
    alpha = s00 / image_norm
    keep = s01 / image_norm
    rr1 = alpha * alpha * (s11 - s01 * (s01 / s00))
    beta = rr1 / s00
    both = keep + beta
    curved = both * both * s01 - 2.0 * both * alpha * s11 + alpha * alpha * s12
    alpha1 = rr1 / (shift * rr1 * (1.0 + beta) + curved)
    factors = jnp.stack(
        [
            (s00 + s01) / image_norm - noise_level * alpha1 * both,
            noise_level * alpha1 * alpha,
            keep - shift * alpha1 * both,
            shift * alpha1 * alpha - alpha - alpha1 * both,
            alpha1 * alpha,
        ]
    )
    spread = jnp.zeros((5, 4, sides), jnp.float32)
    for mask in range(4):
        piece = factors if mask == 0 else exchange(factors, mask, "rep")
        spread = lax.dynamic_update_slice_in_dim(spread, piece[:, None], member ^ mask, 1)
    factor = spread.reshape(5, 4 * sides, 1)
    posterior = factor[0] * right_side + factor[1] * w0_all
    residual = factor[2] * right_side + factor[3] * w0_all + factor[4] * w1_all
    return (posterior, residual)


def solution(mesh):
    return jax.shard_map(
        shards,
        mesh=mesh,
        in_specs=(P(None, "blk"), P(None, "blk"), P()),
        out_specs=(P(None, "blk"), P(None, "blk")),
        check_vma=False,
    )
```

time: 189 us -> 146 us (0.77)
  Pallas kernels: 90.2 us -> 67.7 us
  local copies, waits for them, and re-layouts: 19.7 us -> 8.23 us
  other arithmetic: 11.7 us -> 3.83 us
    pallas_call x4, Pallas kernels: 77.3 us -> 54.8 us  [apply_pairs(): pl.pallas_call(partial(apply_kernel, own, sums), out_shape=out_shape, in_...]
    slice x9 -> x0, local copies, waits for them, and re-layouts: 4.27 us -> none  [the longest x1 1.08 us: shards(): w0 = apply_pairs(cross_lists, cols, around[16:24], around[0:16], part)]
    reduce_sum x5 -> x0, other arithmetic: 4.25 us -> none  [the longest x2 3.86 us: close_lists(): table = jnp.sum(jnp.where(match, source - columns, 0), axis=2) + columns]
    another operation x1 -> x0, local copies, waits for them, and re-layouts: 2.58 us -> none  [pair_flags(): jnp.stack([before[1], before[3], after[1], after[2], before[2], before[4]...]
    unnamed x37 -> x29, local copies, waits for them, and re-layouts: 8.18 us -> 7.25 us
  transfers between devices with their start and end apart: 18 -> 18, of which waited for: 9 -> 8; matrix products, arithmetic and copies ran while one was open for 7% -> 1% of each run, Pallas kernels for 38% -> 36%
where the time goes in v2:
time: 146 us; the launch traced here: 144 us
  Pallas kernels  67.7 us (46%)
  starting transfers between devices  34.6 us (24%)
  waiting for transfers between devices  14.9 us (10%)
  between operations  14.3 us (10%)
  local copies, waits for them, and re-layouts  8.23 us (6%)
  other arithmetic  3.83 us (3%)
    pallas_call x4, Pallas kernels, apply_pairs(): pl.pallas_call(partial(apply_kernel, own, sums), out_shape=out_shape, in_...  54.8 us
    ppermute x12, starting transfers between devices, exchange(): return lax.ppermute(values, axis, [(i, i ^ mask) for i in devices])  23 us
    ppermute x12, waiting for transfers between devices, exchange(): return lax.ppermute(values, axis, [(i, i ^ mask) for i in devices])  14.9 us
    ppermute x4, starting transfers between devices, from_behind(): return lax.ppermute(block, axis, route)  11.5 us
    unnamed x29, local copies, waits for them, and re-layouts  7.25 us
    pallas_call x1, Pallas kernels, sort_points(): pl.pallas_call(sort_kernel, out_shape=(jax.ShapeDtypeStruct((24, width),...  6.59 us
    pallas_call x2, Pallas kernels, unsort(): pl.pallas_call(unsort_kernel, out_shape=jax.ShapeDtypeStruct(values.shape...  6.29 us
    add x1, other arithmetic, shards(): residual = factor[2] * right_side + factor[3] * w0_all + factor[4] * w1_all  3.56 us
  transfers between devices with their start and end apart: 18, of which 8 were waited for; matrix products, arithmetic and copies ran while one was open for 1% of the time, Pallas kernels for 36%

profile of v2, /device:TPU:8, one launch (start us, length us, event | category | flops | bytes accessed | tf_op | source)
XLA Modules:
  0.0 143.5 jit_solution(9401666567798838846)
XLA Ops:
  7.3 1.2 copy-done
  8.5 0.8 copy-done.13
  9.4 6.6 %sort_points.1 = (f32[24,4096]{1,0:T(8,128)S(1)}, f32[4096,128]{1,0:T(8,128)S(1)}, s32[8,4096]{1,0:T(8,128)S(1)}, f32[2,32,128]{2,1,0:T(8,128)S(1)}) custom-call(s32[2]{0:T(128)S(1)} %pad_add_fusion.place_ref.refs_0_, f32[3,4096]{1,0:T(4,128)S(1)} %copy-done.13, f32[64,4096]{1,0:T(8,128)S(1)} %copy-done), custom_call_target="tpu_custom_call" | custom-call | tf_op jit(solution)/shard_map/sort_points/pallas_call | solution.py:155
  16.6 1.8 %collective-permute-start = (f32[24,4096]{1,0:T(8,128)S(1)}, f32[24,4096]{1,0:T(8,128)S(1)}, u32[]{:S(2)}, u32[]{:S(2)}) collective-permute-start(f32[24,4096]{1,0:T(8,128)S(1)} %get-tuple-element.10.refs_4_.refs_5_.refs_9_), channel_id=1, source_target_pairs={{0,4},{4,8},{8,12},{12,16},{16,20},{20,24},{24,28},{28,32},{32,36}... | collective-permute-start | bytes 1179656 | tf_op jit(solution)/shard_map/ppermute | solution.py:32
  18.4 1.3 collective-permute-start.1
  19.7 0.8 copy.20.refs_1_
  20.5 20.7 %apply_own.2.refs_8_ = f32[16,4096]{1,0:T(8,128)S(1)} custom-call(s32[2]{0:T(128)S(1)} %pad_add_fusion.place_ref.refs_0_, s32[64,5]{1,0:T(8,128)S(1)} %copy.20.refs_1_, f32[4096,128]{1,0:T(8,128)S(1)} %get-tuple-element.8.refs_2_, f32[2,32,128]{2,1,0:T(8,128)S(1)} %get-tuple-element.9.refs_3_, f32[24,4096]{1,0:T(8,128)S(1)} %get-tuple-element.10.refs_4_.refs_5_.refs_9_, ...), custom_call_target="tpu_custom_call" | custom-call | tf_op jit(solution)/shard_map/apply_own/pallas_call | solution.py:437
  42.0 0.8 copy-done.7
  42.8 6.6 %apply_cross.2.refs_5_.refs_10_.sorted_ref = f32[16,4096]{1,0:T(8,128)S(1)} custom-call(s32[2]{0:T(128)S(1)} %pad_add_fusion.place_ref.refs_0_, s32[64,5]{1,0:T(8,128)S(1)} %copy-done.3, f32[4096,128]{1,0:T(8,128)S(1)} %get-tuple-element.8.refs_2_, f32[2,32,128]{2,1,0:T(8,128)S(1)} %copy-done.7, f32[24,4096]{1,0:T(8,128)S(1)} %collective-permute-done.refs_4_.refs_6_, ...), custom_call_target="tpu_custom_call" | custom-call | tf_op jit(solution)/shard_map/apply_cross/pallas_call | solution.py:437
  49.4 2.8 %unsort.2 = f32[16,4096]{1,0:T(8,128)S(1)} custom-call(f32[16,4096]{1,0:T(8,128)S(1)} %apply_cross.2.refs_5_.refs_10_.sorted_ref, s32[8,4096]{1,0:T(8,128)S(1)} %copy-done.11), custom_call_target="tpu_custom_call" | custom-call | tf_op jit(solution)/shard_map/unsort/pallas_call | solution.py:194
  52.9 7.0 %collective-permute-start.2 = (f32[16,4096]{1,0:T(8,128)S(1)}, f32[16,4096]{1,0:T(8,128)}, u32[]{:S(2)}, u32[]{:S(2)}) collective-permute-start(f32[16,4096]{1,0:T(8,128)S(1)} %apply_cross.2.refs_5_.refs_10_.sorted_ref), channel_id=1, source_target_pairs={{0,4},{4,8},{8,12},{12,16},{16,20},{20,24},{24,28},{28,32},{32,36}... | collective-permute-start | bytes 786440 | tf_op jit(solution)/shard_map/ppermute | solution.py:32
  59.9 1.5 %collective-permute-start.3 = (f32[16,4096]{1,0:T(8,128)S(1)}, f32[16,4096]{1,0:T(8,128)}, u32[]{:S(2)}, u32[]{:S(2)}) collective-permute-start(f32[16,4096]{1,0:T(8,128)S(1)} %apply_cross.2.refs_5_.refs_10_.sorted_ref), channel_id=1, source_target_pairs={{4,0},{8,4},{12,8},{16,12},{20,16},{24,20},{28,24},{32,28},{36,32}... | collective-permute-start | bytes 786440 | tf_op jit(solution)/shard_map/ppermute | solution.py:32
  62.1 0.8 copy-done.8
  62.9 20.7 %apply_own.3.refs_8_ = f32[16,4096]{1,0:T(8,128)S(1)} custom-call(s32[2]{0:T(128)S(1)} %pad_add_fusion.place_ref.refs_0_, s32[64,5]{1,0:T(8,128)S(1)} %copy-done.4, f32[4096,128]{1,0:T(8,128)S(1)} %get-tuple-element.8.refs_2_, f32[2,32,128]{2,1,0:T(8,128)S(1)} %copy-done.8, f32[24,4096]{1,0:T(8,128)S(1)} %get-tuple-element.10.refs_4_.refs_5_.refs_9_, ...), custom_call_target="tpu_custom_call" | custom-call | tf_op jit(solution)/shard_map/apply_own/pallas_call | solution.py:437
  83.7 6.8 %apply_cross.3 = (f32[16,4096]{1,0:T(8,128)S(1)}, f32[16,128]{1,0:T(8,128)S(1)}) custom-call(s32[2]{0:T(128)S(1)} %pad_add_fusion.place_ref.refs_0_, s32[64,5]{1,0:T(8,128)S(1)} %copy-done.5, f32[4096,128]{1,0:T(8,128)S(1)} %get-tuple-element.8.refs_2_, f32[2,32,128]{2,1,0:T(8,128)S(1)} %copy-done.9, f32[24,4096]{1,0:T(8,128)S(1)} %collective-permute-done.refs_4_.refs_6_, ...), custom_call_target="tpu_custom_call" | custom-call | tf_op jit(solution)/shard_map/apply_cross/pallas_call | solution.py:437
  90.5 3.5 %unsort.3 = f32[16,4096]{1,0:T(8,128)} custom-call(f32[16,4096]{1,0:T(8,128)S(1)} %get-tuple-element.13.sorted_ref, s32[8,4096]{1,0:T(8,128)S(1)} %copy-done.12), custom_call_target="tpu_custom_call" | custom-call | tf_op jit(solution)/shard_map/unsort/pallas_call | solution.py:194
  94.0 3.3 %collective-permute-start.4 = (f32[4,16]{0,1:T(8,128)S(1)}, f32[4,16]{0,1:T(8,128)S(1)}, u32[]{:S(2)}, u32[]{:S(2)}) collective-permute-start(f32[4,16]{0,1:T(8,128)S(1)} %slice_bitcast_fusion), channel_id=1, source_target_pairs={{0,4},{4,0},{8,12},{12,8},{16,20},{20,16},{24,28},{28,24},{32,36},... | collective-permute-start | bytes 776 | tf_op jit(solution)/shard_map/ppermute | solution.py:37
  97.4 1.7 %collective-permute-start.5 = (f32[4,16]{0,1:T(8,128)S(1)}, f32[4,16]{0,1:T(8,128)S(1)}, u32[]{:S(2)}, u32[]{:S(2)}) collective-permute-start(f32[4,16]{0,1:T(8,128)S(1)} %slice_bitcast_fusion), channel_id=1, source_target_pairs={{0,8},{4,12},{8,0},{12,4},{16,24},{20,28},{24,16},{28,20},{32,40},... | collective-permute-start | bytes 776 | tf_op jit(solution)/shard_map/ppermute | solution.py:37
  99.1 1.9 %collective-permute-done.5 = f32[4,16]{0,1:T(8,128)S(1)} collective-permute-done((f32[4,16]{0,1:T(8,128)S(1)}, f32[4,16]{0,1:T(8,128)S(1)}, u32[]{:S(2)}, u32[]{:S(2)}) %collective-permute-start.5) | collective-permute-done | bytes 288 | tf_op jit(solution)/shard_map/ppermute | solution.py:37
  101.0 1.2 collective-permute-done.6
  102.2 6.0 %collective-permute-start.7 = (f32[4,16]{0,1:T(8,128)S(1)}, f32[4,16]{0,1:T(8,128)S(1)}, u32[]{:S(2)}, u32[]{:S(2)}) collective-permute-start(f32[4,16]{0,1:T(8,128)S(1)} %add_add_fusion.2), channel_id=1, source_target_pairs={{0,16},{4,20},{8,24},{12,28},{16,0},{20,4},{24,8},{28,12},{32,48},... | collective-permute-start | bytes 776 | tf_op jit(solution)/shard_map/ppermute | solution.py:37
  108.1 2.5 %collective-permute-start.8 = (f32[4,16]{0,1:T(8,128)S(1)}, f32[4,16]{0,1:T(8,128)S(1)}, u32[]{:S(2)}, u32[]{:S(2)}) collective-permute-start(f32[4,16]{0,1:T(8,128)S(1)} %add_add_fusion.2), channel_id=1, source_target_pairs={{0,32},{4,36},{8,40},{12,44},{16,48},{20,52},{24,56},{28,60},{32,0... | collective-permute-start | bytes 776 | tf_op jit(solution)/shard_map/ppermute | solution.py:37
  110.6 1.2 collective-permute-start.9
  111.8 3.9 %collective-permute-done.8 = f32[4,16]{0,1:T(8,128)S(1)} collective-permute-done((f32[4,16]{0,1:T(8,128)S(1)}, f32[4,16]{0,1:T(8,128)S(1)}, u32[]{:S(2)}, u32[]{:S(2)}) %collective-permute-start.8) | collective-permute-done | bytes 288 | tf_op jit(solution)/shard_map/ppermute | solution.py:37
  116.4 1.5 %collective-permute-start.10 = (f32[4,16]{0,1:T(8,128)S(1)}, f32[4,16]{0,1:T(8,128)S(1)}, u32[]{:S(2)}, u32[]{:S(2)}) collective-permute-start(f32[4,16]{0,1:T(8,128)S(1)} %add_add_fusion.1), channel_id=1, source_target_pairs={{0,64},{4,68},{8,72},{12,76},{16,80},{20,84},{24,88},{28,92},{32,9... | collective-permute-start | bytes 776 | tf_op jit(solution)/shard_map/ppermute | solution.py:37
  117.9 2.7 %collective-permute-start.11 = (f32[4,16]{0,1:T(8,128)S(1)}, f32[4,16]{0,1:T(8,128)S(1)}, u32[]{:S(2)}, u32[]{:S(2)}) collective-permute-start(f32[4,16]{0,1:T(8,128)S(1)} %add_add_fusion.1), channel_id=1, source_target_pairs={{0,128},{4,132},{8,136},{12,140},{16,144},{20,148},{24,152},{28,15... | collective-permute-start | bytes 776 | tf_op jit(solution)/shard_map/ppermute | solution.py:37
  121.1 1.9 %collective-permute-done.11 = f32[4,16]{0,1:T(8,128)S(1)} collective-permute-done((f32[4,16]{0,1:T(8,128)S(1)}, f32[4,16]{0,1:T(8,128)S(1)}, u32[]{:S(2)}, u32[]{:S(2)}) %collective-permute-start.11) | collective-permute-done | bytes 288 | tf_op jit(solution)/shard_map/ppermute | solution.py:37
  123.1 2.4 %collective-permute-done.12 = f32[4,16]{0,1:T(8,128)S(1)} collective-permute-done((f32[4,16]{0,1:T(8,128)S(1)}, f32[4,16]{0,1:T(8,128)S(1)}, u32[]{:S(2)}, u32[]{:S(2)}) %collective-permute-start.12) | collective-permute-done | bytes 288 | tf_op jit(solution)/shard_map/ppermute | solution.py:37
  126.3 2.6 %collective-permute-start.14 = (f32[5,16]{0,1:T(8,128)S(1)}, f32[5,16]{0,1:T(8,128)S(1)}, u32[]{:S(2)}, u32[]{:S(2)}) collective-permute-start(f32[5,16]{0,1:T(8,128)S(1)} %stack.20), channel_id=1, source_target_pairs={{0,2},{1,3},{2,0},{3,1},{4,6},{5,7},{6,4},{7,5},{8,10},{9,11},{10,... | collective-permute-start | bytes 968 | tf_op jit(solution)/shard_map/ppermute | solution.py:37
  129.5 1.9 %collective-permute-done.14 = f32[5,16]{0,1:T(8,128)S(1)} collective-permute-done((f32[5,16]{0,1:T(8,128)S(1)}, f32[5,16]{0,1:T(8,128)S(1)}, u32[]{:S(2)}, u32[]{:S(2)}) %collective-permute-start.14) | collective-permute-done | bytes 352 | tf_op jit(solution)/shard_map/ppermute | solution.py:37
  131.5 1.0 collective-permute-done.15
  133.1 3.6 %multiply_add_fusion = (f32[64,4096]{1,0:T(8,128)}, f32[64,4096]{1,0:T(8,128)}) fusion(f32[64,4096]{1,0:T(8,128)} %all-gather.5.cloned.1.call-done, f32[64,4096]{1,0:T(8,128)} %all-gather.3.cloned.1.call-done, f32[64,4096]{1,0:T(8,128)} %sides_ref.1, f32[64]{0:T(128)S(1)} %mul.215, f32[64]{0:T(128)S(1)} %mul.212, f32[64]{0:T(128)S(1)} %mul.209, ...), kind=kLoop, calls=%fused_computation | loop fusion | flops 2097152 | bytes 5244160 | tf_op jit(solution)/shard_map/add | solution.py:505
  (66 shorter events, 6.6 us)
Async XLA Ops:
  7.2 126.0 %all-gather.3.cloned.1.call-start = ((), (), s32[]{:S(2)}) async-start(), calls=%async_computation | async-start | bytes 1310720 | tf_op jit(solution)/shard_map/all_gather | solution.py:476
  7.3 1.2 copy-start
  8.5 0.8 copy-start.13
  16.0 0.7 copy-start.10
  16.6 24.6 %copy-start.6 = (f32[2,32,128]{2,1,0:T(8,128)}, f32[2,32,128]{2,1,0:T(8,128)S(1)}, u32[]{:S(2)}) copy-start(f32[2,32,128]{2,1,0:T(8,128)S(1)} %get-tuple-element.9.refs_3_) | copy-start | bytes 98308
  16.6 24.6 %collective-permute-start = (f32[24,4096]{1,0:T(8,128)S(1)}, f32[24,4096]{1,0:T(8,128)S(1)}, u32[]{:S(2)}, u32[]{:S(2)}) collective-permute-start(f32[24,4096]{1,0:T(8,128)S(1)} %get-tuple-element.10.refs_4_.refs_5_.refs_9_), channel_id=1, source_target_pairs={{0,4},{4,8},{8,12},{12,16},{16,20},{20,24},{24,28},{28,32},{32,36}... | collective-permute-start | bytes 1179656 | tf_op jit(solution)/shard_map/ppermute | solution.py:32
  18.4 22.9 %collective-permute-start.1 = (f32[24,4096]{1,0:T(8,128)S(1)}, f32[24,4096]{1,0:T(8,128)S(1)}, u32[]{:S(2)}, u32[]{:S(2)}) collective-permute-start(f32[24,4096]{1,0:T(8,128)S(1)} %get-tuple-element.10.refs_4_.refs_5_.refs_9_), channel_id=1, source_target_pairs={{4,0},{8,4},{12,8},{16,12},{20,16},{24,20},{28,24},{32,28},{36,32}... | collective-permute-start | bytes 1179656 | tf_op jit(solution)/shard_map/ppermute | solution.py:32
  20.5 20.8 %copy-start.2 = (s32[64,5]{1,0:T(8,128)}, s32[64,5]{1,0:T(8,128)S(1)}, u32[]{:S(2)}) copy-start(s32[64,5]{1,0:T(8,128)S(1)} %copy.20.refs_1_) | copy-start | bytes 3844
  20.5 28.9 %copy-start.11 = (s32[8,4096]{1,0:T(8,128)S(1)}, s32[8,4096]{1,0:T(8,128)}, u32[]{:S(2)}) copy-start(s32[8,4096]{1,0:T(8,128)} %copy-done.10) | copy-start | bytes 393220
  41.3 0.8 copy-start.3
  42.0 0.8 copy-start.7
  52.1 0.7 copy-start.1
  52.9 80.2 %all-gather.5.cloned.1.call-start = ((), (), s32[]{:S(2)}) async-start(), calls=%async_computation.1 | async-start | bytes 1310720 | tf_op jit(solution)/shard_map/all_gather | solution.py:479
  52.9 30.7 %collective-permute-start.2 = (f32[16,4096]{1,0:T(8,128)S(1)}, f32[16,4096]{1,0:T(8,128)}, u32[]{:S(2)}, u32[]{:S(2)}) collective-permute-start(f32[16,4096]{1,0:T(8,128)S(1)} %apply_cross.2.refs_5_.refs_10_.sorted_ref), channel_id=1, source_target_pairs={{0,4},{4,8},{8,12},{12,16},{16,20},{20,24},{24,28},{28,32},{32,36}... | collective-permute-start | bytes 786440 | tf_op jit(solution)/shard_map/ppermute | solution.py:32
  59.9 23.8 %collective-permute-start.3 = (f32[16,4096]{1,0:T(8,128)S(1)}, f32[16,4096]{1,0:T(8,128)}, u32[]{:S(2)}, u32[]{:S(2)}) collective-permute-start(f32[16,4096]{1,0:T(8,128)S(1)} %apply_cross.2.refs_5_.refs_10_.sorted_ref), channel_id=1, source_target_pairs={{4,0},{8,4},{12,8},{16,12},{20,16},{24,20},{28,24},{32,28},{36,32}... | collective-permute-start | bytes 786440 | tf_op jit(solution)/shard_map/ppermute | solution.py:32
  61.4 0.8 copy-start.4
  62.1 0.8 copy-start.8
  62.9 20.8 %copy-start.5 = (s32[64,5]{1,0:T(8,128)S(1)}, s32[64,5]{1,0:T(8,128)}, u32[]{:S(2)}) copy-start(s32[64,5]{1,0:T(8,128)} %copy-done.2) | copy-start | bytes 3844
  62.9 20.8 %copy-start.9 = (f32[2,32,128]{2,1,0:T(8,128)S(1)}, f32[2,32,128]{2,1,0:T(8,128)}, u32[]{:S(2)}) copy-start(f32[2,32,128]{2,1,0:T(8,128)} %copy-done.6) | copy-start | bytes 98308
  83.6 6.8 %copy-start.12 = (s32[8,4096]{1,0:T(8,128)S(1)}, s32[8,4096]{1,0:T(8,128)}, u32[]{:S(2)}) copy-start(s32[8,4096]{1,0:T(8,128)} %copy-done.10) | copy-start | bytes 393220
  94.0 5.1 %collective-permute-start.4 = (f32[4,16]{0,1:T(8,128)S(1)}, f32[4,16]{0,1:T(8,128)S(1)}, u32[]{:S(2)}, u32[]{:S(2)}) collective-permute-start(f32[4,16]{0,1:T(8,128)S(1)} %slice_bitcast_fusion), channel_id=1, source_target_pairs={{0,4},{4,0},{8,12},{12,8},{16,20},{20,16},{24,28},{28,24},{32,36},... | collective-permute-start | bytes 776 | tf_op jit(solution)/shard_map/ppermute | solution.py:37
  97.4 3.7 %collective-permute-start.5 = (f32[4,16]{0,1:T(8,128)S(1)}, f32[4,16]{0,1:T(8,128)S(1)}, u32[]{:S(2)}, u32[]{:S(2)}) collective-permute-start(f32[4,16]{0,1:T(8,128)S(1)} %slice_bitcast_fusion), channel_id=1, source_target_pairs={{0,8},{4,12},{8,0},{12,4},{16,24},{20,28},{24,16},{28,20},{32,40},... | collective-permute-start | bytes 776 | tf_op jit(solution)/shard_map/ppermute | solution.py:37
  99.1 3.1 %collective-permute-start.6 = (f32[4,16]{0,1:T(8,128)S(1)}, f32[4,16]{0,1:T(8,128)S(1)}, u32[]{:S(2)}, u32[]{:S(2)}) collective-permute-start(f32[4,16]{0,1:T(8,128)S(1)} %slice_bitcast_fusion), channel_id=1, source_target_pairs={{0,12},{4,8},{8,4},{12,0},{16,28},{20,24},{24,20},{28,16},{32,44},... | collective-permute-start | bytes 776 | tf_op jit(solution)/shard_map/ppermute | solution.py:37
  102.2 9.6 %collective-permute-start.7 = (f32[4,16]{0,1:T(8,128)S(1)}, f32[4,16]{0,1:T(8,128)S(1)}, u32[]{:S(2)}, u32[]{:S(2)}) collective-permute-start(f32[4,16]{0,1:T(8,128)S(1)} %add_add_fusion.2), channel_id=1, source_target_pairs={{0,16},{4,20},{8,24},{12,28},{16,0},{20,4},{24,8},{28,12},{32,48},... | collective-permute-start | bytes 776 | tf_op jit(solution)/shard_map/ppermute | solution.py:37
  108.1 7.6 %collective-permute-start.8 = (f32[4,16]{0,1:T(8,128)S(1)}, f32[4,16]{0,1:T(8,128)S(1)}, u32[]{:S(2)}, u32[]{:S(2)}) collective-permute-start(f32[4,16]{0,1:T(8,128)S(1)} %add_add_fusion.2), channel_id=1, source_target_pairs={{0,32},{4,36},{8,40},{12,44},{16,48},{20,52},{24,56},{28,60},{32,0... | collective-permute-start | bytes 776 | tf_op jit(solution)/shard_map/ppermute | solution.py:37
  110.6 5.8 %collective-permute-start.9 = (f32[4,16]{0,1:T(8,128)S(1)}, f32[4,16]{0,1:T(8,128)S(1)}, u32[]{:S(2)}, u32[]{:S(2)}) collective-permute-start(f32[4,16]{0,1:T(8,128)S(1)} %add_add_fusion.2), channel_id=1, source_target_pairs={{0,48},{4,52},{8,56},{12,60},{16,32},{20,36},{24,40},{28,44},{32,1... | collective-permute-start | bytes 776 | tf_op jit(solution)/shard_map/ppermute | solution.py:37
  116.4 4.7 %collective-permute-start.10 = (f32[4,16]{0,1:T(8,128)S(1)}, f32[4,16]{0,1:T(8,128)S(1)}, u32[]{:S(2)}, u32[]{:S(2)}) collective-permute-start(f32[4,16]{0,1:T(8,128)S(1)} %add_add_fusion.1), channel_id=1, source_target_pairs={{0,64},{4,68},{8,72},{12,76},{16,80},{20,84},{24,88},{28,92},{32,9... | collective-permute-start | bytes 776 | tf_op jit(solution)/shard_map/ppermute | solution.py:37
  117.9 5.2 %collective-permute-start.11 = (f32[4,16]{0,1:T(8,128)S(1)}, f32[4,16]{0,1:T(8,128)S(1)}, u32[]{:S(2)}, u32[]{:S(2)}) collective-permute-start(f32[4,16]{0,1:T(8,128)S(1)} %add_add_fusion.1), channel_id=1, source_target_pairs={{0,128},{4,132},{8,136},{12,140},{16,144},{20,148},{24,152},{28,15... | collective-permute-start | bytes 776 | tf_op jit(solution)/shard_map/ppermute | solution.py:37
  120.6 4.9 %collective-permute-start.12 = (f32[4,16]{0,1:T(8,128)S(1)}, f32[4,16]{0,1:T(8,128)S(1)}, u32[]{:S(2)}, u32[]{:S(2)}) collective-permute-start(f32[4,16]{0,1:T(8,128)S(1)} %add_add_fusion.1), channel_id=1, source_target_pairs={{0,192},{4,196},{8,200},{12,204},{16,208},{20,212},{24,216},{28,22... | collective-permute-start | bytes 776 | tf_op jit(solution)/shard_map/ppermute | solution.py:37
  125.7 3.7 %collective-permute-start.13 = (f32[5,16]{0,1:T(8,128)S(1)}, f32[5,16]{0,1:T(8,128)S(1)}, u32[]{:S(2)}, u32[]{:S(2)}) collective-permute-start(f32[5,16]{0,1:T(8,128)S(1)} %stack.20), channel_id=1, source_target_pairs={{0,1},{1,0},{2,3},{3,2},{4,5},{5,4},{6,7},{7,6},{8,9},{9,8},{10,11... | collective-permute-start | bytes 968 | tf_op jit(solution)/shard_map/ppermute | solution.py:37
  126.3 5.2 %collective-permute-start.14 = (f32[5,16]{0,1:T(8,128)S(1)}, f32[5,16]{0,1:T(8,128)S(1)}, u32[]{:S(2)}, u32[]{:S(2)}) collective-permute-start(f32[5,16]{0,1:T(8,128)S(1)} %stack.20), channel_id=1, source_target_pairs={{0,2},{1,3},{2,0},{3,1},{4,6},{5,7},{6,4},{7,5},{8,10},{9,11},{10,... | collective-permute-start | bytes 968 | tf_op jit(solution)/shard_map/ppermute | solution.py:37
  128.8 3.7 %collective-permute-start.15 = (f32[5,16]{0,1:T(8,128)S(1)}, f32[5,16]{0,1:T(8,128)S(1)}, u32[]{:S(2)}, u32[]{:S(2)}) collective-permute-start(f32[5,16]{0,1:T(8,128)S(1)} %stack.20), channel_id=1, source_target_pairs={{0,3},{1,2},{2,1},{3,0},{4,7},{5,6},{6,5},{7,4},{8,11},{9,10},{10,... | collective-permute-start | bytes 968 | tf_op jit(solution)/shard_map/ppermute | solution.py:37
Sparse Core Ops, SparseCore 0:
  53.0 33.3 all-gather.2
  94.1 33.5 all-gather.4

commit v3 on v2

--- a/solution.py
+++ b/solution.py
@@ -12,6 +12,8 @@
 TILE = 128
 STRIP = 256
 BATCH = 4
+GROUP = 4
+KEPT = {True: 32, False: 8}
 CELLS_X = 4
 CELLS_Y = 8
 CELLS = CELLS_X * CELLS_Y
@@ -30,19 +32,6 @@
     devices = range(lax.axis_size(axis))
     route = [(i - distance, i) for i in devices if i - distance in devices]
     return lax.ppermute(block, axis, route)
-
-
-def exchange(values, mask, axis):
-    devices = range(lax.axis_size(axis))
-    return lax.ppermute(values, axis, [(i, i ^ mask) for i in devices])
-
-
-def sum_over_blk(values):
-    for base in (1, 4, 16):
-        near = values + exchange(values, base, "blk")
-        far = exchange(values, 2 * base, "blk") + exchange(values, 3 * base, "blk")
-        values = near + far
-    return values
 
 
 def split3(values):
@@ -264,7 +253,7 @@
     return value + 256 * place[:, TILE - 1 :]
 
 
-def apply_kernel(own, sums, *refs):
+def apply_kernel(own, again, *refs):
     refs = list(refs)
     place_ref, active_ref, cols_ref, box_ref = refs[:4]
     del refs[:4]
@@ -272,12 +261,18 @@
     xyz_refs = [refs.pop(0) for _ in range(sources)]
     vec_refs = [refs.pop(0) for _ in range(sources)]
     add_ref = None if own else refs.pop(0)
+    sums = again and not own
     base_refs = [refs.pop(0) for _ in range(2)] if sums else None
+    kept_ref = refs.pop(0) if again else None
     out_ref = refs.pop(0)
+    if not again:
+        kept_ref = refs.pop(0)
     sums_ref = refs.pop(0) if sums else None
-    left_xyz, right_xyz, left_w, right_w, target, tiles, weights, total_ref = refs[:8]
-    table_ref, list_ref, arrived = refs[8:]
+    left_xyz, right_xyz, left_w, right_w, target, bank, weights, total_ref = refs[:8]
+    table_ref, list_ref, arrived, moved = refs[8:]
     rows = out_ref.shape[1] // TILE
+    cells = rows // GROUP
+    kept = KEPT[own]
     null = 2 * rows * sources
     lane = lax.broadcasted_iota(jnp.int32, (8, TILE), 1)
     is_left = lane < SUB
@@ -327,69 +322,129 @@
     left_w[null] = jnp.zeros((32, TILE), jnp.bfloat16)
     right_w[null] = jnp.zeros((32, TILE), jnp.bfloat16)
     total_ref[...] = jnp.zeros_like(total_ref)
-    tiles[1] = jnp.zeros((TILE, 4 * TILE), jnp.bfloat16)
-    weights[1] = jnp.zeros((32, 4 * TILE), jnp.bfloat16)
-
-    def form(side, j, n):
+    bank[kept] = jnp.zeros(bank.shape[1:], jnp.bfloat16)
+    weights[...] = jnp.zeros_like(weights)
+
+    def members(cell):
+        mirror = cell + 3 * cells // 2 - cells * (cell // (cells // 2))
+        return cell, mirror, rows - 1 - mirror, rows - 1 - cell
+
+    def batches(cell):
+        count = list_ref[cell, 0]
+        for j in members(cell)[1:]:
+            count = jnp.maximum(count, list_ref[j, 0])
+        return (count // 256 + BATCH - 1) // BATCH
+
+    def aim(cell):
+        for k, j in enumerate(members(cell)):
+            spot = pl.ds(pl.multiple_of(j * TILE, TILE), TILE)
+            for axis in range(3):
+                target[3 * k + axis] = jnp.broadcast_to(
+                    cols_ref[spot, 16 + axis : 17 + axis], (TILE, TILE)
+                )
+
+    def chunks(j, n, s):
+        return list_ref[j, 4 * n + 2 * s] & 255, list_ref[j, 4 * n + 2 * s + 1] & 255
+
+    def weigh(k, j, n):
         for s in range(2):
-            first = list_ref[j, 4 * n + 2 * s] & 255
-            second = list_ref[j, 4 * n + 2 * s + 1] & 255
+            first, second = chunks(j, n, s)
+            weights[k, :, s * TILE : (s + 1) * TILE] = left_w[first] + right_w[second]
+
+    def form(slot, k, j, n):
+        for s in range(2):
+            first, second = chunks(j, n, s)
             xyz = left_xyz[first] + right_xyz[second]
-            weight = left_w[first] + right_w[second]
-            near = slice(2 * s * TILE, (2 * s + 1) * TILE)
-            far = slice((2 * s + 1) * TILE, (2 * s + 2) * TILE)
-            weights[side, :, near] = weight
-            weights[side, :, far] = weight
+            here = slice(s * TILE, (s + 1) * TILE)
             for r in range(TILE // 16):
                 span = slice(16 * r, 16 * r + 16)
-                dx = target[3 * side, span, :] - xyz[0:1, :]
-                dy = target[3 * side + 1, span, :] - xyz[1:2, :]
-                dz = target[3 * side + 2, span, :] - xyz[2:3, :]
+                dx = target[3 * k, span, :] - xyz[0:1, :]
+                dy = target[3 * k + 1, span, :] - xyz[1:2, :]
+                dz = target[3 * k + 2, span, :] - xyz[2:3, :]
                 square = jnp.maximum(dx * dx + dy * dy + dz * dz, 1e-30)
                 distance = square * lax.rsqrt(square)
                 inside = jnp.maximum(support_radius - distance, 0.0)
                 inside = inside * inside
                 value = (inside * inside) * (distance + 0.25 * support_radius)
                 high = value.astype(jnp.bfloat16)
-                tiles[side, span, near] = high
-                tiles[side, span, far] = (value - high.astype(jnp.float32)).astype(jnp.bfloat16)
-
-    def apply(side):
-        return lax.dot_general(
-            weights[side],
-            tiles[side],
+                low = (value - high.astype(jnp.float32)).astype(jnp.bfloat16)
+                bank[slot, k, 16 * r : 16 * r + 16, here] = high
+                bank[slot, k, TILE + 16 * r : TILE + 16 * r + 16, here] = low
+
+    def apply(slot, k):
+        both = lax.dot_general(
+            weights[k],
+            bank[slot, k],
             (((1,), (1,)), ((), ())),
             preferred_element_type=jnp.float32,
         )
+        return both[:, 0:TILE] + both[:, TILE : 2 * TILE]
+
+    def add(cell, images):
+        for j, image in zip(members(cell), images):
+            total_ref[j] += image
+
+    def transfer(g):
+        ends = (kept_ref.at[g], bank.at[g]) if again else (bank.at[g], kept_ref.at[g])
+        return pltpu.make_async_copy(*ends, moved.at[g])
 
     load.wait()
-
-    def row_pair(j, last):
-        other = rows - 1 - j
-        count = jnp.maximum(list_ref[j, 0], list_ref[other, 0]) // 256
-
-        @pl.when(count > 0)
-        def _():
-            for side, k in enumerate((j, other)):
-                spot = pl.ds(pl.multiple_of(k * TILE, TILE), TILE)
-                for axis in range(3):
-                    target[3 * side + axis] = jnp.broadcast_to(
-                        cols_ref[spot, 16 + axis : 17 + axis], (TILE, TILE)
-                    )
-
-        def step(n, last):
-            image = apply(1)
-            form(0, j, n)
-            total_ref[last] += image
-            image = apply(0)
-            form(1, other, n)
-            total_ref[j] += image
-            return other
-
-        return lax.fori_loop(0, (count + BATCH - 1) // BATCH, step, last)
-
-    last = lax.fori_loop(0, rows // 2, row_pair, 0)
-    total_ref[last] += apply(1)
+    used = lax.fori_loop(0, cells, lambda cell, n: n + batches(cell), 0)
+    used = jnp.minimum(used, kept)
+
+    if again:
+        lax.fori_loop(0, used, lambda g, carry: (transfer(g).start(), carry)[1], 0)
+
+        def row_group(cell, g):
+            def step(n, g):
+                slot = jnp.minimum(g, kept)
+
+                @pl.when(g < kept)
+                def _():
+                    transfer(g).wait()
+
+                @pl.when(g >= kept)
+                def _():
+                    aim(cell)
+                    for k, j in enumerate(members(cell)):
+                        form(slot, k, j, n)
+
+                for k, j in enumerate(members(cell)):
+                    weigh(k, j, n)
+                add(cell, [apply(slot, k) for k in range(GROUP)])
+                return g + 1
+
+            return lax.fori_loop(0, batches(cell), step, g)
+
+        lax.fori_loop(0, cells, row_group, 0)
+    else:
+
+        def row_group(cell, state):
+            count = batches(cell)
+
+            @pl.when(count > 0)
+            def _():
+                aim(cell)
+
+            def step(n, state):
+                g, last_slot, last_cell = state
+                slot = jnp.minimum(g, kept)
+                images = [apply(last_slot, k) for k in range(GROUP)]
+                for k, j in enumerate(members(cell)):
+                    weigh(k, j, n)
+                    form(slot, k, j, n)
+                add(last_cell, images)
+
+                @pl.when(g < kept)
+                def _():
+                    transfer(g).start()
+
+                return g + 1, slot, cell
+
+            return lax.fori_loop(0, count, step, state)
+
+        _, slot, cell = lax.fori_loop(0, cells, row_group, (0, kept, 0))
+        add(cell, [apply(slot, k) for k in range(GROUP)])
 
     def finish(g, running):
         for u in range(4):
@@ -416,46 +471,62 @@
 
     zero = jnp.zeros((16, TILE), jnp.float32)
     result = lax.fori_loop(0, rows // 4, finish, (zero,) * 4 if sums else 0)
+    if not again:
+        lax.fori_loop(0, used, lambda g, carry: (transfer(g).wait(), carry)[1], 0)
     if sums:
         columns = lax.broadcasted_iota(jnp.int32, (16, TILE), 1)
         packed = zero
         for k in range(4):
             packed = jnp.where(columns == k, jnp.sum(result[k], axis=1, keepdims=True), packed)
-        sums_ref[...] = packed
-
-
-def apply_pairs(place, active, cols, box, coords, vectors, added=None, bases=()):
+        turned = jnp.concatenate([packed] + [zero] * 7, axis=0).T
+        line = turned[0:1]
+        for k in range(1, 4):
+            line = line + pltpu.roll(turned[k : k + 1], 16 * k, 1)
+        sums_ref[...] = jnp.broadcast_to(line, sums_ref.shape)
+
+
+def apply_pairs(fixed, coords, vectors, added=None, bases=(), kept=None):
     own = added is None
-    sums = bool(bases)
-    operands = [place, active, cols, box, *coords, *vectors]
+    again = kept is not None
+    operands = [*fixed, *coords, *vectors]
     operands += ([] if own else [added]) + list(bases)
+    specs = [SMEM, SMEM] + [VMEM] * (len(operands) - 2)
     rows = 2 * B // TILE
     slots = 2 * rows * len(coords) + 1
     out_shape = [jax.ShapeDtypeStruct((16, 2 * B), jnp.float32)]
-    if sums:
-        out_shape.append(jax.ShapeDtypeStruct((16, TILE), jnp.float32))
-    result = pl.pallas_call(
-        partial(apply_kernel, own, sums),
+    out_specs = [VMEM]
+    bank = (GROUP, 2 * TILE, 2 * TILE)
+    if again:
+        operands.append(kept)
+        specs.append(pl.BlockSpec(memory_space=pl.ANY))
+    else:
+        out_shape.append(jax.ShapeDtypeStruct((KEPT[own],) + bank, jnp.bfloat16))
+        out_specs.append(pl.BlockSpec(memory_space=pl.ANY))
+    if bases:
+        out_shape.append(jax.ShapeDtypeStruct((256, TILE), jnp.float32))
+        out_specs.append(VMEM)
+    return pl.pallas_call(
+        partial(apply_kernel, own, again),
         out_shape=out_shape,
-        in_specs=[SMEM, SMEM] + [VMEM] * (len(operands) - 2),
-        out_specs=[VMEM] * len(out_shape),
+        in_specs=specs,
+        out_specs=out_specs,
         scratch_shapes=[
             pltpu.VMEM((slots, 8, TILE), jnp.float32),
             pltpu.VMEM((slots, 8, TILE), jnp.float32),
             pltpu.VMEM((slots, 32, TILE), jnp.bfloat16),
             pltpu.VMEM((slots, 32, TILE), jnp.bfloat16),
-            pltpu.VMEM((6, TILE, TILE), jnp.float32),
-            pltpu.VMEM((2, TILE, 4 * TILE), jnp.bfloat16),
-            pltpu.VMEM((2, 32, 4 * TILE), jnp.bfloat16),
+            pltpu.VMEM((3 * GROUP, TILE, TILE), jnp.float32),
+            pltpu.VMEM((KEPT[own] + 1,) + bank, jnp.bfloat16),
+            pltpu.VMEM((GROUP, 32, 2 * TILE), jnp.bfloat16),
             pltpu.VMEM((rows, 32, TILE), jnp.float32),
             pltpu.VMEM((rows, TILE), jnp.int32),
             pltpu.SMEM((rows, TILE), jnp.int32),
             pltpu.SemaphoreType.DMA,
+            pltpu.SemaphoreType.DMA((KEPT[own],)),
         ],
         compiler_params=PARAMS,
-        name="apply_own" if own else "apply_cross",
+        name=("again_" if again else "apply_") + ("own" if own else "cross"),
     )(*operands)
-    return result if sums else result[0]
 
 
 def shards(right_side, points, active):
@@ -470,14 +541,18 @@
     rows, cols, rank, box = sort_points(place, points, right_side)
     around = neighbours(rows)
     fixed = (place, active, cols, box)
-    part = apply_pairs(*fixed, (rows,), (rows,))
-    w0 = apply_pairs(*fixed, around, around, part)
+    part, kept_own = apply_pairs(fixed, (rows,), (rows,))
+    w0, kept_cross = apply_pairs(fixed, around, around, part)
     w0_around = neighbours(w0)
     w0_all = lax.all_gather(unsort(w0, rank), "rep", axis=0, tiled=True)
-    part = apply_pairs(*fixed, (rows,), (w0,))
-    w1, sums = apply_pairs(*fixed, around, w0_around, part, (rows, w0))
-    w1_all = lax.all_gather(unsort(w1, rank), "rep", axis=0, tiled=True)
-    sums = sum_over_blk(sums[:, 0:4].T)
+    (part,) = apply_pairs(fixed, (rows,), (w0,), kept=kept_own)
+    w1, line = apply_pairs(fixed, around, w0_around, part, (rows, w0), kept_cross)
+    line, mine = lax.optimization_barrier((line, unsort(w1, rank)))
+    w1_all = lax.all_gather(mine, "rep", axis=0, tiled=True)
+    lines = lax.all_to_all(line[:, 0:64], ("blk", "rep"), 0, 0, tiled=True)
+    members = lax.axis_size("rep")
+    sums = jnp.sum(lines.reshape(-1, members, 4, sides), axis=0)
+    sums = jnp.transpose(sums, (1, 0, 2)).reshape(4, members * sides)
     s00, s01, s11, s12 = (sums[k] for k in range(4))
     image_norm = shift * s00 + s01
     alpha = s00 / image_norm
@@ -496,11 +571,7 @@
             alpha1 * alpha,
         ]
     )
-    spread = jnp.zeros((5, 4, sides), jnp.float32)
-    for mask in range(4):
-        piece = factors if mask == 0 else exchange(factors, mask, "rep")
-        spread = lax.dynamic_update_slice_in_dim(spread, piece[:, None], member ^ mask, 1)
-    factor = spread.reshape(5, 4 * sides, 1)
+    factor = factors[:, :, None]
     posterior = factor[0] * right_side + factor[1] * w0_all
     residual = factor[2] * right_side + factor[3] * w0_all + factor[4] * w1_all
     return (posterior, residual)

time: 146 us -> 130 us (0.89)
  blocking collectives: 0 us -> 31.3 us
  starting transfers between devices: 34.6 us -> 9.14 us
  waiting for transfers between devices: 14.9 us -> 0.11 us
  Pallas kernels: 67.7 us -> 53.6 us
  local copies, waits for them, and re-layouts: 8.23 us -> 14.8 us
    all_to_all x0 -> x1, blocking collectives: none -> 31.3 us  [shards(): lines = lax.all_to_all(line[:, 0:64], ('blk', 'rep'), 0, 0, tiled=True)]
    ppermute x12 -> x0, starting transfers between devices: 23 us -> none  [exchange(): return lax.ppermute(values, axis, [(i, i ^ mask) for i in devices])]
    ppermute x12 -> x0, waiting for transfers between devices: 14.9 us -> none  [exchange(): return lax.ppermute(values, axis, [(i, i ^ mask) for i in devices])]
    pallas_call x4, Pallas kernels: 54.8 us -> 40.8 us  [apply_pairs(): pl.pallas_call(partial(apply_kernel, own, again), out_shape=out_shape, in...]
    unnamed x29 -> x47, local copies, waits for them, and re-layouts: 7.25 us -> 13.6 us
    ppermute x4, starting transfers between devices: 11.5 us -> 9.07 us  [from_behind(): return lax.ppermute(block, axis, route)]
  transfers between devices with their start and end apart: 18 -> 6, of which waited for: 8 -> 0; matrix products, arithmetic and copies ran while one was open for 1% -> 3% of each run, Pallas kernels for 36% -> 29%
where the time goes in v3:
time: 130 us; the launch traced here: 128 us
  Pallas kernels  53.6 us (41%)
  blocking collectives  31.3 us (24%)
  local copies, waits for them, and re-layouts  14.8 us (11%)
  between operations  14.3 us (11%)
  starting transfers between devices  9.14 us (7%)
  other arithmetic  4.47 us (3%)
    pallas_call x4, Pallas kernels, apply_pairs(): pl.pallas_call(partial(apply_kernel, own, again), out_shape=out_shape, in...  40.8 us
    all_to_all x1, blocking collectives, shards(): lines = lax.all_to_all(line[:, 0:64], ('blk', 'rep'), 0, 0, tiled=True)  31.3 us
    unnamed x47, local copies, waits for them, and re-layouts  13.6 us
    ppermute x4, starting transfers between devices, from_behind(): return lax.ppermute(block, axis, route)  9.07 us
    pallas_call x1, Pallas kernels, sort_points(): pl.pallas_call(sort_kernel, out_shape=(jax.ShapeDtypeStruct((24, width),...  6.58 us
    pallas_call x2, Pallas kernels, unsort(): pl.pallas_call(unsort_kernel, out_shape=jax.ShapeDtypeStruct(values.shape...  6.29 us
    add x1, other arithmetic, shards(): residual = factor[2] * right_side + factor[3] * w0_all + factor[4] * w1_all  3.23 us
  transfers between devices with their start and end apart: 6, of which 0 were waited for; matrix products, arithmetic and copies ran while one was open for 3% of the time, Pallas kernels for 29%

profile of v3, /device:TPU:8, one launch (start us, length us, event | category | flops | bytes accessed | tf_op | source)
XLA Modules:
  0.0 127.8 jit_solution(8998638055650678013)
XLA Ops:
  7.3 1.2 copy-done
  8.5 0.8 copy-done.22
  9.4 6.6 %sort_points.1 = (f32[24,4096]{1,0:T(8,128)S(1)}, f32[4096,128]{1,0:T(8,128)S(1)}, s32[8,4096]{1,0:T(8,128)S(1)}, f32[2,32,128]{2,1,0:T(8,128)S(1)}) custom-call(s32[2]{0:T(128)S(1)} %pad_add_fusion.place_ref.refs_0_, f32[3,4096]{1,0:T(4,128)S(1)} %copy-done.22, f32[64,4096]{1,0:T(8,128)S(1)} %copy-done), custom_call_target="tpu_custom_call" | custom-call | tf_op jit(solution)/shard_map/sort_points/pallas_call | solution.py:144
  16.0 0.6 copy-done.13
  16.6 0.7 copy-done.18
  17.2 1.8 %collective-permute-start = (f32[24,4096]{1,0:T(8,128)S(1)}, f32[24,4096]{1,0:T(8,128)S(1)}, u32[]{:S(2)}, u32[]{:S(2)}) collective-permute-start(f32[24,4096]{1,0:T(8,128)S(1)} %get-tuple-element.16.refs_4_.refs_5_.refs_9_), channel_id=1, source_target_pairs={{0,4},{4,8},{8,12},{12,16},{16,20},{20,24},{24,28},{28,32},{32,36}... | collective-permute-start | bytes 1179656 | tf_op jit(solution)/shard_map/ppermute | solution.py:34
  19.0 1.3 %collective-permute-start.1 = (f32[24,4096]{1,0:T(8,128)S(1)}, f32[24,4096]{1,0:T(8,128)S(1)}, u32[]{:S(2)}, u32[]{:S(2)}) collective-permute-start(f32[24,4096]{1,0:T(8,128)S(1)} %get-tuple-element.16.refs_4_.refs_5_.refs_9_), channel_id=1, source_target_pairs={{4,0},{8,4},{12,8},{16,12},{20,16},{24,20},{28,24},{32,28},{36,32}... | collective-permute-start | bytes 1179656 | tf_op jit(solution)/shard_map/ppermute | solution.py:34
  20.3 1.4 %copy.16.refs_1_ = s32[64,5]{1,0:T(8,128)} copy(s32[64,5]{0,1:T(8,128)} %param.5) | data formatting | bytes 2560 | tf_op args[2]
  21.7 0.8 copy-done.9
  22.4 0.8 copy-done.14
  23.2 16.6 %apply_own.1 = (f32[16,4096]{1,0:T(8,128)S(1)}, bf16[32,4,256,256]{3,2,1,0:T(8,128)(2,1)}) custom-call(s32[2]{0:T(128)S(1)} %pad_add_fusion.place_ref.refs_0_, s32[64,5]{1,0:T(8,128)S(1)} %copy-done.9, f32[4096,128]{1,0:T(8,128)S(1)} %get-tuple-element.14.refs_2_, f32[2,32,128]{2,1,0:T(8,128)S(1)} %copy-done.14, ...), custom_call_target="tpu_custom_call" | custom-call | tf_op jit(solution)/shard_map/apply_own/pallas_call | solution.py:508
  39.8 0.8 copy-done.10
  40.6 0.8 copy-done.15
  41.4 7.6 %apply_cross.1 = (f32[16,4096]{1,0:T(8,128)S(1)}, bf16[8,4,256,256]{3,2,1,0:T(8,128)(2,1)}) custom-call(s32[2]{0:T(128)S(1)} %pad_add_fusion.place_ref.refs_0_, s32[64,5]{1,0:T(8,128)S(1)} %copy-done.10, f32[4096,128]{1,0:T(8,128)S(1)} %get-tuple-element.14.refs_2_, f32[2,32,128]{2,1,0:T(8,128)S(1)} %copy-done.15, ...), custom_call_target="tpu_custom_call" | custom-call | tf_op jit(solution)/shard_map/apply_cross/pallas_call | solution.py:508
  49.0 2.8 %unsort.3 = f32[16,4096]{1,0:T(8,128)S(1)} custom-call(f32[16,4096]{1,0:T(8,128)S(1)} %get-tuple-element.18.refs_5_.refs_10_.sorted_ref, s32[8,4096]{1,0:T(8,128)S(1)} %copy-done.19), custom_call_target="tpu_custom_call" | custom-call | tf_op jit(solution)/shard_map/unsort/pallas_call | solution.py:183
  51.8 0.7 copy-done.8
  52.6 4.7 %collective-permute-start.2 = (f32[16,4096]{1,0:T(8,128)S(1)}, f32[16,4096]{1,0:T(8,128)S(1)}, u32[]{:S(2)}, u32[]{:S(2)}) collective-permute-start(f32[16,4096]{1,0:T(8,128)S(1)} %get-tuple-element.18.refs_5_.refs_10_.sorted_ref), channel_id=1, source_target_pairs={{0,4},{4,8},{8,12},{12,16},{16,20},{20,24},{24,28},{28,32},{32,36}... | collective-permute-start | bytes 786440 | tf_op jit(solution)/shard_map/ppermute | solution.py:34
  57.3 1.3 %collective-permute-start.3 = (f32[16,4096]{1,0:T(8,128)S(1)}, f32[16,4096]{1,0:T(8,128)S(1)}, u32[]{:S(2)}, u32[]{:S(2)}) collective-permute-start(f32[16,4096]{1,0:T(8,128)S(1)} %get-tuple-element.18.refs_5_.refs_10_.sorted_ref), channel_id=1, source_target_pairs={{4,0},{8,4},{12,8},{16,12},{20,16},{24,20},{28,24},{32,28},{36,32}... | collective-permute-start | bytes 786440 | tf_op jit(solution)/shard_map/ppermute | solution.py:34
  58.6 0.7 copy-done.11
  59.4 0.8 copy-done.16
  60.1 10.2 %again_own.1.refs_8_ = f32[16,4096]{1,0:T(8,128)S(1)} custom-call(s32[2]{0:T(128)S(1)} %pad_add_fusion.place_ref.refs_0_, s32[64,5]{1,0:T(8,128)S(1)} %copy-done.11, f32[4096,128]{1,0:T(8,128)S(1)} %get-tuple-element.14.refs_2_, f32[2,32,128]{2,1,0:T(8,128)S(1)} %copy-done.16, f32[24,4096]{1,0:T(8,128)S(1)} %get-tuple-element.16.refs_4_.refs_5_.refs_9_, ...), custom_call_target="tpu_custom_call" | custom-call | tf_op jit(solution)/shard_map/again_own/pallas_call | solution.py:508
  70.4 1.0 copy-done.3
  71.4 1.0 copy-done.5
  72.4 0.9 copy-done.7
  73.4 6.4 %again_cross.1 = (f32[16,4096]{1,0:T(8,128)S(1)}, f32[256,128]{1,0:T(8,128)S(1)}) custom-call(s32[2]{0:T(128)S(1)} %pad_add_fusion.place_ref.refs_0_, s32[64,5]{1,0:T(8,128)S(1)} %copy-done.12, f32[4096,128]{1,0:T(8,128)S(1)} %get-tuple-element.14.refs_2_, f32[2,32,128]{2,1,0:T(8,128)S(1)} %copy-done.17, f32[24,4096]{1,0:T(8,128)S(1)} %copy-done.3, ...), custom_call_target="tpu_custom_call" | custom-call | tf_op jit(solution)/shard_map/again_cross/pallas_call | solution.py:508
  79.8 0.6 copy-done.21
  80.4 3.5 %unsort.2 = f32[16,4096]{1,0:T(8,128)} custom-call(f32[16,4096]{1,0:T(8,128)S(1)} %get-tuple-element.22.sorted_ref, s32[8,4096]{1,0:T(8,128)S(1)} %copy-done.20), custom_call_target="tpu_custom_call" | custom-call | tf_op jit(solution)/shard_map/unsort/pallas_call | solution.py:183
  84.0 31.3 %all_to_all.9 = f32[256,1,64]{2,1,0:T(1,128)S(1)} all-to-all(f32[256,1,64]{2,1,0:T(1,128)} %bitcast.7), channel_id=1, replica_groups=mesh['blk'=64,'rep'=4] {'blk','rep'}, dimensions={0} | all-to-all | bytes 131072 | tf_op jit(solution)/shard_map/all_to_all | solution.py:552
  115.3 0.5 broadcast.113
  115.8 1.0 reduce.19
  116.8 0.3 reshape.230
  117.7 3.2 %multiply_add_fusion = (f32[64,4096]{1,0:T(8,128)}, f32[64,4096]{1,0:T(8,128)}) fusion(f32[64,4096]{1,0:T(8,128)} %all-gather.5.cloned.1.call-done, f32[64,4096]{1,0:T(8,128)} %all-gather.3.cloned.1.call-done, f32[64,4096]{1,0:T(8,128)S(1)} %copy-done.1, f32[64]{0:T(128)S(1)} %get-tuple-element.40, f32[64]{0:T(128)S(1)} %get-tuple-element.38, ...), kind=kLoop, calls=%fused_computation | loop fusion | flops 2097152 | bytes 5244160 | tf_op jit(solution)/shard_map/add | solution.py:576
  (51 shorter events, 0.9 us)
Async XLA Ops:
  7.2 110.5 %all-gather.3.cloned.1.call-start = ((), (), s32[]{:S(2)}) async-start(), calls=%async_computation.1 | async-start | bytes 1310720 | tf_op jit(solution)/shard_map/all_gather | solution.py:547
  7.3 1.2 copy-start
  8.5 0.8 copy-start.22
  15.9 0.6 copy-start.13
  16.6 0.7 copy-start.18
  17.2 22.6 %collective-permute-start = (f32[24,4096]{1,0:T(8,128)S(1)}, f32[24,4096]{1,0:T(8,128)S(1)}, u32[]{:S(2)}, u32[]{:S(2)}) collective-permute-start(f32[24,4096]{1,0:T(8,128)S(1)} %get-tuple-element.16.refs_4_.refs_5_.refs_9_), channel_id=1, source_target_pairs={{0,4},{4,8},{8,12},{12,16},{16,20},{20,24},{24,28},{28,32},{32,36}... | collective-permute-start | bytes 1179656 | tf_op jit(solution)/shard_map/ppermute | solution.py:34
  19.0 20.8 %collective-permute-start.1 = (f32[24,4096]{1,0:T(8,128)S(1)}, f32[24,4096]{1,0:T(8,128)S(1)}, u32[]{:S(2)}, u32[]{:S(2)}) collective-permute-start(f32[24,4096]{1,0:T(8,128)S(1)} %get-tuple-element.16.refs_4_.refs_5_.refs_9_), channel_id=1, source_target_pairs={{4,0},{8,4},{12,8},{16,12},{20,16},{24,20},{28,24},{32,28},{36,32}... | collective-permute-start | bytes 1179656 | tf_op jit(solution)/shard_map/ppermute | solution.py:34
  21.7 0.8 copy-start.9
  22.4 0.8 copy-start.14
  23.2 25.8 %copy-start.19 = (s32[8,4096]{1,0:T(8,128)S(1)}, s32[8,4096]{1,0:T(8,128)}, u32[]{:S(2)}) copy-start(s32[8,4096]{1,0:T(8,128)} %copy-done.18) | copy-start | bytes 393220
  39.8 30.6 %copy-start.2 = (f32[24,4096]{1,0:T(8,128)}, f32[24,4096]{1,0:T(8,128)S(1)}, u32[]{:S(2)}) copy-start(f32[24,4096]{1,0:T(8,128)S(1)} %collective-permute-done.refs_4_.refs_6_) | copy-start | bytes 1179652
  39.8 30.6 %copy-start.4 = (f32[24,4096]{1,0:T(8,128)}, f32[24,4096]{1,0:T(8,128)S(1)}, u32[]{:S(2)}) copy-start(f32[24,4096]{1,0:T(8,128)S(1)} %collective-permute-done.1.refs_5_.refs_7_) | copy-start | bytes 1179652
  39.8 0.8 copy-start.10
  40.6 0.8 copy-start.15
  49.0 21.4 %copy-start.6 = (f32[16,4096]{1,0:T(8,128)}, f32[16,4096]{1,0:T(8,128)S(1)}, u32[]{:S(2)}) copy-start(f32[16,4096]{1,0:T(8,128)S(1)} %get-tuple-element.18.refs_5_.refs_10_.sorted_ref) | copy-start | bytes 786436
  51.8 0.7 copy-start.8
  52.5 65.2 %all-gather.5.cloned.1.call-start = ((), (), s32[]{:S(2)}) async-start(), calls=%async_computation.2 | async-start | bytes 1310720 | tf_op jit(solution)/shard_map/all_gather | solution.py:551
  52.6 17.8 %collective-permute-start.2 = (f32[16,4096]{1,0:T(8,128)S(1)}, f32[16,4096]{1,0:T(8,128)S(1)}, u32[]{:S(2)}, u32[]{:S(2)}) collective-permute-start(f32[16,4096]{1,0:T(8,128)S(1)} %get-tuple-element.18.refs_5_.refs_10_.sorted_ref), channel_id=1, source_target_pairs={{0,4},{4,8},{8,12},{12,16},{16,20},{20,24},{24,28},{28,32},{32,36}... | collective-permute-start | bytes 786440 | tf_op jit(solution)/shard_map/ppermute | solution.py:34
  57.3 13.1 %collective-permute-start.3 = (f32[16,4096]{1,0:T(8,128)S(1)}, f32[16,4096]{1,0:T(8,128)S(1)}, u32[]{:S(2)}, u32[]{:S(2)}) collective-permute-start(f32[16,4096]{1,0:T(8,128)S(1)} %get-tuple-element.18.refs_5_.refs_10_.sorted_ref), channel_id=1, source_target_pairs={{4,0},{8,4},{12,8},{16,12},{20,16},{24,20},{28,24},{32,28},{36,32}... | collective-permute-start | bytes 786440 | tf_op jit(solution)/shard_map/ppermute | solution.py:34
  58.6 0.8 copy-start.11
  59.4 0.8 copy-start.16
  60.1 10.3 %copy-start.12 = (s32[64,5]{1,0:T(8,128)S(1)}, s32[64,5]{1,0:T(8,128)}, u32[]{:S(2)}) copy-start(s32[64,5]{1,0:T(8,128)} %copy.16.refs_1_) | copy-start | bytes 3844
  60.1 10.3 %copy-start.17 = (f32[2,32,128]{2,1,0:T(8,128)S(1)}, f32[2,32,128]{2,1,0:T(8,128)}, u32[]{:S(2)}) copy-start(f32[2,32,128]{2,1,0:T(8,128)} %copy-done.13) | copy-start | bytes 98308
  70.4 1.0 copy-start.3
  71.4 1.0 copy-start.5
  72.4 0.9 copy-start.7
  73.4 7.0 %copy-start.20 = (s32[8,4096]{1,0:T(8,128)S(1)}, s32[8,4096]{1,0:T(8,128)}, u32[]{:S(2)}) copy-start(s32[8,4096]{1,0:T(8,128)} %copy-done.18) | copy-start | bytes 393220
  73.4 44.3 %copy-start.1 = (f32[64,4096]{1,0:T(8,128)S(1)}, f32[64,4096]{1,0:T(8,128)}, u32[]{:S(2)}) copy-start(f32[64,4096]{1,0:T(8,128)} %sides_ref.1) | copy-start | bytes 3145732
  79.8 0.7 copy-start.21
Sparse Core Ops, SparseCore 0:
  52.7 32.2 all-gather.2
  87.3 30.3 all-gather.4

commit v4 on v3

--- a/solution.py
+++ b/solution.py
@@ -13,7 +13,8 @@
 STRIP = 256
 BATCH = 4
 GROUP = 4
-KEPT = {True: 32, False: 8}
+KEPT = {True: 24, False: 8}
+EARLY = {True: 12, False: 4}
 CELLS_X = 4
 CELLS_Y = 8
 CELLS = CELLS_X * CELLS_Y
@@ -25,13 +26,19 @@
 profile_scale = 4.0 / support_radius**5
 VMEM = pl.BlockSpec(memory_space=pltpu.VMEM)
 SMEM = pl.BlockSpec(memory_space=pltpu.SMEM)
-PARAMS = pltpu.CompilerParams(vmem_limit_bytes=48 * 1024 * 1024)
+ANY = pl.BlockSpec(memory_space=pl.ANY)
+LIMIT = 48 * 1024 * 1024
 
 
 def from_behind(block, axis, distance):
     devices = range(lax.axis_size(axis))
     route = [(i - distance, i) for i in devices if i - distance in devices]
     return lax.ppermute(block, axis, route)
+
+
+def exchange(values, mask, axis):
+    devices = range(lax.axis_size(axis))
+    return lax.ppermute(values, axis, [(i, i ^ mask) for i in devices])
 
 
 def split3(values):
@@ -55,8 +62,9 @@
 
 
 def sort_kernel(
-    place_ref,
-    points_ref,
+    count,
+    meta_ref,
+    points_hbm,
     sides_ref,
     rows_ref,
     cols_ref,
@@ -66,11 +74,18 @@
     feature_ref,
     split_ref,
     edge_ref,
+    points_ref,
     arrived,
 ):
-    first = pl.multiple_of(place_ref[1] * 16, 16)
-    fetch = pltpu.make_async_copy(sides_ref.at[pl.ds(first, 16), :], vector_ref, arrived)
+    first = pl.multiple_of(meta_ref[1] * 16, 16)
+    locate = pltpu.make_async_copy(points_hbm, points_ref, arrived.at[0])
+    locate.start()
+    fetch = pltpu.make_async_copy(
+        sides_ref.at[pl.ds(first, 16), :], vector_ref, arrived.at[1]
+    )
     fetch.start()
+    for own in (True, False):
+        box_ref[2 if own else 3] = pair_flags(own, meta_ref, count, box_ref.shape[1:])
     upper = lax.broadcasted_iota(jnp.int32, (TILE, TILE), 0) <= lax.broadcasted_iota(
         jnp.int32, (TILE, TILE), 1
     )
@@ -82,6 +97,7 @@
     number = lax.broadcasted_iota(jnp.int32, (CELLS, TILE), 0).astype(jnp.float32)
     feature_ref[16:32, :] = jnp.zeros((16, B), jnp.float32)
     split_ref[96:128, :] = jnp.zeros((32, B), jnp.bfloat16)
+    locate.wait()
     for c in range(2):
         span = slice(c * B, (c + 1) * B)
         cell = cell_of(points_ref[0:1, span], CELLS_X) * CELLS_Y + cell_of(
@@ -139,28 +155,29 @@
             ]
 
 
-def sort_points(place, points, right_side):
+def sort_points(count, meta, points, right_side):
     width = 2 * B
     return pl.pallas_call(
-        sort_kernel,
+        partial(sort_kernel, count),
         out_shape=(
             jax.ShapeDtypeStruct((24, width), jnp.float32),
             jax.ShapeDtypeStruct((width, TILE), jnp.float32),
             jax.ShapeDtypeStruct((8, width), jnp.int32),
-            jax.ShapeDtypeStruct((2, width // TILE, TILE), jnp.float32),
+            jax.ShapeDtypeStruct((4, width // TILE, TILE), jnp.float32),
         ),
-        in_specs=[SMEM, VMEM, pl.BlockSpec(memory_space=pl.ANY)],
+        in_specs=[SMEM, ANY, ANY],
         out_specs=(VMEM, VMEM, VMEM, VMEM),
         scratch_shapes=[
             pltpu.VMEM((16, width), jnp.float32),
             pltpu.VMEM((32, B), jnp.float32),
             pltpu.VMEM((128, B), jnp.bfloat16),
             pltpu.VMEM((2, TILE, TILE), jnp.float32),
-            pltpu.SemaphoreType.DMA,
+            pltpu.VMEM((3, width), jnp.float32),
+            pltpu.SemaphoreType.DMA((2,)),
         ],
-        compiler_params=PARAMS,
+        compiler_params=pltpu.CompilerParams(vmem_limit_bytes=LIMIT),
         name="sort_points",
-    )(place, points, right_side)
+    )(meta, points, right_side)
 
 
 def unsort_kernel(sorted_ref, rank_ref, out_ref, split_ref, total_ref):
@@ -186,14 +203,33 @@
         in_specs=[VMEM, VMEM],
         out_specs=VMEM,
         scratch_shapes=[pltpu.VMEM((48, B), jnp.bfloat16), pltpu.VMEM((48, B), jnp.float32)],
-        compiler_params=PARAMS,
+        compiler_params=pltpu.CompilerParams(vmem_limit_bytes=LIMIT),
         name="unsort",
     )(values, rank)
 
 
-def pair_table(own, place_ref, active_ref, box_ref, xyz_refs, null):
-    shape = (box_ref.shape[1], TILE)
-    row = lax.broadcasted_iota(jnp.int32, shape, 0)
+def pair_flags(own, meta_ref, count, shape):
+    is_second = lax.broadcasted_iota(jnp.int32, shape, 0) >= shape[0] // 2
+    quarter = lax.broadcasted_iota(jnp.int32, shape, 1) // (TILE // 4)
+    column = meta_ref[0]
+    if own:
+        flag = jnp.where(is_second == (quarter == 1), 1, meta_ref[2])
+        return jnp.where(quarter < 2, flag, 0).astype(jnp.float32)
+    has_behind = jnp.where(column >= 1, 1, 0)
+    has_ahead = jnp.where(column + 1 < count, 1, 0)
+    flag = jnp.zeros(shape, jnp.int32)
+    for c in range(2):
+        for q in range(4):
+            if q < 2:
+                value = meta_ref[8 + 2 * q + c] * has_behind
+            else:
+                value = meta_ref[3 + 2 * c + (q - 2)] * has_ahead
+            flag = jnp.where((is_second == (c == 1)) & (quarter == q), value, flag)
+    return flag.astype(jnp.float32)
+
+
+def pair_table(own, box_ref, xyz_refs, null):
+    shape = box_ref.shape[1:]
     lane = lax.broadcasted_iota(jnp.int32, shape, 1)
     total = jnp.zeros(shape, jnp.float32)
     for axis in range(3):
@@ -209,29 +245,7 @@
         gap = jnp.maximum(jnp.maximum(low_s - high_t, low_t - high_s), 0.0)
         total = total + gap * gap
     near = total <= support_radius * support_radius * (1.0 + 1e-4)
-    column = place_ref[0]
-    count = active_ref.shape[0]
-    is_second = row >= shape[0] // 2
-    quarter = lane // (TILE // 4)
-    if own:
-        across = active_ref[column, 0]
-        same = is_second == (quarter == 1)
-        flag = jnp.where(same, 1, across)
-        flag = jnp.where(quarter < 2, flag, 0)
-    else:
-        behind = jnp.maximum(column - 1, 0)
-        has_behind = jnp.where(column >= 1, 1, 0)
-        has_ahead = jnp.where(column + 1 < count, 1, 0)
-        flag = jnp.zeros(shape, jnp.int32)
-        for c in range(2):
-            for q in range(4):
-                if q < 2:
-                    value = active_ref[behind, 1 + 2 * q + c] * has_behind
-                else:
-                    value = active_ref[column, 1 + 2 * c + (q - 2)] * has_ahead
-                here = (is_second == (c == 1)) & (quarter == q)
-                flag = jnp.where(here, value, flag)
-    near = near & (flag > 0)
+    near = near & (box_ref[2 if own else 3] > 0.0)
     upper = lax.broadcasted_iota(jnp.int32, (TILE, TILE), 0) <= lax.broadcasted_iota(
         jnp.int32, (TILE, TILE), 1
     )
@@ -255,21 +269,21 @@
 
 def apply_kernel(own, again, *refs):
     refs = list(refs)
-    place_ref, active_ref, cols_ref, box_ref = refs[:4]
-    del refs[:4]
+    cols_ref, box_ref = refs[:2]
+    del refs[:2]
     sources = 1 if own else 2
     xyz_refs = [refs.pop(0) for _ in range(sources)]
     vec_refs = [refs.pop(0) for _ in range(sources)]
     add_ref = None if own else refs.pop(0)
     sums = again and not own
     base_refs = [refs.pop(0) for _ in range(2)] if sums else None
-    kept_ref = refs.pop(0) if again else None
+    if again:
+        list_ref, kept_ref = refs.pop(0), refs.pop(0)
     out_ref = refs.pop(0)
     if not again:
-        kept_ref = refs.pop(0)
+        table_ref, kept_ref = refs.pop(0), refs.pop(0)
     sums_ref = refs.pop(0) if sums else None
-    left_xyz, right_xyz, left_w, right_w, target, bank, weights, total_ref = refs[:8]
-    table_ref, list_ref, arrived, moved = refs[8:]
+    left_xyz, right_xyz, left_w, right_w, target, bank, weights, total_ref, moved = refs[:9]
     rows = out_ref.shape[1] // TILE
     cells = rows // GROUP
     kept = KEPT[own]
@@ -277,9 +291,18 @@
     lane = lax.broadcasted_iota(jnp.int32, (8, TILE), 1)
     is_left = lane < SUB
 
-    table_ref[...] = pair_table(own, place_ref, active_ref, box_ref, xyz_refs, null)
-    load = pltpu.make_async_copy(table_ref, list_ref, arrived)
-    load.start()
+    def transfer(g):
+        ends = (kept_ref.at[g], bank.at[g]) if again else (bank.at[g], kept_ref.at[g])
+        return pltpu.make_async_copy(*ends, moved.at[g])
+
+    if again:
+        for g in range(EARLY[own]):
+            transfer(g).start()
+    else:
+        list_ref, arrived = refs[9:]
+        table_ref[...] = pair_table(own, box_ref, xyz_refs, null)
+        load = pltpu.make_async_copy(table_ref, list_ref, arrived)
+        load.start()
 
     def spread(values):
         turned = pltpu.roll(values, SUB, 1)
@@ -297,6 +320,13 @@
         low = (values - high.astype(jnp.float32)).astype(jnp.bfloat16)
         return jnp.concatenate([high, low], axis=0)
 
+    def prepare_xyz(s, spot, slot):
+        xyz = spread(xyz_refs[s][16:24, spot])
+        left_xyz[slot] = xyz[0]
+        right_xyz[slot] = xyz[1]
+        left_xyz[slot + 1] = xyz[2]
+        right_xyz[slot + 1] = xyz[3]
+
     for s in range(sources):
 
         def prepare(g, carry):
@@ -304,11 +334,8 @@
                 t = g * 4 + u
                 spot = pl.ds(pl.multiple_of(t * TILE, TILE), TILE)
                 slot = 2 * (t + s * rows)
-                xyz = spread(xyz_refs[s][16:24, spot])
-                left_xyz[slot] = xyz[0]
-                right_xyz[slot] = xyz[1]
-                left_xyz[slot + 1] = xyz[2]
-                right_xyz[slot + 1] = xyz[3]
+                if not again:
+                    prepare_xyz(s, spot, slot)
                 vec = spread(vec_refs[s][0:16, spot])
                 left_w[slot] = parts(vec[0])
                 right_w[slot] = parts(vec[1])
@@ -384,16 +411,25 @@
         for j, image in zip(members(cell), images):
             total_ref[j] += image
 
-    def transfer(g):
-        ends = (kept_ref.at[g], bank.at[g]) if again else (bank.at[g], kept_ref.at[g])
-        return pltpu.make_async_copy(*ends, moved.at[g])
-
-    load.wait()
-    used = lax.fori_loop(0, cells, lambda cell, n: n + batches(cell), 0)
-    used = jnp.minimum(used, kept)
+    if not again:
+        load.wait()
+    needed = lax.fori_loop(0, cells, lambda cell, n: n + batches(cell), 0)
+    used = jnp.minimum(needed, kept)
 
     if again:
-        lax.fori_loop(0, used, lambda g, carry: (transfer(g).start(), carry)[1], 0)
+        early = EARLY[own]
+        lax.fori_loop(early, used, lambda g, carry: (transfer(g).start(), carry)[1], 0)
+
+        @pl.when(needed > kept)
+        def _():
+            for s in range(sources):
+
+                def prepare_again(t, carry):
+                    spot = pl.ds(pl.multiple_of(t * TILE, TILE), TILE)
+                    prepare_xyz(s, spot, 2 * (t + s * rows))
+                    return carry
+
+                lax.fori_loop(0, rows, prepare_again, 0)
 
         def row_group(cell, g):
             def step(n, g):
@@ -417,6 +453,7 @@
             return lax.fori_loop(0, batches(cell), step, g)
 
         lax.fori_loop(0, cells, row_group, 0)
+        lax.fori_loop(used, early, lambda g, carry: (transfer(g).wait(), carry)[1], 0)
     else:
 
         def row_group(cell, state):
@@ -490,18 +527,21 @@
     again = kept is not None
     operands = [*fixed, *coords, *vectors]
     operands += ([] if own else [added]) + list(bases)
-    specs = [SMEM, SMEM] + [VMEM] * (len(operands) - 2)
+    specs = [VMEM] * len(operands)
     rows = 2 * B // TILE
     slots = 2 * rows * len(coords) + 1
     out_shape = [jax.ShapeDtypeStruct((16, 2 * B), jnp.float32)]
     out_specs = [VMEM]
     bank = (GROUP, 2 * TILE, 2 * TILE)
     if again:
-        operands.append(kept)
-        specs.append(pl.BlockSpec(memory_space=pl.ANY))
+        operands += kept
+        specs += [SMEM, ANY]
+        scratch = []
     else:
+        out_shape.append(jax.ShapeDtypeStruct((rows, TILE), jnp.int32))
         out_shape.append(jax.ShapeDtypeStruct((KEPT[own],) + bank, jnp.bfloat16))
-        out_specs.append(pl.BlockSpec(memory_space=pl.ANY))
+        out_specs += [VMEM, ANY]
+        scratch = [pltpu.SMEM((rows, TILE), jnp.int32), pltpu.SemaphoreType.DMA]
     if bases:
         out_shape.append(jax.ShapeDtypeStruct((256, TILE), jnp.float32))
         out_specs.append(VMEM)
@@ -519,62 +559,102 @@
             pltpu.VMEM((KEPT[own] + 1,) + bank, jnp.bfloat16),
             pltpu.VMEM((GROUP, 32, 2 * TILE), jnp.bfloat16),
             pltpu.VMEM((rows, 32, TILE), jnp.float32),
-            pltpu.VMEM((rows, TILE), jnp.int32),
-            pltpu.SMEM((rows, TILE), jnp.int32),
-            pltpu.SemaphoreType.DMA,
             pltpu.SemaphoreType.DMA((KEPT[own],)),
+            *scratch,
         ],
-        compiler_params=PARAMS,
+        compiler_params=pltpu.CompilerParams(vmem_limit_bytes=LIMIT),
         name=("again_" if again else "apply_") + ("own" if own else "cross"),
     )(*operands)
+
+
+def finish_kernel(lines_ref, sides_ref, w0_ref, *refs):
+    pieces, (posterior_ref, residual_ref, factor_ref) = refs[:4], refs[4:]
+
+    @pl.when(pl.program_id(0) == 0)
+    def _():
+        lines = lines_ref[...]
+        row = lax.broadcasted_iota(jnp.int32, lines.shape, 0)
+        sums = [
+            jnp.sum(jnp.where((row & 3) == q, lines, 0.0), axis=0, keepdims=True)
+            for q in range(4)
+        ]
+        sums = jnp.concatenate(sums + [jnp.zeros((4, lines.shape[1]), jnp.float32)], axis=0)
+        sums = jnp.concatenate([sums, jnp.ones_like(sums)], axis=1)
+        sums = jnp.concatenate([sums, jnp.ones((TILE - 8, TILE), jnp.float32)], axis=0).T
+        s00, s01, s11, s12 = (sums[16 * k : 16 * k + 16] for k in range(4))
+        image_norm = shift * s00 + s01
+        alpha = s00 / image_norm
+        keep = s01 / image_norm
+        rr1 = alpha * alpha * (s11 - s01 * (s01 / s00))
+        beta = rr1 / s00
+        both = keep + beta
+        curved = both * both * s01 - 2.0 * both * alpha * s11 + alpha * alpha * s12
+        alpha1 = rr1 / (shift * rr1 * (1.0 + beta) + curved)
+        factor_ref[0] = (s00 + s01) / image_norm - noise_level * alpha1 * both
+        factor_ref[1] = noise_level * alpha1 * alpha
+        factor_ref[2] = keep - shift * alpha1 * both
+        factor_ref[3] = shift * alpha1 * alpha - alpha - alpha1 * both
+        factor_ref[4] = alpha1 * alpha
+
+    for member in range(4):
+
+        @pl.when(lax.axis_index("rep") == member)
+        def _():
+            for q in range(4):
+                rows = slice(16 * q, 16 * q + 16)
+                factor = [factor_ref[k, :, q : q + 1] for k in range(5)]
+                side = sides_ref[rows, :]
+                first = w0_ref[rows, :]
+                second = pieces[q ^ member][...]
+                posterior_ref[rows, :] = factor[0] * side + factor[1] * first
+                residual_ref[rows, :] = (
+                    factor[2] * side + factor[3] * first + factor[4] * second
+                )
+
+
+def finish_sides(lines, right_side, w0_all, pieces):
+    width = 1024
+    full = pl.BlockSpec((64, width), lambda i: (0, i))
+    part = pl.BlockSpec((16, width), lambda i: (0, i))
+    shape = jax.ShapeDtypeStruct(right_side.shape, jnp.float32)
+    return pl.pallas_call(
+        finish_kernel,
+        grid=(right_side.shape[1] // width,),
+        out_shape=(shape, shape),
+        in_specs=[pl.BlockSpec(lines.shape, lambda i: (0, 0)), full, full] + [part] * 4,
+        out_specs=(full, full),
+        scratch_shapes=[pltpu.VMEM((5, 16, TILE), jnp.float32)],
+        compiler_params=pltpu.CompilerParams(vmem_limit_bytes=LIMIT),
+        name="finish_sides",
+    )(lines, right_side, w0_all, *pieces)
 
 
 def shards(right_side, points, active):
     column = lax.axis_index("blk")
     member = lax.axis_index("rep")
     sides = right_side.shape[0] // lax.axis_size("rep")
+    here = lax.dynamic_slice_in_dim(active, column, 1, 0)[0]
+    before = lax.dynamic_slice_in_dim(active, jnp.maximum(column - 1, 0), 1, 0)[0]
     place = jnp.stack([column, member]).astype(jnp.int32)
+    meta = jnp.concatenate([place, here, before])
 
     def neighbours(values):
         return from_behind(values, "blk", 1), from_behind(values, "blk", -1)
 
-    rows, cols, rank, box = sort_points(place, points, right_side)
+    rows, cols, rank, box = sort_points(lax.axis_size("blk"), meta, points, right_side)
     around = neighbours(rows)
-    fixed = (place, active, cols, box)
-    part, kept_own = apply_pairs(fixed, (rows,), (rows,))
-    w0, kept_cross = apply_pairs(fixed, around, around, part)
+    fixed = (cols, box)
+    part, *kept_own = apply_pairs(fixed, (rows,), (rows,))
+    w0, *kept_cross = apply_pairs(fixed, around, around, part)
     w0_around = neighbours(w0)
     w0_all = lax.all_gather(unsort(w0, rank), "rep", axis=0, tiled=True)
     (part,) = apply_pairs(fixed, (rows,), (w0,), kept=kept_own)
     w1, line = apply_pairs(fixed, around, w0_around, part, (rows, w0), kept_cross)
     line, mine = lax.optimization_barrier((line, unsort(w1, rank)))
-    w1_all = lax.all_gather(mine, "rep", axis=0, tiled=True)
+    pieces = [mine] + [exchange(mine, mask, "rep") for mask in (1, 3, 2)]
+    pieces = [pieces[k] for k in (0, 1, 3, 2)]
     lines = lax.all_to_all(line[:, 0:64], ("blk", "rep"), 0, 0, tiled=True)
-    members = lax.axis_size("rep")
-    sums = jnp.sum(lines.reshape(-1, members, 4, sides), axis=0)
-    sums = jnp.transpose(sums, (1, 0, 2)).reshape(4, members * sides)
-    s00, s01, s11, s12 = (sums[k] for k in range(4))
-    image_norm = shift * s00 + s01
-    alpha = s00 / image_norm
-    keep = s01 / image_norm
-    rr1 = alpha * alpha * (s11 - s01 * (s01 / s00))
-    beta = rr1 / s00
-    both = keep + beta
-    curved = both * both * s01 - 2.0 * both * alpha * s11 + alpha * alpha * s12
-    alpha1 = rr1 / (shift * rr1 * (1.0 + beta) + curved)
-    factors = jnp.stack(
-        [
-            (s00 + s01) / image_norm - noise_level * alpha1 * both,
-            noise_level * alpha1 * alpha,
-            keep - shift * alpha1 * both,
-            shift * alpha1 * alpha - alpha - alpha1 * both,
-            alpha1 * alpha,
-        ]
-    )
-    factor = factors[:, :, None]
-    posterior = factor[0] * right_side + factor[1] * w0_all
-    residual = factor[2] * right_side + factor[3] * w0_all + factor[4] * w1_all
-    return (posterior, residual)
+    return finish_sides(lines, right_side, w0_all, pieces)
 
 
 def solution(mesh):

time: 130 us -> 117 us (0.900)
  local copies, waits for them, and re-layouts: 14.8 us -> 6.83 us
  starting transfers between devices: 9.14 us -> 13.9 us
  other arithmetic: 4.47 us -> 0.08 us
  Pallas kernels: 53.6 us -> 50.2 us
  blocking collectives: 31.3 us -> 29.7 us
    unnamed x47 -> x28, local copies, waits for them, and re-layouts: 13.6 us -> 5.85 us
    pallas_call x4, Pallas kernels: 40.8 us -> 34.7 us  [apply_pairs(): pl.pallas_call(partial(apply_kernel, own, again), out_shape=out_shape, in...]
    ppermute x0 -> x3, starting transfers between devices: none -> 4.1 us  [exchange(): return lax.ppermute(values, axis, [(i, i ^ mask) for i in devices])]
    add x1 -> x0, other arithmetic: 3.23 us -> none  [shards(): residual = factor[2] * right_side + factor[3] * w0_all + factor[4] * w1_all]
    pallas_call x1 -> x2, Pallas kernels: 6.58 us -> 9.23 us  [the longest x1 6.69 us: sort_points(): pl.pallas_call(partial(sort_kernel, count), out_shape=(jax.ShapeDtypeStru...]
    all_to_all x1, blocking collectives: 31.3 us -> 29.7 us  [shards(): lines = lax.all_to_all(line[:, 0:64], ('blk', 'rep'), 0, 0, tiled=True)]
  transfers between devices with their start and end apart: 6 -> 8, of which waited for: 0 -> 0; matrix products, arithmetic and copies ran while one was open for 3% -> 0% of each run, Pallas kernels for 29% -> 27%
where the time goes in v4:
time: 117 us; the launch traced here: 115 us
  Pallas kernels  50.2 us (43%)
  blocking collectives  29.7 us (25%)
  between operations  14.3 us (12%)
  starting transfers between devices  13.9 us (12%)
  local copies, waits for them, and re-layouts  6.83 us (6%)
    pallas_call x4, Pallas kernels, apply_pairs(): pl.pallas_call(partial(apply_kernel, own, again), out_shape=out_shape, in...  34.7 us
    all_to_all x1, blocking collectives, shards(): lines = lax.all_to_all(line[:, 0:64], ('blk', 'rep'), 0, 0, tiled=True)  29.7 us
    ppermute x4, starting transfers between devices, from_behind(): return lax.ppermute(block, axis, route)  9.72 us
    pallas_call x1, Pallas kernels, sort_points(): pl.pallas_call(partial(sort_kernel, count), out_shape=(jax.ShapeDtypeStru...  6.69 us
    pallas_call x2, Pallas kernels, unsort(): pl.pallas_call(unsort_kernel, out_shape=jax.ShapeDtypeStruct(values.shape...  6.28 us
    unnamed x28, local copies, waits for them, and re-layouts  5.85 us
    ppermute x3, starting transfers between devices, exchange(): return lax.ppermute(values, axis, [(i, i ^ mask) for i in devices])  4.1 us
    pallas_call x1, Pallas kernels, finish_sides(): pl.pallas_call(finish_kernel, grid=(right_side.shape[1] // width,), out_s...  2.54 us
  transfers between devices with their start and end apart: 8, of which 0 were waited for; matrix products, arithmetic and copies ran while one was open for 0% of the time, Pallas kernels for 27%

profile of v4, /device:TPU:8, one launch (start us, length us, event | category | flops | bytes accessed | tf_op | source)
XLA Modules:
  0.0 115.0 jit_solution(4987057416225938128)
XLA Ops:
  7.2 0.0 all-gather.2.cloned.1.call-start
  7.2 1.0 dynamic-slice_reduce_fusion.1
  8.2 0.1 pad_add_fusion.meta_ref
  8.3 1.2 %copy-done = f32[64,4096]{1,0:T(8,128)S(1)} copy-done((f32[64,4096]{1,0:T(8,128)S(1)}, f32[64,4096]{1,0:T(8,128)}, u32[]{:S(2)}) %copy-start) | copy-done | bytes 1048600
  9.5 0.8 copy-done.13
  10.4 6.7 %sort_points.1 = (f32[24,4096]{1,0:T(8,128)S(1)}, f32[4096,128]{1,0:T(8,128)S(1)}, s32[8,4096]{1,0:T(8,128)S(1)}, f32[4,32,128]{2,1,0:T(8,128)S(1)}) custom-call(s32[12]{0:T(128)S(1)} %pad_add_fusion.meta_ref, f32[3,4096]{1,0:T(4,128)S(1)} %copy-done.13, f32[64,4096]{1,0:T(8,128)S(1)} %copy-done), custom_call_target="tpu_custom_call" | custom-call | tf_op jit(solution)/shard_map/sort_points/pallas_call | solution.py:160
  17.1 1.3 %collective-permute-start.1 = (f32[24,4096]{1,0:T(8,128)S(1)}, f32[24,4096]{1,0:T(8,128)S(1)}, u32[]{:S(2)}, u32[]{:S(2)}) collective-permute-start(f32[24,4096]{1,0:T(8,128)S(1)} %get-tuple-element.18.refs_2_.refs_3_.refs_7_), channel_id=1, source_target_pairs={{4,0},{8,4},{12,8},{16,12},{20,16},{24,20},{28,24},{32,28},{36,32}... | collective-permute-start | bytes 1179656 | tf_op jit(solution)/shard_map/ppermute | solution.py:36
  18.4 3.1 %collective-permute-start = (f32[24,4096]{1,0:T(8,128)S(1)}, f32[24,4096]{1,0:T(8,128)S(1)}, u32[]{:S(2)}, u32[]{:S(2)}) collective-permute-start(f32[24,4096]{1,0:T(8,128)S(1)} %get-tuple-element.18.refs_2_.refs_3_.refs_7_), channel_id=1, source_target_pairs={{0,4},{4,8},{8,12},{12,16},{16,20},{20,24},{24,28},{28,32},{32,36}... | collective-permute-start | bytes 1179656 | tf_op jit(solution)/shard_map/ppermute | solution.py:36
  21.4 15.4 %apply_own.1 = (f32[16,4096]{1,0:T(8,128)S(1)}, s32[32,128]{1,0:T(8,128)S(1)}, bf16[24,4,256,256]{3,2,1,0:T(8,128)(2,1)}) custom-call(f32[4096,128]{1,0:T(8,128)S(1)} %get-tuple-element.16.refs_0_, f32[4,32,128]{2,1,0:T(8,128)S(1)} %get-tuple-element.17.refs_1_, f32[24,4096]{1,0:T(8,128)S(1)} %get-tuple-element.18.refs_2_.refs_3_.refs_7_, ...), custom_call_target="tpu_custom_call" | custom-call | tf_op jit(solution)/shard_map/apply_own/pallas_call | solution.py:548
  36.9 0.0 collective-permute-done.1.refs_3_.refs_5_
  36.9 0.0 copy-start.4
  36.9 6.6 %apply_cross.1 = (f32[16,4096]{1,0:T(8,128)S(1)}, s32[32,128]{1,0:T(8,128)S(1)}, bf16[8,4,256,256]{3,2,1,0:T(8,128)(2,1)}) custom-call(f32[4096,128]{1,0:T(8,128)S(1)} %get-tuple-element.16.refs_0_, f32[4,32,128]{2,1,0:T(8,128)S(1)} %get-tuple-element.17.refs_1_, f32[24,4096]{1,0:T(8,128)S(1)} %collective-permute-done.refs_2_.refs_4_, ...), custom_call_target="tpu_custom_call" | custom-call | tf_op jit(solution)/shard_map/apply_cross/pallas_call | solution.py:548
  43.5 0.0 copy-start.2
  43.5 0.7 copy-done.2
  44.3 3.5 %unsort.3 = f32[16,4096]{1,0:T(8,128)} custom-call(f32[16,4096]{1,0:T(8,128)S(1)} %get-tuple-element.20.refs_3_.refs_8_.sorted_ref, s32[8,4096]{1,0:T(8,128)S(1)} %get-tuple-element.27.rank_ref), custom_call_target="tpu_custom_call" | custom-call | tf_op jit(solution)/shard_map/unsort/pallas_call | solution.py:200
  47.8 0.0 all-gather.2.cloned.1.call-update
  47.8 1.3 %collective-permute-start.3 = (f32[16,4096]{1,0:T(8,128)S(1)}, f32[16,4096]{1,0:T(8,128)S(1)}, u32[]{:S(2)}, u32[]{:S(2)}) collective-permute-start(f32[16,4096]{1,0:T(8,128)S(1)} %get-tuple-element.20.refs_3_.refs_8_.sorted_ref), channel_id=1, source_target_pairs={{4,0},{8,4},{12,8},{16,12},{20,16},{24,20},{28,24},{32,28},{36,32}... | collective-permute-start | bytes 786440 | tf_op jit(solution)/shard_map/ppermute | solution.py:36
  49.1 4.1 %collective-permute-start.2 = (f32[16,4096]{1,0:T(8,128)S(1)}, f32[16,4096]{1,0:T(8,128)S(1)}, u32[]{:S(2)}, u32[]{:S(2)}) collective-permute-start(f32[16,4096]{1,0:T(8,128)S(1)} %get-tuple-element.20.refs_3_.refs_8_.sorted_ref), channel_id=1, source_target_pairs={{0,4},{4,8},{8,12},{12,16},{16,20},{20,24},{24,28},{28,32},{32,36}... | collective-permute-start | bytes 786440 | tf_op jit(solution)/shard_map/ppermute | solution.py:36
  53.2 0.0 copy-start.3
  53.2 0.0 copy-start.5
  53.2 8.1 %again_own.1.refs_6_ = f32[16,4096]{1,0:T(8,128)S(1)} custom-call(f32[4096,128]{1,0:T(8,128)S(1)} %get-tuple-element.16.refs_0_, f32[4,32,128]{2,1,0:T(8,128)S(1)} %get-tuple-element.17.refs_1_, f32[24,4096]{1,0:T(8,128)S(1)} %get-tuple-element.18.refs_2_.refs_3_.refs_7_, f32[16,4096]{1,0:T(8,128)S(1)} %get-tuple-element.20.refs_3_.refs_8_.sorted_ref, ...), custom_call_target="tpu_custom_call" | custom-call | tf_op jit(solution)/shard_map/again_own/pallas_call | solution.py:548
  61.4 0.9 copy-done.7
  62.4 0.8 copy-done.9
  63.2 4.6 %again_cross.1 = (f32[16,4096]{1,0:T(8,128)S(1)}, f32[256,128]{1,0:T(8,128)S(1)}) custom-call(f32[4096,128]{1,0:T(8,128)S(1)} %get-tuple-element.16.refs_0_, f32[4,32,128]{2,1,0:T(8,128)S(1)} %copy-done.9, f32[24,4096]{1,0:T(8,128)S(1)} %copy-done.5, f32[24,4096]{1,0:T(8,128)S(1)} %copy-done.3, f32[16,4096]{1,0:T(8,128)S(1)} %collective-permute-done.2.refs_4_, ...), custom_call_target="tpu_custom_call" | custom-call | tf_op jit(solution)/shard_map/again_cross/pallas_call | solution.py:548
  67.8 2.8 %unsort.2.refs_0_ = f32[16,4096]{1,0:T(8,128)S(1)} custom-call(f32[16,4096]{1,0:T(8,128)S(1)} %get-tuple-element.26.sorted_ref, s32[8,4096]{1,0:T(8,128)S(1)} %copy-done.12), custom_call_target="tpu_custom_call" | custom-call | tf_op jit(solution)/shard_map/unsort/pallas_call | solution.py:200
  70.5 1.6 %collective-permute-start.6 = (f32[16,4096]{1,0:T(8,128)S(1)}, f32[16,4096]{1,0:T(8,128)S(1)}, u32[]{:S(2)}, u32[]{:S(2)}) collective-permute-start(f32[16,4096]{1,0:T(8,128)S(1)} %unsort.2.refs_0_), channel_id=1, source_target_pairs={{0,3},{1,2},{2,1},{3,0},{4,7},{5,6},{6,5},{7,4},{8,11},{9,10},{10,... | collective-permute-start | bytes 786440 | tf_op jit(solution)/shard_map/ppermute | solution.py:41
  72.1 1.6 %collective-permute-start.5 = (f32[16,4096]{1,0:T(8,128)S(1)}, f32[16,4096]{1,0:T(8,128)S(1)}, u32[]{:S(2)}, u32[]{:S(2)}) collective-permute-start(f32[16,4096]{1,0:T(8,128)S(1)} %unsort.2.refs_0_), channel_id=1, source_target_pairs={{0,2},{1,3},{2,0},{3,1},{4,6},{5,7},{6,4},{7,5},{8,10},{9,11},{10,... | collective-permute-start | bytes 786440 | tf_op jit(solution)/shard_map/ppermute | solution.py:41
  73.8 0.9 collective-permute-start.4
  74.6 29.7 %all_to_all.11 = f32[256,1,64]{2,1,0:T(1,128)S(1)} all-to-all(f32[256,1,64]{2,1,0:T(1,128)S(1)} %bitcast.8), channel_id=1, replica_groups=mesh['blk'=64,'rep'=4] {'blk','rep'}, dimensions={0} | all-to-all | bytes 131072 | tf_op jit(solution)/shard_map/all_to_all | solution.py:656
  104.3 0.0 all-gather.2.cloned.1.call-done.w0_ref
  104.4 1.2 %copy-done.10 = f32[64,4096]{1,0:T(8,128)S(1)} copy-done((f32[64,4096]{1,0:T(8,128)S(1)}, f32[64,4096]{1,0:T(8,128)}, u32[]{:S(2)}) %copy-start.10) | copy-done | bytes 1048600
  105.6 2.5 %finish_sides.1 = (f32[64,4096]{1,0:T(8,128)}, f32[64,4096]{1,0:T(8,128)}) custom-call(f32[256,64]{1,0:T(8,128)S(1)} %bitcast.7, f32[64,4096]{1,0:T(8,128)S(1)} %copy-done.1, f32[64,4096]{1,0:T(8,128)S(1)} %copy-done.10, f32[16,4096]{1,0:T(8,128)S(1)} %unsort.2.refs_0_, f32[16,4096]{1,0:T(8,128)S(1)} %collective-permute-done.4.refs_1_, ...), custom_call_target="tpu_custom_call" | custom-call | tf_op jit(solution)/shard_map/finish_sides/pallas_call | solution.py:620
  (24 shorter events, 0.1 us)
Async XLA Ops:
  7.2 97.2 %all-gather.2.cloned.1.call-start = ((), (), s32[]{:S(2)}) async-start(), calls=%async_computation.1 | async-start | bytes 1310720 | tf_op jit(solution)/shard_map/all_gather | solution.py:650
  8.3 1.2 %copy-start = (f32[64,4096]{1,0:T(8,128)S(1)}, f32[64,4096]{1,0:T(8,128)}, u32[]{:S(2)}) copy-start(f32[64,4096]{1,0:T(8,128)} %sides_ref.3) | copy-start | bytes 3145732
  9.5 0.8 copy-start.13
  17.1 27.2 %copy-start.11 = (s32[8,4096]{1,0:T(8,128)}, s32[8,4096]{1,0:T(8,128)S(1)}, u32[]{:S(2)}) copy-start(s32[8,4096]{1,0:T(8,128)S(1)} %get-tuple-element.27.rank_ref) | copy-start | bytes 393220
  17.1 44.3 %copy-start.8 = (f32[4,32,128]{2,1,0:T(8,128)}, f32[4,32,128]{2,1,0:T(8,128)S(1)}, u32[]{:S(2)}) copy-start(f32[4,32,128]{2,1,0:T(8,128)S(1)} %get-tuple-element.17.refs_1_) | copy-start | bytes 196612
  17.1 19.8 %collective-permute-start.1 = (f32[24,4096]{1,0:T(8,128)S(1)}, f32[24,4096]{1,0:T(8,128)S(1)}, u32[]{:S(2)}, u32[]{:S(2)}) collective-permute-start(f32[24,4096]{1,0:T(8,128)S(1)} %get-tuple-element.18.refs_2_.refs_3_.refs_7_), channel_id=1, source_target_pairs={{4,0},{8,4},{12,8},{16,12},{20,16},{24,20},{28,24},{32,28},{36,32}... | collective-permute-start | bytes 1179656 | tf_op jit(solution)/shard_map/ppermute | solution.py:36
  18.4 18.5 %collective-permute-start = (f32[24,4096]{1,0:T(8,128)S(1)}, f32[24,4096]{1,0:T(8,128)S(1)}, u32[]{:S(2)}, u32[]{:S(2)}) collective-permute-start(f32[24,4096]{1,0:T(8,128)S(1)} %get-tuple-element.18.refs_2_.refs_3_.refs_7_), channel_id=1, source_target_pairs={{0,4},{4,8},{8,12},{12,16},{16,20},{20,24},{24,28},{28,32},{32,36}... | collective-permute-start | bytes 1179656 | tf_op jit(solution)/shard_map/ppermute | solution.py:36
  36.9 6.6 %copy-start.4 = (f32[24,4096]{1,0:T(8,128)}, f32[24,4096]{1,0:T(8,128)S(1)}, u32[]{:S(2)}) copy-start(f32[24,4096]{1,0:T(8,128)S(1)} %collective-permute-done.refs_2_.refs_4_) | copy-start | bytes 1179652
  43.5 0.7 copy-start.2
  44.3 17.1 %copy-start.6 = (f32[16,4096]{1,0:T(8,128)}, f32[16,4096]{1,0:T(8,128)S(1)}, u32[]{:S(2)}) copy-start(f32[16,4096]{1,0:T(8,128)S(1)} %get-tuple-element.20.refs_3_.refs_8_.sorted_ref) | copy-start | bytes 786436
  47.8 13.6 %collective-permute-start.3 = (f32[16,4096]{1,0:T(8,128)S(1)}, f32[16,4096]{1,0:T(8,128)S(1)}, u32[]{:S(2)}, u32[]{:S(2)}) collective-permute-start(f32[16,4096]{1,0:T(8,128)S(1)} %get-tuple-element.20.refs_3_.refs_8_.sorted_ref), channel_id=1, source_target_pairs={{4,0},{8,4},{12,8},{16,12},{20,16},{24,20},{28,24},{32,28},{36,32}... | collective-permute-start | bytes 786440 | tf_op jit(solution)/shard_map/ppermute | solution.py:36
  49.1 12.3 %collective-permute-start.2 = (f32[16,4096]{1,0:T(8,128)S(1)}, f32[16,4096]{1,0:T(8,128)S(1)}, u32[]{:S(2)}, u32[]{:S(2)}) collective-permute-start(f32[16,4096]{1,0:T(8,128)S(1)} %get-tuple-element.20.refs_3_.refs_8_.sorted_ref), channel_id=1, source_target_pairs={{0,4},{4,8},{8,12},{12,16},{16,20},{20,24},{24,28},{28,32},{32,36}... | collective-permute-start | bytes 786440 | tf_op jit(solution)/shard_map/ppermute | solution.py:36
  53.2 8.2 %copy-start.3 = (f32[24,4096]{1,0:T(8,128)S(1)}, f32[24,4096]{1,0:T(8,128)}, u32[]{:S(2)}) copy-start(f32[24,4096]{1,0:T(8,128)} %copy-done.2) | copy-start | bytes 1179652
  53.2 8.2 %copy-start.5 = (f32[24,4096]{1,0:T(8,128)S(1)}, f32[24,4096]{1,0:T(8,128)}, u32[]{:S(2)}) copy-start(f32[24,4096]{1,0:T(8,128)} %copy-done.4) | copy-start | bytes 1179652
  61.4 1.0 copy-start.7
  62.4 0.8 copy-start.9
  63.2 4.6 %copy-start.12 = (s32[8,4096]{1,0:T(8,128)S(1)}, s32[8,4096]{1,0:T(8,128)}, u32[]{:S(2)}) copy-start(s32[8,4096]{1,0:T(8,128)} %copy-done.11) | copy-start | bytes 393220
  63.2 41.1 %copy-start.1 = (f32[64,4096]{1,0:T(8,128)S(1)}, f32[64,4096]{1,0:T(8,128)}, u32[]{:S(2)}) copy-start(f32[64,4096]{1,0:T(8,128)} %sides_ref.3) | copy-start | bytes 3145732
  70.5 33.8 %collective-permute-start.6 = (f32[16,4096]{1,0:T(8,128)S(1)}, f32[16,4096]{1,0:T(8,128)S(1)}, u32[]{:S(2)}, u32[]{:S(2)}) collective-permute-start(f32[16,4096]{1,0:T(8,128)S(1)} %unsort.2.refs_0_), channel_id=1, source_target_pairs={{0,3},{1,2},{2,1},{3,0},{4,7},{5,6},{6,5},{7,4},{8,11},{9,10},{10,... | collective-permute-start | bytes 786440 | tf_op jit(solution)/shard_map/ppermute | solution.py:41
  72.1 32.2 %collective-permute-start.5 = (f32[16,4096]{1,0:T(8,128)S(1)}, f32[16,4096]{1,0:T(8,128)S(1)}, u32[]{:S(2)}, u32[]{:S(2)}) collective-permute-start(f32[16,4096]{1,0:T(8,128)S(1)} %unsort.2.refs_0_), channel_id=1, source_target_pairs={{0,2},{1,3},{2,0},{3,1},{4,6},{5,7},{6,4},{7,5},{8,10},{9,11},{10,... | collective-permute-start | bytes 786440 | tf_op jit(solution)/shard_map/ppermute | solution.py:41
  73.8 30.5 %collective-permute-start.4 = (f32[16,4096]{1,0:T(8,128)S(1)}, f32[16,4096]{1,0:T(8,128)S(1)}, u32[]{:S(2)}, u32[]{:S(2)}) collective-permute-start(f32[16,4096]{1,0:T(8,128)S(1)} %unsort.2.refs_0_), channel_id=1, source_target_pairs={{0,1},{1,0},{2,3},{3,2},{4,5},{5,4},{6,7},{7,6},{8,9},{9,8},{10,11... | collective-permute-start | bytes 786440 | tf_op jit(solution)/shard_map/ppermute | solution.py:41
  104.4 1.2 %copy-start.10 = (f32[64,4096]{1,0:T(8,128)S(1)}, f32[64,4096]{1,0:T(8,128)}, u32[]{:S(2)}) copy-start(f32[64,4096]{1,0:T(8,128)} %all-gather.2.cloned.1.call-done.w0_ref) | copy-start | bytes 3145732
Sparse Core Ops, SparseCore 0:
  47.9 37.0 all-gather.1

commit v5 on v4

--- a/solution.py
+++ b/solution.py
@@ -567,8 +567,8 @@
     )(*operands)
 
 
-def finish_kernel(lines_ref, sides_ref, w0_ref, *refs):
-    pieces, (posterior_ref, residual_ref, factor_ref) = refs[:4], refs[4:]
+def finish_kernel(lines_ref, sides_ref, *refs):
+    posterior_ref, residual_ref, factor_ref = refs[8:]
 
     @pl.when(pl.program_id(0) == 0)
     def _():
@@ -604,15 +604,15 @@
                 rows = slice(16 * q, 16 * q + 16)
                 factor = [factor_ref[k, :, q : q + 1] for k in range(5)]
                 side = sides_ref[rows, :]
-                first = w0_ref[rows, :]
-                second = pieces[q ^ member][...]
+                first = refs[q ^ member][...]
+                second = refs[4 + (q ^ member)][...]
                 posterior_ref[rows, :] = factor[0] * side + factor[1] * first
                 residual_ref[rows, :] = (
                     factor[2] * side + factor[3] * first + factor[4] * second
                 )
 
 
-def finish_sides(lines, right_side, w0_all, pieces):
+def finish_sides(lines, right_side, pieces):
     width = 1024
     full = pl.BlockSpec((64, width), lambda i: (0, i))
     part = pl.BlockSpec((16, width), lambda i: (0, i))
@@ -621,12 +621,12 @@
         finish_kernel,
         grid=(right_side.shape[1] // width,),
         out_shape=(shape, shape),
-        in_specs=[pl.BlockSpec(lines.shape, lambda i: (0, 0)), full, full] + [part] * 4,
+        in_specs=[pl.BlockSpec(lines.shape, lambda i: (0, 0)), full] + [part] * 8,
         out_specs=(full, full),
         scratch_shapes=[pltpu.VMEM((5, 16, TILE), jnp.float32)],
         compiler_params=pltpu.CompilerParams(vmem_limit_bytes=LIMIT),
         name="finish_sides",
-    )(lines, right_side, w0_all, *pieces)
+    )(lines, right_side, *pieces)
 
 
 def shards(right_side, points, active):
@@ -638,6 +638,9 @@
     place = jnp.stack([column, member]).astype(jnp.int32)
     meta = jnp.concatenate([place, here, before])
 
+    def spread(values):
+        return [values] + [exchange(values, mask, "rep") for mask in (1, 2, 3)]
+
     def neighbours(values):
         return from_behind(values, "blk", 1), from_behind(values, "blk", -1)
 
@@ -647,14 +650,13 @@
     part, *kept_own = apply_pairs(fixed, (rows,), (rows,))
     w0, *kept_cross = apply_pairs(fixed, around, around, part)
     w0_around = neighbours(w0)
-    w0_all = lax.all_gather(unsort(w0, rank), "rep", axis=0, tiled=True)
+    w0_pieces = spread(unsort(w0, rank))
     (part,) = apply_pairs(fixed, (rows,), (w0,), kept=kept_own)
     w1, line = apply_pairs(fixed, around, w0_around, part, (rows, w0), kept_cross)
     line, mine = lax.optimization_barrier((line, unsort(w1, rank)))
-    pieces = [mine] + [exchange(mine, mask, "rep") for mask in (1, 3, 2)]
-    pieces = [pieces[k] for k in (0, 1, 3, 2)]
+    w1_pieces = spread(mine)
     lines = lax.all_to_all(line[:, 0:64], ("blk", "rep"), 0, 0, tiled=True)
-    return finish_sides(lines, right_side, w0_all, pieces)
+    return finish_sides(lines, right_side, w0_pieces + w1_pieces)
 
 
 def solution(mesh):

time: 117 us -> 103 us (0.88)
  blocking collectives: 29.7 us -> 0 us
  starting transfers between devices: 13.9 us -> 34.6 us
  between operations: 14.3 us -> 0.79 us
  waiting for transfers between devices: 0.06 us -> 12.3 us
  local copies, waits for them, and re-layouts: 6.83 us -> 3.06 us
    all_to_all x1 -> x0, blocking collectives: 29.7 us -> none  [shards(): lines = lax.all_to_all(line[:, 0:64], ('blk', 'rep'), 0, 0, tiled=True)]
    all_to_all x0 -> x1, starting transfers between devices: none -> 16.7 us  [shards(): lines = lax.all_to_all(line[:, 0:64], ('blk', 'rep'), 0, 0, tiled=True)]
    all_to_all x0 -> x1, waiting for transfers between devices: none -> 12.2 us  [shards(): lines = lax.all_to_all(line[:, 0:64], ('blk', 'rep'), 0, 0, tiled=True)]
    ppermute x3 -> x6, starting transfers between devices: 4.1 us -> 8.22 us  [exchange(): return lax.ppermute(values, axis, [(i, i ^ mask) for i in devices])]
    unnamed x28 -> x6, local copies, waits for them, and re-layouts: 5.85 us -> 2.08 us
  transfers between devices with their start and end apart: 8 -> 11, of which waited for: 0 -> 1; matrix products, arithmetic and copies ran while one was open for 0% -> 0% of each run, Pallas kernels for 27% -> 34%
where the time goes in v5:
time: 103 us; the launch traced here: 101 us
  Pallas kernels  50.2 us (49%)
  starting transfers between devices  34.6 us (34%)
  waiting for transfers between devices  12.3 us (12%)
  local copies, waits for them, and re-layouts  3.06 us (3%)
    pallas_call x4, Pallas kernels, apply_pairs(): pl.pallas_call(partial(apply_kernel, own, again), out_shape=out_shape, in...  35.3 us
    all_to_all x1, starting transfers between devices, shards(): lines = lax.all_to_all(line[:, 0:64], ('blk', 'rep'), 0, 0, tiled=True)  16.7 us
    all_to_all x1, waiting for transfers between devices, shards(): lines = lax.all_to_all(line[:, 0:64], ('blk', 'rep'), 0, 0, tiled=True)  12.2 us
    ppermute x4, starting transfers between devices, from_behind(): return lax.ppermute(block, axis, route)  9.7 us
    ppermute x6, starting transfers between devices, exchange(): return lax.ppermute(values, axis, [(i, i ^ mask) for i in devices])  8.22 us
    pallas_call x1, Pallas kernels, sort_points(): pl.pallas_call(partial(sort_kernel, count), out_shape=(jax.ShapeDtypeStru...  6.7 us
    pallas_call x2, Pallas kernels, unsort(): pl.pallas_call(unsort_kernel, out_shape=jax.ShapeDtypeStruct(values.shape...  5.55 us
    pallas_call x1, Pallas kernels, finish_sides(): pl.pallas_call(finish_kernel, grid=(right_side.shape[1] // width,), out_s...  2.64 us
  transfers between devices with their start and end apart: 11, of which 1 were waited for; matrix products, arithmetic and copies ran while one was open for 0% of the time, Pallas kernels for 34%

profile of v5, /device:TPU:8, one launch (start us, length us, event | category | flops | bytes accessed | tf_op | source)
XLA Modules:
  0.0 101.0 jit_solution(3379563286005356068)
XLA Ops:
  0.6 1.0 dynamic-slice_reduce_fusion.1
  1.6 0.1 pad_add_fusion.meta_ref
  1.7 1.2 %copy-done = f32[64,4096]{1,0:T(8,128)S(1)} copy-done((f32[64,4096]{1,0:T(8,128)S(1)}, f32[64,4096]{1,0:T(8,128)}, u32[]{:S(2)}) %copy-start) | copy-done | bytes 1048600
  2.9 0.8 copy-done.2
  3.8 6.7 %sort_points.1 = (f32[24,4096]{1,0:T(8,128)S(1)}, f32[4096,128]{1,0:T(8,128)S(1)}, s32[8,4096]{1,0:T(8,128)S(1)}, f32[4,32,128]{2,1,0:T(8,128)S(1)}) custom-call(s32[12]{0:T(128)S(1)} %pad_add_fusion.meta_ref, f32[3,4096]{1,0:T(4,128)S(1)} %copy-done.2, f32[64,4096]{1,0:T(8,128)S(1)} %copy-done), custom_call_target="tpu_custom_call" | custom-call | tf_op jit(solution)/shard_map/sort_points/pallas_call | solution.py:160
  10.5 1.3 %collective-permute-start.1 = (f32[24,4096]{1,0:T(8,128)S(1)}, f32[24,4096]{1,0:T(8,128)S(1)}, u32[]{:S(2)}, u32[]{:S(2)}) collective-permute-start(f32[24,4096]{1,0:T(8,128)S(1)} %get-tuple-element.18.refs_2_.refs_3_.refs_7_), channel_id=1, source_target_pairs={{4,0},{8,4},{12,8},{16,12},{20,16},{24,20},{28,24},{32,28},{36,32}... | collective-permute-start | bytes 1179656 | tf_op jit(solution)/shard_map/ppermute | solution.py:36
  11.8 3.1 %collective-permute-start = (f32[24,4096]{1,0:T(8,128)S(1)}, f32[24,4096]{1,0:T(8,128)S(1)}, u32[]{:S(2)}, u32[]{:S(2)}) collective-permute-start(f32[24,4096]{1,0:T(8,128)S(1)} %get-tuple-element.18.refs_2_.refs_3_.refs_7_), channel_id=1, source_target_pairs={{0,4},{4,8},{8,12},{12,16},{16,20},{20,24},{24,28},{28,32},{32,36}... | collective-permute-start | bytes 1179656 | tf_op jit(solution)/shard_map/ppermute | solution.py:36
  14.8 15.4 %apply_own.1 = (f32[16,4096]{1,0:T(8,128)S(1)}, s32[32,128]{1,0:T(8,128)S(1)}, bf16[24,4,256,256]{3,2,1,0:T(8,128)(2,1)}) custom-call(f32[4096,128]{1,0:T(8,128)S(1)} %get-tuple-element.16.refs_0_, f32[4,32,128]{2,1,0:T(8,128)S(1)} %get-tuple-element.17.refs_1_, f32[24,4096]{1,0:T(8,128)S(1)} %get-tuple-element.18.refs_2_.refs_3_.refs_7_, ...), custom_call_target="tpu_custom_call" | custom-call | tf_op jit(solution)/shard_map/apply_own/pallas_call | solution.py:548
  30.3 0.0 collective-permute-done.1.refs_3_.refs_5_
  30.3 0.0 collective-permute-done.refs_2_.refs_4_
  30.3 6.5 %apply_cross.1 = (f32[16,4096]{1,0:T(8,128)S(1)}, s32[32,128]{1,0:T(8,128)S(1)}, bf16[8,4,256,256]{3,2,1,0:T(8,128)(2,1)}) custom-call(f32[4096,128]{1,0:T(8,128)S(1)} %get-tuple-element.16.refs_0_, f32[4,32,128]{2,1,0:T(8,128)S(1)} %get-tuple-element.17.refs_1_, f32[24,4096]{1,0:T(8,128)S(1)} %collective-permute-done.refs_2_.refs_4_, ...), custom_call_target="tpu_custom_call" | custom-call | tf_op jit(solution)/shard_map/apply_cross/pallas_call | solution.py:548
  36.8 1.3 %collective-permute-start.3 = (f32[16,4096]{1,0:T(8,128)S(1)}, f32[16,4096]{1,0:T(8,128)S(1)}, u32[]{:S(2)}, u32[]{:S(2)}) collective-permute-start(f32[16,4096]{1,0:T(8,128)S(1)} %get-tuple-element.20.refs_3_.refs_8_.sorted_ref), channel_id=1, source_target_pairs={{4,0},{8,4},{12,8},{16,12},{20,16},{24,20},{28,24},{32,28},{36,32}... | collective-permute-start | bytes 786440 | tf_op jit(solution)/shard_map/ppermute | solution.py:36
  38.1 4.1 %collective-permute-start.2 = (f32[16,4096]{1,0:T(8,128)S(1)}, f32[16,4096]{1,0:T(8,128)S(1)}, u32[]{:S(2)}, u32[]{:S(2)}) collective-permute-start(f32[16,4096]{1,0:T(8,128)S(1)} %get-tuple-element.20.refs_3_.refs_8_.sorted_ref), channel_id=1, source_target_pairs={{0,4},{4,8},{8,12},{12,16},{16,20},{20,24},{24,28},{28,32},{32,36}... | collective-permute-start | bytes 786440 | tf_op jit(solution)/shard_map/ppermute | solution.py:36
  42.2 2.8 %unsort.3.refs_0_ = f32[16,4096]{1,0:T(8,128)S(1)} custom-call(f32[16,4096]{1,0:T(8,128)S(1)} %get-tuple-element.20.refs_3_.refs_8_.sorted_ref, s32[8,4096]{1,0:T(8,128)S(1)} %get-tuple-element.27.rank_ref), custom_call_target="tpu_custom_call" | custom-call | tf_op jit(solution)/shard_map/unsort/pallas_call | solution.py:200
  45.0 1.6 %collective-permute-start.6 = (f32[16,4096]{1,0:T(8,128)S(1)}, f32[16,4096]{1,0:T(8,128)S(1)}, u32[]{:S(2)}, u32[]{:S(2)}) collective-permute-start(f32[16,4096]{1,0:T(8,128)S(1)} %unsort.3.refs_0_), channel_id=1, source_target_pairs={{0,3},{1,2},{2,1},{3,0},{4,7},{5,6},{6,5},{7,4},{8,11},{9,10},{10,... | collective-permute-start | bytes 786440 | tf_op jit(solution)/shard_map/ppermute | solution.py:41
  46.6 1.6 %collective-permute-start.5 = (f32[16,4096]{1,0:T(8,128)S(1)}, f32[16,4096]{1,0:T(8,128)S(1)}, u32[]{:S(2)}, u32[]{:S(2)}) collective-permute-start(f32[16,4096]{1,0:T(8,128)S(1)} %unsort.3.refs_0_), channel_id=1, source_target_pairs={{0,2},{1,3},{2,0},{3,1},{4,6},{5,7},{6,4},{7,5},{8,10},{9,11},{10,... | collective-permute-start | bytes 786440 | tf_op jit(solution)/shard_map/ppermute | solution.py:41
  48.2 0.9 collective-permute-start.4
  49.1 8.3 %again_own.1.refs_6_ = f32[16,4096]{1,0:T(8,128)S(1)} custom-call(f32[4096,128]{1,0:T(8,128)S(1)} %get-tuple-element.16.refs_0_, f32[4,32,128]{2,1,0:T(8,128)S(1)} %get-tuple-element.17.refs_1_, f32[24,4096]{1,0:T(8,128)S(1)} %get-tuple-element.18.refs_2_.refs_3_.refs_7_, f32[16,4096]{1,0:T(8,128)S(1)} %get-tuple-element.20.refs_3_.refs_8_.sorted_ref, ...), custom_call_target="tpu_custom_call" | custom-call | tf_op jit(solution)/shard_map/again_own/pallas_call | solution.py:548
  57.4 0.0 collective-permute-done.3.refs_5_
  57.4 0.0 copy-start.1
  57.5 5.0 %again_cross.1 = (f32[16,4096]{1,0:T(8,128)S(1)}, f32[256,128]{1,0:T(8,128)}) custom-call(f32[4096,128]{1,0:T(8,128)S(1)} %get-tuple-element.16.refs_0_, f32[4,32,128]{2,1,0:T(8,128)S(1)} %get-tuple-element.17.refs_1_, f32[24,4096]{1,0:T(8,128)S(1)} %collective-permute-done.refs_2_.refs_4_, f32[24,4096]{1,0:T(8,128)S(1)} %collective-permute-done.1.refs_3_.refs_5_, ...), custom_call_target="tpu_custom_call" | custom-call | tf_op jit(solution)/shard_map/again_cross/pallas_call | solution.py:548
  62.5 2.8 %unsort.2.refs_4_ = f32[16,4096]{1,0:T(8,128)S(1)} custom-call(f32[16,4096]{1,0:T(8,128)S(1)} %get-tuple-element.26.sorted_ref, s32[8,4096]{1,0:T(8,128)S(1)} %get-tuple-element.27.rank_ref), custom_call_target="tpu_custom_call" | custom-call | tf_op jit(solution)/shard_map/unsort/pallas_call | solution.py:200
  65.3 1.6 %collective-permute-start.9 = (f32[16,4096]{1,0:T(8,128)S(1)}, f32[16,4096]{1,0:T(8,128)S(1)}, u32[]{:S(2)}, u32[]{:S(2)}) collective-permute-start(f32[16,4096]{1,0:T(8,128)S(1)} %unsort.2.refs_4_), channel_id=1, source_target_pairs={{0,3},{1,2},{2,1},{3,0},{4,7},{5,6},{6,5},{7,4},{8,11},{9,10},{10,... | collective-permute-start | bytes 786440 | tf_op jit(solution)/shard_map/ppermute | solution.py:41
  66.9 1.7 %collective-permute-start.8 = (f32[16,4096]{1,0:T(8,128)S(1)}, f32[16,4096]{1,0:T(8,128)S(1)}, u32[]{:S(2)}, u32[]{:S(2)}) collective-permute-start(f32[16,4096]{1,0:T(8,128)S(1)} %unsort.2.refs_4_), channel_id=1, source_target_pairs={{0,2},{1,3},{2,0},{3,1},{4,6},{5,7},{6,4},{7,5},{8,10},{9,11},{10,... | collective-permute-start | bytes 786440 | tf_op jit(solution)/shard_map/ppermute | solution.py:41
  68.5 0.0 collective-permute-done.6.refs_3_
  68.5 0.8 collective-permute-start.7
  69.4 16.7 %all-to-all-start = ((f32[256,1,64]{2,1,0:T(1,128)}), f32[256,1,64]{2,1,0:T(1,128)S(1)}, u32[]{:S(2)}, u32[]{:S(2)}) async-start(f32[256,1,64]{2,1,0:T(1,128)} %bitcast.3), calls=%async_computation | async-start | bytes 262144 | tf_op jit(solution)/shard_map/all_to_all | solution.py:658
  86.1 0.0 collective-permute-done.5.refs_2_
  86.1 12.2 %all-to-all-done = f32[256,1,64]{2,1,0:T(1,128)S(1)} async-done(((f32[256,1,64]{2,1,0:T(1,128)}), f32[256,1,64]{2,1,0:T(1,128)S(1)}, u32[]{:S(2)}, u32[]{:S(2)}) %all-to-all-start) | async-done | bytes 65568 | tf_op jit(solution)/shard_map/all_to_all | solution.py:658
  98.3 0.0 collective-permute-done.8.refs_6_
  98.3 0.0 collective-permute-done.7.refs_5_
  98.3 2.6 %finish_sides.1 = (f32[64,4096]{1,0:T(8,128)}, f32[64,4096]{1,0:T(8,128)}) custom-call(f32[256,64]{1,0:T(8,128)S(1)} %bitcast.7, f32[64,4096]{1,0:T(8,128)S(1)} %copy-done.1, f32[16,4096]{1,0:T(8,128)S(1)} %unsort.3.refs_0_, f32[16,4096]{1,0:T(8,128)S(1)} %collective-permute-done.4.refs_1_, f32[16,4096]{1,0:T(8,128)S(1)} %collective-permute-done.5.refs_2_, ...), custom_call_target="tpu_custom_call" | custom-call | tf_op jit(solution)/shard_map/finish_sides/pallas_call | solution.py:620
  (6 shorter events, 0.0 us)
Async XLA Ops:
  1.7 1.2 %copy-start = (f32[64,4096]{1,0:T(8,128)S(1)}, f32[64,4096]{1,0:T(8,128)}, u32[]{:S(2)}) copy-start(f32[64,4096]{1,0:T(8,128)} %sides_ref.3) | copy-start | bytes 3145732
  2.9 0.8 copy-start.2
  10.5 19.8 %collective-permute-start.1 = (f32[24,4096]{1,0:T(8,128)S(1)}, f32[24,4096]{1,0:T(8,128)S(1)}, u32[]{:S(2)}, u32[]{:S(2)}) collective-permute-start(f32[24,4096]{1,0:T(8,128)S(1)} %get-tuple-element.18.refs_2_.refs_3_.refs_7_), channel_id=1, source_target_pairs={{4,0},{8,4},{12,8},{16,12},{20,16},{24,20},{28,24},{32,28},{36,32}... | collective-permute-start | bytes 1179656 | tf_op jit(solution)/shard_map/ppermute | solution.py:36
  11.8 18.5 %collective-permute-start = (f32[24,4096]{1,0:T(8,128)S(1)}, f32[24,4096]{1,0:T(8,128)S(1)}, u32[]{:S(2)}, u32[]{:S(2)}) collective-permute-start(f32[24,4096]{1,0:T(8,128)S(1)} %get-tuple-element.18.refs_2_.refs_3_.refs_7_), channel_id=1, source_target_pairs={{0,4},{4,8},{8,12},{12,16},{16,20},{20,24},{24,28},{28,32},{32,36}... | collective-permute-start | bytes 1179656 | tf_op jit(solution)/shard_map/ppermute | solution.py:36
  36.8 20.6 %collective-permute-start.3 = (f32[16,4096]{1,0:T(8,128)S(1)}, f32[16,4096]{1,0:T(8,128)S(1)}, u32[]{:S(2)}, u32[]{:S(2)}) collective-permute-start(f32[16,4096]{1,0:T(8,128)S(1)} %get-tuple-element.20.refs_3_.refs_8_.sorted_ref), channel_id=1, source_target_pairs={{4,0},{8,4},{12,8},{16,12},{20,16},{24,20},{28,24},{32,28},{36,32}... | collective-permute-start | bytes 786440 | tf_op jit(solution)/shard_map/ppermute | solution.py:36
  38.1 19.3 %collective-permute-start.2 = (f32[16,4096]{1,0:T(8,128)S(1)}, f32[16,4096]{1,0:T(8,128)S(1)}, u32[]{:S(2)}, u32[]{:S(2)}) collective-permute-start(f32[16,4096]{1,0:T(8,128)S(1)} %get-tuple-element.20.refs_3_.refs_8_.sorted_ref), channel_id=1, source_target_pairs={{0,4},{4,8},{8,12},{12,16},{16,20},{20,24},{24,28},{28,32},{32,36}... | collective-permute-start | bytes 786440 | tf_op jit(solution)/shard_map/ppermute | solution.py:36
  45.0 23.5 %collective-permute-start.6 = (f32[16,4096]{1,0:T(8,128)S(1)}, f32[16,4096]{1,0:T(8,128)S(1)}, u32[]{:S(2)}, u32[]{:S(2)}) collective-permute-start(f32[16,4096]{1,0:T(8,128)S(1)} %unsort.3.refs_0_), channel_id=1, source_target_pairs={{0,3},{1,2},{2,1},{3,0},{4,7},{5,6},{6,5},{7,4},{8,11},{9,10},{10,... | collective-permute-start | bytes 786440 | tf_op jit(solution)/shard_map/ppermute | solution.py:41
  46.6 39.5 %collective-permute-start.5 = (f32[16,4096]{1,0:T(8,128)S(1)}, f32[16,4096]{1,0:T(8,128)S(1)}, u32[]{:S(2)}, u32[]{:S(2)}) collective-permute-start(f32[16,4096]{1,0:T(8,128)S(1)} %unsort.3.refs_0_), channel_id=1, source_target_pairs={{0,2},{1,3},{2,0},{3,1},{4,6},{5,7},{6,4},{7,5},{8,10},{9,11},{10,... | collective-permute-start | bytes 786440 | tf_op jit(solution)/shard_map/ppermute | solution.py:41
  48.2 37.9 %collective-permute-start.4 = (f32[16,4096]{1,0:T(8,128)S(1)}, f32[16,4096]{1,0:T(8,128)S(1)}, u32[]{:S(2)}, u32[]{:S(2)}) collective-permute-start(f32[16,4096]{1,0:T(8,128)S(1)} %unsort.3.refs_0_), channel_id=1, source_target_pairs={{0,1},{1,0},{2,3},{3,2},{4,5},{5,4},{6,7},{7,6},{8,9},{9,8},{10,11... | collective-permute-start | bytes 786440 | tf_op jit(solution)/shard_map/ppermute | solution.py:41
  57.4 40.9 %copy-start.1 = (f32[64,4096]{1,0:T(8,128)S(1)}, f32[64,4096]{1,0:T(8,128)}, u32[]{:S(2)}) copy-start(f32[64,4096]{1,0:T(8,128)} %sides_ref.3) | copy-start | bytes 3145732
  65.3 33.1 %collective-permute-start.9 = (f32[16,4096]{1,0:T(8,128)S(1)}, f32[16,4096]{1,0:T(8,128)S(1)}, u32[]{:S(2)}, u32[]{:S(2)}) collective-permute-start(f32[16,4096]{1,0:T(8,128)S(1)} %unsort.2.refs_4_), channel_id=1, source_target_pairs={{0,3},{1,2},{2,1},{3,0},{4,7},{5,6},{6,5},{7,4},{8,11},{9,10},{10,... | collective-permute-start | bytes 786440 | tf_op jit(solution)/shard_map/ppermute | solution.py:41
  66.9 31.5 %collective-permute-start.8 = (f32[16,4096]{1,0:T(8,128)S(1)}, f32[16,4096]{1,0:T(8,128)S(1)}, u32[]{:S(2)}, u32[]{:S(2)}) collective-permute-start(f32[16,4096]{1,0:T(8,128)S(1)} %unsort.2.refs_4_), channel_id=1, source_target_pairs={{0,2},{1,3},{2,0},{3,1},{4,6},{5,7},{6,4},{7,5},{8,10},{9,11},{10,... | collective-permute-start | bytes 786440 | tf_op jit(solution)/shard_map/ppermute | solution.py:41
  68.5 29.8 %collective-permute-start.7 = (f32[16,4096]{1,0:T(8,128)S(1)}, f32[16,4096]{1,0:T(8,128)S(1)}, u32[]{:S(2)}, u32[]{:S(2)}) collective-permute-start(f32[16,4096]{1,0:T(8,128)S(1)} %unsort.2.refs_4_), channel_id=1, source_target_pairs={{0,1},{1,0},{2,3},{3,2},{4,5},{5,4},{6,7},{7,6},{8,9},{9,8},{10,11... | collective-permute-start | bytes 786440 | tf_op jit(solution)/shard_map/ppermute | solution.py:41
  69.4 28.9 %all-to-all-start = ((f32[256,1,64]{2,1,0:T(1,128)}), f32[256,1,64]{2,1,0:T(1,128)S(1)}, u32[]{:S(2)}, u32[]{:S(2)}) async-start(f32[256,1,64]{2,1,0:T(1,128)} %bitcast.3), calls=%async_computation | async-start | bytes 262144 | tf_op jit(solution)/shard_map/all_to_all | solution.py:658

commit v6 on v5

--- a/solution.py
+++ b/solution.py
@@ -50,8 +50,15 @@
 
 
 def one_hot_strip(rank, start):
-    place = lax.broadcasted_iota(jnp.int32, (STRIP, B), 0) + start
-    return jnp.where(rank == place, 1.0, 0.0).astype(jnp.bfloat16)
+    place = lax.broadcasted_iota(jnp.int32, (TILE, B), 0).astype(jnp.bfloat16)
+    one, zero = jnp.ones((), jnp.bfloat16), jnp.zeros((), jnp.bfloat16)
+    blocks = []
+    for t in range(STRIP // TILE):
+        local = rank - (start + t * TILE)
+        local = jnp.where((local >= 0) & (local < TILE), local, -1)
+        local = local.astype(jnp.float32).astype(jnp.bfloat16)
+        blocks.append(jnp.where(local == place, one, zero))
+    return jnp.concatenate(blocks, axis=0)
 
 
 def cell_of(values, cells):
@@ -63,7 +70,7 @@
 
 def sort_kernel(
     count,
-    meta_ref,
+    active_ref,
     points_hbm,
     sides_ref,
     rows_ref,
@@ -77,7 +84,8 @@
     points_ref,
     arrived,
 ):
-    first = pl.multiple_of(meta_ref[1] * 16, 16)
+    column = lax.axis_index("blk")
+    first = pl.multiple_of(lax.axis_index("rep") * 16, 16)
     locate = pltpu.make_async_copy(points_hbm, points_ref, arrived.at[0])
     locate.start()
     fetch = pltpu.make_async_copy(
@@ -85,7 +93,7 @@
     )
     fetch.start()
     for own in (True, False):
-        box_ref[2 if own else 3] = pair_flags(own, meta_ref, count, box_ref.shape[1:])
+        box_ref[2 if own else 3] = pair_flags(own, active_ref, column, count, box_ref.shape[1:])
     upper = lax.broadcasted_iota(jnp.int32, (TILE, TILE), 0) <= lax.broadcasted_iota(
         jnp.int32, (TILE, TILE), 1
     )
@@ -93,7 +101,7 @@
     lower = lax.broadcasted_iota(jnp.int32, (CELLS, CELLS), 0) > lax.broadcasted_iota(
         jnp.int32, (CELLS, CELLS), 1
     )
-    lower = jnp.where(lower, 1.0, 0.0)
+    lower = jnp.where(lower, 1.0, 0.0).astype(jnp.bfloat16)
     number = lax.broadcasted_iota(jnp.int32, (CELLS, TILE), 0).astype(jnp.float32)
     feature_ref[16:32, :] = jnp.zeros((16, B), jnp.float32)
     split_ref[96:128, :] = jnp.zeros((32, B), jnp.bfloat16)
@@ -104,16 +112,27 @@
             points_ref[1:2, span], CELLS_Y
         )
         base = jnp.zeros((CELLS, TILE), jnp.float32)
-        chosen, place = [], []
+        chosen = [
+            jnp.where(number == cell[:, t * TILE : (t + 1) * TILE], 1.0, 0.0)
+            for t in range(B // TILE)
+        ]
+        counts = jnp.dot(
+            jnp.concatenate(chosen, axis=0).astype(jnp.bfloat16),
+            upper,
+            preferred_element_type=jnp.float32,
+        )
+        place = []
         for t in range(B // TILE):
-            hit = jnp.where(number == cell[:, t * TILE : (t + 1) * TILE], 1.0, 0.0)
-            count = jnp.dot(hit.astype(jnp.bfloat16), upper, preferred_element_type=jnp.float32)
-            chosen.append(hit)
+            count = counts[t * CELLS : (t + 1) * CELLS, :]
             place.append(count + base)
             base = base + count[:, TILE - 1 :]
+        high = jnp.floor(base * (1.0 / 64.0))
         offset = jnp.dot(
-            lower, base, precision=lax.Precision.HIGHEST, preferred_element_type=jnp.float32
+            lower,
+            jnp.concatenate([high, base - 64.0 * high], axis=1).astype(jnp.bfloat16),
+            preferred_element_type=jnp.float32,
         )
+        offset = 64.0 * offset[:, 0:TILE] + offset[:, TILE : 2 * TILE]
         for t in range(B // TILE):
             rank = jnp.sum(chosen[t] * (place[t] + (offset - 1.0)), axis=0, keepdims=True)
             rank_ref[0:1, c * B + t * TILE : c * B + (t + 1) * TILE] = rank.astype(jnp.int32)
@@ -155,7 +174,7 @@
             ]
 
 
-def sort_points(count, meta, points, right_side):
+def sort_points(count, active, points, right_side):
     width = 2 * B
     return pl.pallas_call(
         partial(sort_kernel, count),
@@ -177,7 +196,7 @@
         ],
         compiler_params=pltpu.CompilerParams(vmem_limit_bytes=LIMIT),
         name="sort_points",
-    )(meta, points, right_side)
+    )(active, points, right_side)
 
 
 def unsort_kernel(sorted_ref, rank_ref, out_ref, split_ref, total_ref):
@@ -208,22 +227,22 @@
     )(values, rank)
 
 
-def pair_flags(own, meta_ref, count, shape):
+def pair_flags(own, active_ref, column, count, shape):
     is_second = lax.broadcasted_iota(jnp.int32, shape, 0) >= shape[0] // 2
     quarter = lax.broadcasted_iota(jnp.int32, shape, 1) // (TILE // 4)
-    column = meta_ref[0]
     if own:
-        flag = jnp.where(is_second == (quarter == 1), 1, meta_ref[2])
+        flag = jnp.where(is_second == (quarter == 1), 1, active_ref[0, column])
         return jnp.where(quarter < 2, flag, 0).astype(jnp.float32)
+    behind = jnp.maximum(column - 1, 0)
     has_behind = jnp.where(column >= 1, 1, 0)
     has_ahead = jnp.where(column + 1 < count, 1, 0)
     flag = jnp.zeros(shape, jnp.int32)
     for c in range(2):
         for q in range(4):
             if q < 2:
-                value = meta_ref[8 + 2 * q + c] * has_behind
+                value = active_ref[1 + 2 * q + c, behind] * has_behind
             else:
-                value = meta_ref[3 + 2 * c + (q - 2)] * has_ahead
+                value = active_ref[1 + 2 * c + (q - 2), column] * has_ahead
             flag = jnp.where((is_second == (c == 1)) & (quarter == q), value, flag)
     return flag.astype(jnp.float32)
 
@@ -630,21 +649,13 @@
 
 
 def shards(right_side, points, active):
-    column = lax.axis_index("blk")
-    member = lax.axis_index("rep")
-    sides = right_side.shape[0] // lax.axis_size("rep")
-    here = lax.dynamic_slice_in_dim(active, column, 1, 0)[0]
-    before = lax.dynamic_slice_in_dim(active, jnp.maximum(column - 1, 0), 1, 0)[0]
-    place = jnp.stack([column, member]).astype(jnp.int32)
-    meta = jnp.concatenate([place, here, before])
-
     def spread(values):
         return [values] + [exchange(values, mask, "rep") for mask in (1, 2, 3)]
 
     def neighbours(values):
         return from_behind(values, "blk", 1), from_behind(values, "blk", -1)
 
-    rows, cols, rank, box = sort_points(lax.axis_size("blk"), meta, points, right_side)
+    rows, cols, rank, box = sort_points(lax.axis_size("blk"), active.T, points, right_side)
     around = neighbours(rows)
     fixed = (cols, box)
     part, *kept_own = apply_pairs(fixed, (rows,), (rows,))
@@ -653,7 +664,7 @@
     w0_pieces = spread(unsort(w0, rank))
     (part,) = apply_pairs(fixed, (rows,), (w0,), kept=kept_own)
     w1, line = apply_pairs(fixed, around, w0_around, part, (rows, w0), kept_cross)
-    line, mine = lax.optimization_barrier((line, unsort(w1, rank)))
+    mine = unsort(w1, rank)
     w1_pieces = spread(mine)
     lines = lax.all_to_all(line[:, 0:64], ("blk", "rep"), 0, 0, tiled=True)
     return finish_sides(lines, right_side, w0_pieces + w1_pieces)

time: 103 us -> 102 us (level)
    unnamed x6 -> x8, local copies, waits for them, and re-layouts: 2.08 us -> 2.75 us
where the time goes in v6:
time: 102 us; the launch traced here: 100 us
  Pallas kernels  49.9 us (49%)
  starting transfers between devices  34.6 us (34%)
  waiting for transfers between devices  12.3 us (12%)
  local copies, waits for them, and re-layouts  2.75 us (3%)
    pallas_call x4, Pallas kernels, apply_pairs(): pl.pallas_call(partial(apply_kernel, own, again), out_shape=out_shape, in...  35.3 us
    all_to_all x1, starting transfers between devices, shards(): lines = lax.all_to_all(line[:, 0:64], ('blk', 'rep'), 0, 0, tiled=True)  16.7 us
    all_to_all x1, waiting for transfers between devices, shards(): lines = lax.all_to_all(line[:, 0:64], ('blk', 'rep'), 0, 0, tiled=True)  12.2 us
    ppermute x4, starting transfers between devices, from_behind(): return lax.ppermute(block, axis, route)  9.69 us
    ppermute x6, starting transfers between devices, exchange(): return lax.ppermute(values, axis, [(i, i ^ mask) for i in devices])  8.23 us
    pallas_call x1, Pallas kernels, sort_points(): pl.pallas_call(partial(sort_kernel, count), out_shape=(jax.ShapeDtypeStru...  6.56 us
    pallas_call x2, Pallas kernels, unsort(): pl.pallas_call(unsort_kernel, out_shape=jax.ShapeDtypeStruct(values.shape...  5.39 us
    unnamed x8, local copies, waits for them, and re-layouts  2.75 us
  transfers between devices with their start and end apart: 11, of which 1 were waited for; matrix products, arithmetic and copies ran while one was open for 0% of the time, Pallas kernels for 34%

profile of v6, /device:TPU:8, one launch (start us, length us, event | category | flops | bytes accessed | tf_op | source)
XLA Modules:
  0.0 100.3 jit_solution(2856072487127028628)
XLA Ops:
  0.6 0.0 copy-start
  0.6 1.2 %copy-done = f32[64,4096]{1,0:T(8,128)S(1)} copy-done((f32[64,4096]{1,0:T(8,128)S(1)}, f32[64,4096]{1,0:T(8,128)}, u32[]{:S(2)}) %copy-start) | copy-done | bytes 1048600
  1.9 0.8 copy-done.2
  2.7 0.7 copy-done.3
  3.4 6.6 %sort_points.1 = (f32[24,4096]{1,0:T(8,128)S(1)}, f32[4096,128]{1,0:T(8,128)S(1)}, s32[8,4096]{1,0:T(8,128)S(1)}, f32[4,32,128]{2,1,0:T(8,128)S(1)}) custom-call(s32[5,64]{1,0:T(8,128)S(1)} %bitcast.7, f32[3,4096]{1,0:T(4,128)S(1)} %copy-done.2, f32[64,4096]{1,0:T(8,128)S(1)} %copy-done), custom_call_target="tpu_custom_call" | custom-call | tf_op jit(solution)/shard_map/sort_points/pallas_call | solution.py:179
  10.0 1.3 %collective-permute-start.1 = (f32[24,4096]{1,0:T(8,128)S(1)}, f32[24,4096]{1,0:T(8,128)S(1)}, u32[]{:S(2)}, u32[]{:S(2)}) collective-permute-start(f32[24,4096]{1,0:T(8,128)S(1)} %get-tuple-element.16.refs_2_.refs_3_.refs_7_), channel_id=1, source_target_pairs={{4,0},{8,4},{12,8},{16,12},{20,16},{24,20},{28,24},{32,28},{36,32}... | collective-permute-start | bytes 1179656 | tf_op jit(solution)/shard_map/ppermute | solution.py:36
  11.3 3.1 %collective-permute-start = (f32[24,4096]{1,0:T(8,128)S(1)}, f32[24,4096]{1,0:T(8,128)S(1)}, u32[]{:S(2)}, u32[]{:S(2)}) collective-permute-start(f32[24,4096]{1,0:T(8,128)S(1)} %get-tuple-element.16.refs_2_.refs_3_.refs_7_), channel_id=1, source_target_pairs={{0,4},{4,8},{8,12},{12,16},{16,20},{20,24},{24,28},{28,32},{32,36}... | collective-permute-start | bytes 1179656 | tf_op jit(solution)/shard_map/ppermute | solution.py:36
  14.3 15.4 %apply_own.1 = (f32[16,4096]{1,0:T(8,128)S(1)}, s32[32,128]{1,0:T(8,128)S(1)}, bf16[24,4,256,256]{3,2,1,0:T(8,128)(2,1)}) custom-call(f32[4096,128]{1,0:T(8,128)S(1)} %get-tuple-element.14.refs_0_, f32[4,32,128]{2,1,0:T(8,128)S(1)} %get-tuple-element.15.refs_1_, f32[24,4096]{1,0:T(8,128)S(1)} %get-tuple-element.16.refs_2_.refs_3_.refs_7_, ...), custom_call_target="tpu_custom_call" | custom-call | tf_op jit(solution)/shard_map/apply_own/pallas_call | solution.py:567
  29.8 0.0 collective-permute-done.1.refs_3_.refs_5_
  29.8 0.0 collective-permute-done.refs_2_.refs_4_
  29.8 6.5 %apply_cross.1 = (f32[16,4096]{1,0:T(8,128)S(1)}, s32[32,128]{1,0:T(8,128)S(1)}, bf16[8,4,256,256]{3,2,1,0:T(8,128)(2,1)}) custom-call(f32[4096,128]{1,0:T(8,128)S(1)} %get-tuple-element.14.refs_0_, f32[4,32,128]{2,1,0:T(8,128)S(1)} %get-tuple-element.15.refs_1_, f32[24,4096]{1,0:T(8,128)S(1)} %collective-permute-done.refs_2_.refs_4_, ...), custom_call_target="tpu_custom_call" | custom-call | tf_op jit(solution)/shard_map/apply_cross/pallas_call | solution.py:567
  36.3 1.3 %collective-permute-start.3 = (f32[16,4096]{1,0:T(8,128)S(1)}, f32[16,4096]{1,0:T(8,128)S(1)}, u32[]{:S(2)}, u32[]{:S(2)}) collective-permute-start(f32[16,4096]{1,0:T(8,128)S(1)} %get-tuple-element.18.refs_3_.refs_8_.sorted_ref), channel_id=1, source_target_pairs={{4,0},{8,4},{12,8},{16,12},{20,16},{24,20},{28,24},{32,28},{36,32}... | collective-permute-start | bytes 786440 | tf_op jit(solution)/shard_map/ppermute | solution.py:36
  37.6 4.1 %collective-permute-start.2 = (f32[16,4096]{1,0:T(8,128)S(1)}, f32[16,4096]{1,0:T(8,128)S(1)}, u32[]{:S(2)}, u32[]{:S(2)}) collective-permute-start(f32[16,4096]{1,0:T(8,128)S(1)} %get-tuple-element.18.refs_3_.refs_8_.sorted_ref), channel_id=1, source_target_pairs={{0,4},{4,8},{8,12},{12,16},{16,20},{20,24},{24,28},{28,32},{32,36}... | collective-permute-start | bytes 786440 | tf_op jit(solution)/shard_map/ppermute | solution.py:36
  41.7 2.7 %unsort.2.refs_0_ = f32[16,4096]{1,0:T(8,128)S(1)} custom-call(f32[16,4096]{1,0:T(8,128)S(1)} %get-tuple-element.18.refs_3_.refs_8_.sorted_ref, s32[8,4096]{1,0:T(8,128)S(1)} %get-tuple-element.24.rank_ref), custom_call_target="tpu_custom_call" | custom-call | tf_op jit(solution)/shard_map/unsort/pallas_call | solution.py:219
  44.4 1.6 %collective-permute-start.6 = (f32[16,4096]{1,0:T(8,128)S(1)}, f32[16,4096]{1,0:T(8,128)S(1)}, u32[]{:S(2)}, u32[]{:S(2)}) collective-permute-start(f32[16,4096]{1,0:T(8,128)S(1)} %unsort.2.refs_0_), channel_id=1, source_target_pairs={{0,3},{1,2},{2,1},{3,0},{4,7},{5,6},{6,5},{7,4},{8,11},{9,10},{10,... | collective-permute-start | bytes 786440 | tf_op jit(solution)/shard_map/ppermute | solution.py:41
  46.0 1.7 %collective-permute-start.5 = (f32[16,4096]{1,0:T(8,128)S(1)}, f32[16,4096]{1,0:T(8,128)S(1)}, u32[]{:S(2)}, u32[]{:S(2)}) collective-permute-start(f32[16,4096]{1,0:T(8,128)S(1)} %unsort.2.refs_0_), channel_id=1, source_target_pairs={{0,2},{1,3},{2,0},{3,1},{4,6},{5,7},{6,4},{7,5},{8,10},{9,11},{10,... | collective-permute-start | bytes 786440 | tf_op jit(solution)/shard_map/ppermute | solution.py:41
  47.6 0.8 collective-permute-start.4
  48.5 8.3 %again_own.1.refs_6_ = f32[16,4096]{1,0:T(8,128)S(1)} custom-call(f32[4096,128]{1,0:T(8,128)S(1)} %get-tuple-element.14.refs_0_, f32[4,32,128]{2,1,0:T(8,128)S(1)} %get-tuple-element.15.refs_1_, f32[24,4096]{1,0:T(8,128)S(1)} %get-tuple-element.16.refs_2_.refs_3_.refs_7_, f32[16,4096]{1,0:T(8,128)S(1)} %get-tuple-element.18.refs_3_.refs_8_.sorted_ref, ...), custom_call_target="tpu_custom_call" | custom-call | tf_op jit(solution)/shard_map/again_own/pallas_call | solution.py:567
  56.8 0.0 collective-permute-done.3.refs_5_
  56.8 0.0 collective-permute-done.2.refs_4_
  56.8 0.0 copy-start.1
  56.8 5.0 %again_cross.1 = (f32[16,4096]{1,0:T(8,128)S(1)}, f32[256,128]{1,0:T(8,128)}) custom-call(f32[4096,128]{1,0:T(8,128)S(1)} %get-tuple-element.14.refs_0_, f32[4,32,128]{2,1,0:T(8,128)S(1)} %get-tuple-element.15.refs_1_, f32[24,4096]{1,0:T(8,128)S(1)} %collective-permute-done.refs_2_.refs_4_, f32[24,4096]{1,0:T(8,128)S(1)} %collective-permute-done.1.refs_3_.refs_5_, ...), custom_call_target="tpu_custom_call" | custom-call | tf_op jit(solution)/shard_map/again_cross/pallas_call | solution.py:567
  61.9 2.7 %unsort.3.refs_4_ = f32[16,4096]{1,0:T(8,128)S(1)} custom-call(f32[16,4096]{1,0:T(8,128)S(1)} %get-tuple-element.25.sorted_ref, s32[8,4096]{1,0:T(8,128)S(1)} %get-tuple-element.24.rank_ref), custom_call_target="tpu_custom_call" | custom-call | tf_op jit(solution)/shard_map/unsort/pallas_call | solution.py:219
  64.6 1.6 %collective-permute-start.9 = (f32[16,4096]{1,0:T(8,128)S(1)}, f32[16,4096]{1,0:T(8,128)S(1)}, u32[]{:S(2)}, u32[]{:S(2)}) collective-permute-start(f32[16,4096]{1,0:T(8,128)S(1)} %unsort.3.refs_4_), channel_id=1, source_target_pairs={{0,3},{1,2},{2,1},{3,0},{4,7},{5,6},{6,5},{7,4},{8,11},{9,10},{10,... | collective-permute-start | bytes 786440 | tf_op jit(solution)/shard_map/ppermute | solution.py:41
  66.2 1.7 %collective-permute-start.8 = (f32[16,4096]{1,0:T(8,128)S(1)}, f32[16,4096]{1,0:T(8,128)S(1)}, u32[]{:S(2)}, u32[]{:S(2)}) collective-permute-start(f32[16,4096]{1,0:T(8,128)S(1)} %unsort.3.refs_4_), channel_id=1, source_target_pairs={{0,2},{1,3},{2,0},{3,1},{4,6},{5,7},{6,4},{7,5},{8,10},{9,11},{10,... | collective-permute-start | bytes 786440 | tf_op jit(solution)/shard_map/ppermute | solution.py:41
  67.9 0.0 collective-permute-done.6.refs_3_
  67.9 0.8 collective-permute-start.7
  68.7 16.7 %all-to-all-start = ((f32[256,1,64]{2,1,0:T(1,128)}), f32[256,1,64]{2,1,0:T(1,128)S(1)}, u32[]{:S(2)}, u32[]{:S(2)}) async-start(f32[256,1,64]{2,1,0:T(1,128)} %bitcast.2), calls=%async_computation | async-start | bytes 262144 | tf_op jit(solution)/shard_map/all_to_all | solution.py:669
  85.4 0.0 collective-permute-done.4.refs_1_
  85.4 12.2 %all-to-all-done = f32[256,1,64]{2,1,0:T(1,128)S(1)} async-done(((f32[256,1,64]{2,1,0:T(1,128)}), f32[256,1,64]{2,1,0:T(1,128)S(1)}, u32[]{:S(2)}, u32[]{:S(2)}) %all-to-all-start) | async-done | bytes 65568 | tf_op jit(solution)/shard_map/all_to_all | solution.py:669
  97.7 0.0 collective-permute-done.9.refs_7_
  97.7 2.6 %finish_sides.1 = (f32[64,4096]{1,0:T(8,128)}, f32[64,4096]{1,0:T(8,128)}) custom-call(f32[256,64]{1,0:T(8,128)S(1)} %bitcast.6, f32[64,4096]{1,0:T(8,128)S(1)} %copy-done.1, f32[16,4096]{1,0:T(8,128)S(1)} %unsort.2.refs_0_, f32[16,4096]{1,0:T(8,128)S(1)} %collective-permute-done.4.refs_1_, f32[16,4096]{1,0:T(8,128)S(1)} %collective-permute-done.5.refs_2_, ...), custom_call_target="tpu_custom_call" | custom-call | tf_op jit(solution)/shard_map/finish_sides/pallas_call | solution.py:639
  (6 shorter events, 0.0 us)
Async XLA Ops:
  0.6 1.2 %copy-start = (f32[64,4096]{1,0:T(8,128)S(1)}, f32[64,4096]{1,0:T(8,128)}, u32[]{:S(2)}) copy-start(f32[64,4096]{1,0:T(8,128)} %sides_ref.3) | copy-start | bytes 3145732
  1.9 0.8 copy-start.2
  2.7 0.7 copy-start.3
  10.0 19.8 %collective-permute-start.1 = (f32[24,4096]{1,0:T(8,128)S(1)}, f32[24,4096]{1,0:T(8,128)S(1)}, u32[]{:S(2)}, u32[]{:S(2)}) collective-permute-start(f32[24,4096]{1,0:T(8,128)S(1)} %get-tuple-element.16.refs_2_.refs_3_.refs_7_), channel_id=1, source_target_pairs={{4,0},{8,4},{12,8},{16,12},{20,16},{24,20},{28,24},{32,28},{36,32}... | collective-permute-start | bytes 1179656 | tf_op jit(solution)/shard_map/ppermute | solution.py:36
  11.3 18.5 %collective-permute-start = (f32[24,4096]{1,0:T(8,128)S(1)}, f32[24,4096]{1,0:T(8,128)S(1)}, u32[]{:S(2)}, u32[]{:S(2)}) collective-permute-start(f32[24,4096]{1,0:T(8,128)S(1)} %get-tuple-element.16.refs_2_.refs_3_.refs_7_), channel_id=1, source_target_pairs={{0,4},{4,8},{8,12},{12,16},{16,20},{20,24},{24,28},{28,32},{32,36}... | collective-permute-start | bytes 1179656 | tf_op jit(solution)/shard_map/ppermute | solution.py:36
  36.3 20.5 %collective-permute-start.3 = (f32[16,4096]{1,0:T(8,128)S(1)}, f32[16,4096]{1,0:T(8,128)S(1)}, u32[]{:S(2)}, u32[]{:S(2)}) collective-permute-start(f32[16,4096]{1,0:T(8,128)S(1)} %get-tuple-element.18.refs_3_.refs_8_.sorted_ref), channel_id=1, source_target_pairs={{4,0},{8,4},{12,8},{16,12},{20,16},{24,20},{28,24},{32,28},{36,32}... | collective-permute-start | bytes 786440 | tf_op jit(solution)/shard_map/ppermute | solution.py:36
  37.6 19.2 %collective-permute-start.2 = (f32[16,4096]{1,0:T(8,128)S(1)}, f32[16,4096]{1,0:T(8,128)S(1)}, u32[]{:S(2)}, u32[]{:S(2)}) collective-permute-start(f32[16,4096]{1,0:T(8,128)S(1)} %get-tuple-element.18.refs_3_.refs_8_.sorted_ref), channel_id=1, source_target_pairs={{0,4},{4,8},{8,12},{12,16},{16,20},{20,24},{24,28},{28,32},{32,36}... | collective-permute-start | bytes 786440 | tf_op jit(solution)/shard_map/ppermute | solution.py:36
  44.4 23.5 %collective-permute-start.6 = (f32[16,4096]{1,0:T(8,128)S(1)}, f32[16,4096]{1,0:T(8,128)S(1)}, u32[]{:S(2)}, u32[]{:S(2)}) collective-permute-start(f32[16,4096]{1,0:T(8,128)S(1)} %unsort.2.refs_0_), channel_id=1, source_target_pairs={{0,3},{1,2},{2,1},{3,0},{4,7},{5,6},{6,5},{7,4},{8,11},{9,10},{10,... | collective-permute-start | bytes 786440 | tf_op jit(solution)/shard_map/ppermute | solution.py:41
  46.0 39.5 %collective-permute-start.5 = (f32[16,4096]{1,0:T(8,128)S(1)}, f32[16,4096]{1,0:T(8,128)S(1)}, u32[]{:S(2)}, u32[]{:S(2)}) collective-permute-start(f32[16,4096]{1,0:T(8,128)S(1)} %unsort.2.refs_0_), channel_id=1, source_target_pairs={{0,2},{1,3},{2,0},{3,1},{4,6},{5,7},{6,4},{7,5},{8,10},{9,11},{10,... | collective-permute-start | bytes 786440 | tf_op jit(solution)/shard_map/ppermute | solution.py:41
  47.6 37.8 %collective-permute-start.4 = (f32[16,4096]{1,0:T(8,128)S(1)}, f32[16,4096]{1,0:T(8,128)S(1)}, u32[]{:S(2)}, u32[]{:S(2)}) collective-permute-start(f32[16,4096]{1,0:T(8,128)S(1)} %unsort.2.refs_0_), channel_id=1, source_target_pairs={{0,1},{1,0},{2,3},{3,2},{4,5},{5,4},{6,7},{7,6},{8,9},{9,8},{10,11... | collective-permute-start | bytes 786440 | tf_op jit(solution)/shard_map/ppermute | solution.py:41
  56.8 40.9 %copy-start.1 = (f32[64,4096]{1,0:T(8,128)S(1)}, f32[64,4096]{1,0:T(8,128)}, u32[]{:S(2)}) copy-start(f32[64,4096]{1,0:T(8,128)} %sides_ref.3) | copy-start | bytes 3145732
  64.6 33.1 %collective-permute-start.9 = (f32[16,4096]{1,0:T(8,128)S(1)}, f32[16,4096]{1,0:T(8,128)S(1)}, u32[]{:S(2)}, u32[]{:S(2)}) collective-permute-start(f32[16,4096]{1,0:T(8,128)S(1)} %unsort.3.refs_4_), channel_id=1, source_target_pairs={{0,3},{1,2},{2,1},{3,0},{4,7},{5,6},{6,5},{7,4},{8,11},{9,10},{10,... | collective-permute-start | bytes 786440 | tf_op jit(solution)/shard_map/ppermute | solution.py:41
  66.2 31.5 %collective-permute-start.8 = (f32[16,4096]{1,0:T(8,128)S(1)}, f32[16,4096]{1,0:T(8,128)S(1)}, u32[]{:S(2)}, u32[]{:S(2)}) collective-permute-start(f32[16,4096]{1,0:T(8,128)S(1)} %unsort.3.refs_4_), channel_id=1, source_target_pairs={{0,2},{1,3},{2,0},{3,1},{4,6},{5,7},{6,4},{7,5},{8,10},{9,11},{10,... | collective-permute-start | bytes 786440 | tf_op jit(solution)/shard_map/ppermute | solution.py:41
  67.9 29.8 %collective-permute-start.7 = (f32[16,4096]{1,0:T(8,128)S(1)}, f32[16,4096]{1,0:T(8,128)S(1)}, u32[]{:S(2)}, u32[]{:S(2)}) collective-permute-start(f32[16,4096]{1,0:T(8,128)S(1)} %unsort.3.refs_4_), channel_id=1, source_target_pairs={{0,1},{1,0},{2,3},{3,2},{4,5},{5,4},{6,7},{7,6},{8,9},{9,8},{10,11... | collective-permute-start | bytes 786440 | tf_op jit(solution)/shard_map/ppermute | solution.py:41
  68.7 29.0 %all-to-all-start = ((f32[256,1,64]{2,1,0:T(1,128)}), f32[256,1,64]{2,1,0:T(1,128)S(1)}, u32[]{:S(2)}, u32[]{:S(2)}) async-start(f32[256,1,64]{2,1,0:T(1,128)} %bitcast.2), calls=%async_computation | async-start | bytes 262144 | tf_op jit(solution)/shard_map/all_to_all | solution.py:669

commit v7 on v6

--- a/solution.py
+++ b/solution.py
@@ -14,7 +14,7 @@
 BATCH = 4
 GROUP = 4
 KEPT = {True: 24, False: 8}
-EARLY = {True: 12, False: 4}
+EARLY = {True: 20, False: 4}
 CELLS_X = 4
 CELLS_Y = 8
 CELLS = CELLS_X * CELLS_Y

time: 102 us -> 102 us (level)
  no operation moved by 1% of the time
where the time goes in v7:
time: 102 us; the launch traced here: 100 us
  Pallas kernels  49.9 us (49%)
  starting transfers between devices  34.6 us (34%)
  waiting for transfers between devices  12.3 us (12%)
  local copies, waits for them, and re-layouts  2.75 us (3%)
    pallas_call x4, Pallas kernels, apply_pairs(): pl.pallas_call(partial(apply_kernel, own, again), out_shape=out_shape, in...  35.3 us
    all_to_all x1, starting transfers between devices, shards(): lines = lax.all_to_all(line[:, 0:64], ('blk', 'rep'), 0, 0, tiled=True)  16.7 us
    all_to_all x1, waiting for transfers between devices, shards(): lines = lax.all_to_all(line[:, 0:64], ('blk', 'rep'), 0, 0, tiled=True)  12.2 us
    ppermute x4, starting transfers between devices, from_behind(): return lax.ppermute(block, axis, route)  9.68 us
    ppermute x6, starting transfers between devices, exchange(): return lax.ppermute(values, axis, [(i, i ^ mask) for i in devices])  8.24 us
    pallas_call x1, Pallas kernels, sort_points(): pl.pallas_call(partial(sort_kernel, count), out_shape=(jax.ShapeDtypeStru...  6.56 us
    pallas_call x2, Pallas kernels, unsort(): pl.pallas_call(unsort_kernel, out_shape=jax.ShapeDtypeStruct(values.shape...  5.36 us
    unnamed x8, local copies, waits for them, and re-layouts  2.75 us
  transfers between devices with their start and end apart: 11, of which 1 were waited for; matrix products, arithmetic and copies ran while one was open for 0% of the time, Pallas kernels for 34%

profile of v7, /device:TPU:8, one launch (start us, length us, event | category | flops | bytes accessed | tf_op | source)
XLA Modules:
  0.0 100.3 jit_solution(10489893245346748234)
XLA Ops:
  0.6 0.0 copy-start
  0.6 1.2 %copy-done = f32[64,4096]{1,0:T(8,128)S(1)} copy-done((f32[64,4096]{1,0:T(8,128)S(1)}, f32[64,4096]{1,0:T(8,128)}, u32[]{:S(2)}) %copy-start) | copy-done | bytes 1048600
  1.9 0.8 copy-done.2
  2.7 0.7 copy-done.3
  3.4 6.6 %sort_points.1 = (f32[24,4096]{1,0:T(8,128)S(1)}, f32[4096,128]{1,0:T(8,128)S(1)}, s32[8,4096]{1,0:T(8,128)S(1)}, f32[4,32,128]{2,1,0:T(8,128)S(1)}) custom-call(s32[5,64]{1,0:T(8,128)S(1)} %bitcast.7, f32[3,4096]{1,0:T(4,128)S(1)} %copy-done.2, f32[64,4096]{1,0:T(8,128)S(1)} %copy-done), custom_call_target="tpu_custom_call" | custom-call | tf_op jit(solution)/shard_map/sort_points/pallas_call | solution.py:179
  10.0 1.3 %collective-permute-start.1 = (f32[24,4096]{1,0:T(8,128)S(1)}, f32[24,4096]{1,0:T(8,128)S(1)}, u32[]{:S(2)}, u32[]{:S(2)}) collective-permute-start(f32[24,4096]{1,0:T(8,128)S(1)} %get-tuple-element.16.refs_2_.refs_3_.refs_7_), channel_id=1, source_target_pairs={{4,0},{8,4},{12,8},{16,12},{20,16},{24,20},{28,24},{32,28},{36,32}... | collective-permute-start | bytes 1179656 | tf_op jit(solution)/shard_map/ppermute | solution.py:36
  11.3 3.1 %collective-permute-start = (f32[24,4096]{1,0:T(8,128)S(1)}, f32[24,4096]{1,0:T(8,128)S(1)}, u32[]{:S(2)}, u32[]{:S(2)}) collective-permute-start(f32[24,4096]{1,0:T(8,128)S(1)} %get-tuple-element.16.refs_2_.refs_3_.refs_7_), channel_id=1, source_target_pairs={{0,4},{4,8},{8,12},{12,16},{16,20},{20,24},{24,28},{28,32},{32,36}... | collective-permute-start | bytes 1179656 | tf_op jit(solution)/shard_map/ppermute | solution.py:36
  14.3 15.4 %apply_own.1 = (f32[16,4096]{1,0:T(8,128)S(1)}, s32[32,128]{1,0:T(8,128)S(1)}, bf16[24,4,256,256]{3,2,1,0:T(8,128)(2,1)}) custom-call(f32[4096,128]{1,0:T(8,128)S(1)} %get-tuple-element.14.refs_0_, f32[4,32,128]{2,1,0:T(8,128)S(1)} %get-tuple-element.15.refs_1_, f32[24,4096]{1,0:T(8,128)S(1)} %get-tuple-element.16.refs_2_.refs_3_.refs_7_, ...), custom_call_target="tpu_custom_call" | custom-call | tf_op jit(solution)/shard_map/apply_own/pallas_call | solution.py:567
  29.8 0.0 collective-permute-done.1.refs_3_.refs_5_
  29.8 0.0 collective-permute-done.refs_2_.refs_4_
  29.8 6.6 %apply_cross.1 = (f32[16,4096]{1,0:T(8,128)S(1)}, s32[32,128]{1,0:T(8,128)S(1)}, bf16[8,4,256,256]{3,2,1,0:T(8,128)(2,1)}) custom-call(f32[4096,128]{1,0:T(8,128)S(1)} %get-tuple-element.14.refs_0_, f32[4,32,128]{2,1,0:T(8,128)S(1)} %get-tuple-element.15.refs_1_, f32[24,4096]{1,0:T(8,128)S(1)} %collective-permute-done.refs_2_.refs_4_, ...), custom_call_target="tpu_custom_call" | custom-call | tf_op jit(solution)/shard_map/apply_cross/pallas_call | solution.py:567
  36.3 1.3 %collective-permute-start.3 = (f32[16,4096]{1,0:T(8,128)S(1)}, f32[16,4096]{1,0:T(8,128)S(1)}, u32[]{:S(2)}, u32[]{:S(2)}) collective-permute-start(f32[16,4096]{1,0:T(8,128)S(1)} %get-tuple-element.18.refs_3_.refs_8_.sorted_ref), channel_id=1, source_target_pairs={{4,0},{8,4},{12,8},{16,12},{20,16},{24,20},{28,24},{32,28},{36,32}... | collective-permute-start | bytes 786440 | tf_op jit(solution)/shard_map/ppermute | solution.py:36
  37.6 4.0 %collective-permute-start.2 = (f32[16,4096]{1,0:T(8,128)S(1)}, f32[16,4096]{1,0:T(8,128)S(1)}, u32[]{:S(2)}, u32[]{:S(2)}) collective-permute-start(f32[16,4096]{1,0:T(8,128)S(1)} %get-tuple-element.18.refs_3_.refs_8_.sorted_ref), channel_id=1, source_target_pairs={{0,4},{4,8},{8,12},{12,16},{16,20},{20,24},{24,28},{28,32},{32,36}... | collective-permute-start | bytes 786440 | tf_op jit(solution)/shard_map/ppermute | solution.py:36
  41.7 2.7 %unsort.2.refs_0_ = f32[16,4096]{1,0:T(8,128)S(1)} custom-call(f32[16,4096]{1,0:T(8,128)S(1)} %get-tuple-element.18.refs_3_.refs_8_.sorted_ref, s32[8,4096]{1,0:T(8,128)S(1)} %get-tuple-element.24.rank_ref), custom_call_target="tpu_custom_call" | custom-call | tf_op jit(solution)/shard_map/unsort/pallas_call | solution.py:219
  44.4 1.6 %collective-permute-start.6 = (f32[16,4096]{1,0:T(8,128)S(1)}, f32[16,4096]{1,0:T(8,128)S(1)}, u32[]{:S(2)}, u32[]{:S(2)}) collective-permute-start(f32[16,4096]{1,0:T(8,128)S(1)} %unsort.2.refs_0_), channel_id=1, source_target_pairs={{0,3},{1,2},{2,1},{3,0},{4,7},{5,6},{6,5},{7,4},{8,11},{9,10},{10,... | collective-permute-start | bytes 786440 | tf_op jit(solution)/shard_map/ppermute | solution.py:41
  46.0 1.8 %collective-permute-start.5 = (f32[16,4096]{1,0:T(8,128)S(1)}, f32[16,4096]{1,0:T(8,128)S(1)}, u32[]{:S(2)}, u32[]{:S(2)}) collective-permute-start(f32[16,4096]{1,0:T(8,128)S(1)} %unsort.2.refs_0_), channel_id=1, source_target_pairs={{0,2},{1,3},{2,0},{3,1},{4,6},{5,7},{6,4},{7,5},{8,10},{9,11},{10,... | collective-permute-start | bytes 786440 | tf_op jit(solution)/shard_map/ppermute | solution.py:41
  47.7 0.7 collective-permute-start.4
  48.5 8.3 %again_own.1.refs_6_ = f32[16,4096]{1,0:T(8,128)S(1)} custom-call(f32[4096,128]{1,0:T(8,128)S(1)} %get-tuple-element.14.refs_0_, f32[4,32,128]{2,1,0:T(8,128)S(1)} %get-tuple-element.15.refs_1_, f32[24,4096]{1,0:T(8,128)S(1)} %get-tuple-element.16.refs_2_.refs_3_.refs_7_, f32[16,4096]{1,0:T(8,128)S(1)} %get-tuple-element.18.refs_3_.refs_8_.sorted_ref, ...), custom_call_target="tpu_custom_call" | custom-call | tf_op jit(solution)/shard_map/again_own/pallas_call | solution.py:567
  56.8 0.0 collective-permute-done.3.refs_5_
  56.8 0.0 collective-permute-done.2.refs_4_
  56.8 0.0 copy-start.1
  56.8 5.0 %again_cross.1 = (f32[16,4096]{1,0:T(8,128)S(1)}, f32[256,128]{1,0:T(8,128)}) custom-call(f32[4096,128]{1,0:T(8,128)S(1)} %get-tuple-element.14.refs_0_, f32[4,32,128]{2,1,0:T(8,128)S(1)} %get-tuple-element.15.refs_1_, f32[24,4096]{1,0:T(8,128)S(1)} %collective-permute-done.refs_2_.refs_4_, f32[24,4096]{1,0:T(8,128)S(1)} %collective-permute-done.1.refs_3_.refs_5_, ...), custom_call_target="tpu_custom_call" | custom-call | tf_op jit(solution)/shard_map/again_cross/pallas_call | solution.py:567
  61.8 2.7 %unsort.3.refs_4_ = f32[16,4096]{1,0:T(8,128)S(1)} custom-call(f32[16,4096]{1,0:T(8,128)S(1)} %get-tuple-element.25.sorted_ref, s32[8,4096]{1,0:T(8,128)S(1)} %get-tuple-element.24.rank_ref), custom_call_target="tpu_custom_call" | custom-call | tf_op jit(solution)/shard_map/unsort/pallas_call | solution.py:219
  64.5 1.6 %collective-permute-start.9 = (f32[16,4096]{1,0:T(8,128)S(1)}, f32[16,4096]{1,0:T(8,128)S(1)}, u32[]{:S(2)}, u32[]{:S(2)}) collective-permute-start(f32[16,4096]{1,0:T(8,128)S(1)} %unsort.3.refs_4_), channel_id=1, source_target_pairs={{0,3},{1,2},{2,1},{3,0},{4,7},{5,6},{6,5},{7,4},{8,11},{9,10},{10,... | collective-permute-start | bytes 786440 | tf_op jit(solution)/shard_map/ppermute | solution.py:41
  66.1 1.8 %collective-permute-start.8 = (f32[16,4096]{1,0:T(8,128)S(1)}, f32[16,4096]{1,0:T(8,128)S(1)}, u32[]{:S(2)}, u32[]{:S(2)}) collective-permute-start(f32[16,4096]{1,0:T(8,128)S(1)} %unsort.3.refs_4_), channel_id=1, source_target_pairs={{0,2},{1,3},{2,0},{3,1},{4,6},{5,7},{6,4},{7,5},{8,10},{9,11},{10,... | collective-permute-start | bytes 786440 | tf_op jit(solution)/shard_map/ppermute | solution.py:41
  67.9 0.0 collective-permute-done.6.refs_3_
  67.9 0.8 collective-permute-start.7
  68.7 16.7 %all-to-all-start = ((f32[256,1,64]{2,1,0:T(1,128)}), f32[256,1,64]{2,1,0:T(1,128)S(1)}, u32[]{:S(2)}, u32[]{:S(2)}) async-start(f32[256,1,64]{2,1,0:T(1,128)} %bitcast.2), calls=%async_computation | async-start | bytes 262144 | tf_op jit(solution)/shard_map/all_to_all | solution.py:669
  85.4 0.0 collective-permute-done.5.refs_2_
  85.4 12.2 %all-to-all-done = f32[256,1,64]{2,1,0:T(1,128)S(1)} async-done(((f32[256,1,64]{2,1,0:T(1,128)}), f32[256,1,64]{2,1,0:T(1,128)S(1)}, u32[]{:S(2)}, u32[]{:S(2)}) %all-to-all-start) | async-done | bytes 65568 | tf_op jit(solution)/shard_map/all_to_all | solution.py:669
  97.6 0.0 collective-permute-done.7.refs_5_
  97.6 2.6 %finish_sides.1 = (f32[64,4096]{1,0:T(8,128)}, f32[64,4096]{1,0:T(8,128)}) custom-call(f32[256,64]{1,0:T(8,128)S(1)} %bitcast.6, f32[64,4096]{1,0:T(8,128)S(1)} %copy-done.1, f32[16,4096]{1,0:T(8,128)S(1)} %unsort.2.refs_0_, f32[16,4096]{1,0:T(8,128)S(1)} %collective-permute-done.4.refs_1_, f32[16,4096]{1,0:T(8,128)S(1)} %collective-permute-done.5.refs_2_, ...), custom_call_target="tpu_custom_call" | custom-call | tf_op jit(solution)/shard_map/finish_sides/pallas_call | solution.py:639
  (6 shorter events, 0.0 us)
Async XLA Ops:
  0.6 1.2 %copy-start = (f32[64,4096]{1,0:T(8,128)S(1)}, f32[64,4096]{1,0:T(8,128)}, u32[]{:S(2)}) copy-start(f32[64,4096]{1,0:T(8,128)} %sides_ref.3) | copy-start | bytes 3145732
  1.9 0.8 copy-start.2
  2.7 0.7 copy-start.3
  10.0 19.8 %collective-permute-start.1 = (f32[24,4096]{1,0:T(8,128)S(1)}, f32[24,4096]{1,0:T(8,128)S(1)}, u32[]{:S(2)}, u32[]{:S(2)}) collective-permute-start(f32[24,4096]{1,0:T(8,128)S(1)} %get-tuple-element.16.refs_2_.refs_3_.refs_7_), channel_id=1, source_target_pairs={{4,0},{8,4},{12,8},{16,12},{20,16},{24,20},{28,24},{32,28},{36,32}... | collective-permute-start | bytes 1179656 | tf_op jit(solution)/shard_map/ppermute | solution.py:36
  11.3 18.5 %collective-permute-start = (f32[24,4096]{1,0:T(8,128)S(1)}, f32[24,4096]{1,0:T(8,128)S(1)}, u32[]{:S(2)}, u32[]{:S(2)}) collective-permute-start(f32[24,4096]{1,0:T(8,128)S(1)} %get-tuple-element.16.refs_2_.refs_3_.refs_7_), channel_id=1, source_target_pairs={{0,4},{4,8},{8,12},{12,16},{16,20},{20,24},{24,28},{28,32},{32,36}... | collective-permute-start | bytes 1179656 | tf_op jit(solution)/shard_map/ppermute | solution.py:36
  36.3 20.4 %collective-permute-start.3 = (f32[16,4096]{1,0:T(8,128)S(1)}, f32[16,4096]{1,0:T(8,128)S(1)}, u32[]{:S(2)}, u32[]{:S(2)}) collective-permute-start(f32[16,4096]{1,0:T(8,128)S(1)} %get-tuple-element.18.refs_3_.refs_8_.sorted_ref), channel_id=1, source_target_pairs={{4,0},{8,4},{12,8},{16,12},{20,16},{24,20},{28,24},{32,28},{36,32}... | collective-permute-start | bytes 786440 | tf_op jit(solution)/shard_map/ppermute | solution.py:36
  37.6 19.1 %collective-permute-start.2 = (f32[16,4096]{1,0:T(8,128)S(1)}, f32[16,4096]{1,0:T(8,128)S(1)}, u32[]{:S(2)}, u32[]{:S(2)}) collective-permute-start(f32[16,4096]{1,0:T(8,128)S(1)} %get-tuple-element.18.refs_3_.refs_8_.sorted_ref), channel_id=1, source_target_pairs={{0,4},{4,8},{8,12},{12,16},{16,20},{20,24},{24,28},{28,32},{32,36}... | collective-permute-start | bytes 786440 | tf_op jit(solution)/shard_map/ppermute | solution.py:36
  44.4 23.5 %collective-permute-start.6 = (f32[16,4096]{1,0:T(8,128)S(1)}, f32[16,4096]{1,0:T(8,128)S(1)}, u32[]{:S(2)}, u32[]{:S(2)}) collective-permute-start(f32[16,4096]{1,0:T(8,128)S(1)} %unsort.2.refs_0_), channel_id=1, source_target_pairs={{0,3},{1,2},{2,1},{3,0},{4,7},{5,6},{6,5},{7,4},{8,11},{9,10},{10,... | collective-permute-start | bytes 786440 | tf_op jit(solution)/shard_map/ppermute | solution.py:41
  46.0 39.4 %collective-permute-start.5 = (f32[16,4096]{1,0:T(8,128)S(1)}, f32[16,4096]{1,0:T(8,128)S(1)}, u32[]{:S(2)}, u32[]{:S(2)}) collective-permute-start(f32[16,4096]{1,0:T(8,128)S(1)} %unsort.2.refs_0_), channel_id=1, source_target_pairs={{0,2},{1,3},{2,0},{3,1},{4,6},{5,7},{6,4},{7,5},{8,10},{9,11},{10,... | collective-permute-start | bytes 786440 | tf_op jit(solution)/shard_map/ppermute | solution.py:41
  47.7 37.6 %collective-permute-start.4 = (f32[16,4096]{1,0:T(8,128)S(1)}, f32[16,4096]{1,0:T(8,128)S(1)}, u32[]{:S(2)}, u32[]{:S(2)}) collective-permute-start(f32[16,4096]{1,0:T(8,128)S(1)} %unsort.2.refs_0_), channel_id=1, source_target_pairs={{0,1},{1,0},{2,3},{3,2},{4,5},{5,4},{6,7},{7,6},{8,9},{9,8},{10,11... | collective-permute-start | bytes 786440 | tf_op jit(solution)/shard_map/ppermute | solution.py:41
  56.8 40.9 %copy-start.1 = (f32[64,4096]{1,0:T(8,128)S(1)}, f32[64,4096]{1,0:T(8,128)}, u32[]{:S(2)}) copy-start(f32[64,4096]{1,0:T(8,128)} %sides_ref.3) | copy-start | bytes 3145732
  64.5 33.1 %collective-permute-start.9 = (f32[16,4096]{1,0:T(8,128)S(1)}, f32[16,4096]{1,0:T(8,128)S(1)}, u32[]{:S(2)}, u32[]{:S(2)}) collective-permute-start(f32[16,4096]{1,0:T(8,128)S(1)} %unsort.3.refs_4_), channel_id=1, source_target_pairs={{0,3},{1,2},{2,1},{3,0},{4,7},{5,6},{6,5},{7,4},{8,11},{9,10},{10,... | collective-permute-start | bytes 786440 | tf_op jit(solution)/shard_map/ppermute | solution.py:41
  66.1 31.5 %collective-permute-start.8 = (f32[16,4096]{1,0:T(8,128)S(1)}, f32[16,4096]{1,0:T(8,128)S(1)}, u32[]{:S(2)}, u32[]{:S(2)}) collective-permute-start(f32[16,4096]{1,0:T(8,128)S(1)} %unsort.3.refs_4_), channel_id=1, source_target_pairs={{0,2},{1,3},{2,0},{3,1},{4,6},{5,7},{6,4},{7,5},{8,10},{9,11},{10,... | collective-permute-start | bytes 786440 | tf_op jit(solution)/shard_map/ppermute | solution.py:41
  67.9 29.7 %collective-permute-start.7 = (f32[16,4096]{1,0:T(8,128)S(1)}, f32[16,4096]{1,0:T(8,128)S(1)}, u32[]{:S(2)}, u32[]{:S(2)}) collective-permute-start(f32[16,4096]{1,0:T(8,128)S(1)} %unsort.3.refs_4_), channel_id=1, source_target_pairs={{0,1},{1,0},{2,3},{3,2},{4,5},{5,4},{6,7},{7,6},{8,9},{9,8},{10,11... | collective-permute-start | bytes 786440 | tf_op jit(solution)/shard_map/ppermute | solution.py:41
  68.7 29.0 %all-to-all-start = ((f32[256,1,64]{2,1,0:T(1,128)}), f32[256,1,64]{2,1,0:T(1,128)S(1)}, u32[]{:S(2)}, u32[]{:S(2)}) async-start(f32[256,1,64]{2,1,0:T(1,128)} %bitcast.2), calls=%async_computation | async-start | bytes 262144 | tf_op jit(solution)/shard_map/all_to_all | solution.py:669
